TPU v7x, 32 devices: a whole 2x2x4 slice. The times are simulated.
32 devices in a mesh: dp: 4 (over y, core), expert: 8 (over z, x).
Axes of the slice: x: 2, y: 2, z: 4, core: 2. Of those that a mesh axis runs over, the one named last changes fastest.
Arguments:
- tokens: bfloat16 [4096, 2048], P(('dp', 'expert')), may hold values from -6 to 6
- expert_ids: int32 [4096, 2], P(('dp', 'expert')), may hold values from 0 to 7, all different within a row; in each aligned block of 128 rows (0 to 127, 128 to 255, ...) at most 48 rows name the same one
- upstream: bfloat16 [4096, 2048], P(('dp', 'expert')), may hold values from -6 to 6
- gain: float32 [2048], replicated, may hold values from 0.5 to 1.5
- router: bfloat16 [2048, 8], replicated, may hold values from -0.125 to 0.125
- gate_weight_matrix: bfloat16 [8, 2048, 1024], P('expert', 'dp'), may hold values from -0.125 to 0.125
- up_weight: bfloat16 [8, 2048, 1024], P('expert', 'dp'), may hold values from -0.125 to 0.125
- down_weight: bfloat16 [8, 1024, 2048], P('expert', None, 'dp'), may hold values from -0.1875 to 0.1875
Outputs:
- mixed: bfloat16 [4096, 2048], P(('dp', 'expert'))
- d_tokens: bfloat16 [4096, 2048], P(('dp', 'expert'))
- gate_weight_gradient: bfloat16 [8, 2048, 1024], P('expert', 'dp')
- up_weight_gradient: bfloat16 [8, 2048, 1024], P('expert', 'dp')
- down_weight_gradient: bfloat16 [8, 1024, 2048], P('expert', None, 'dp')
- d_router: float32 [2048, 8], replicated
- d_gain: float32 [2048], replicated
Inputs may be any that keep to these rules, and one draw needn't show every extreme that they name: `expert_ids`: the two experts of a token differ. Among the tokens of one device (aligned blocks of 128 rows) no expert is named more than 48 times, and in some block one expert is named exactly 48 times.
All inputs are finite; a program needn't handle non-finite values.
Results may differ from a plain program's by a relative error of at most 0.014.
Values may be sent and summed in bfloat16 or wider, within the bound.
A program may use at most 128 MiB of HBM per device.

v0:
```python
import jax
import jax.numpy as jnp
from jax import lax
from jax.sharding import PartitionSpec as P

norm_eps = 1e-06


def slot_layout(expert_ids, experts, capacity):
    flattened = expert_ids.reshape(-1)
    onehot = (flattened[:, None] == jnp.arange(experts, dtype=jnp.int32)[None, :]).astype(jnp.int32)
    ranking = jnp.sum(jnp.cumsum(onehot, axis=0) * onehot, axis=1) - 1
    slot_ids = flattened * capacity + ranking
    sources = (
        jnp.zeros((experts * capacity,), jnp.int32)
        .at[slot_ids]
        .set(jnp.arange(flattened.shape[0], dtype=jnp.int32))
    )
    counts = jnp.sum(onehot, axis=0)
    slots_occupied = (jnp.arange(capacity, dtype=jnp.int32)[None, :] < counts[:, None]).reshape(-1)
    return (slot_ids, sources, slots_occupied)


def transposed_product(left, right):
    return lax.dot_general(
        left, right, (((1,), (1,)), ((), ())), preferred_element_type=jnp.float32
    )


def inner_product(left, right):
    return lax.dot_general(
        left, right, (((0,), (0,)), ((), ())), preferred_element_type=jnp.float32
    )


def on_device(
    tokens, expert_ids, upstream, gain, router, gate_weight_matrix, up_weight, down_weight
):
    experts = lax.axis_size("expert")
    tok_rows = tokens.shape[0]
    width = tokens.shape[1]
    feed = gate_weight_matrix.shape[2]
    capacity = 3 * tok_rows // experts
    source = tokens.astype(jnp.float32)
    inverse = lax.rsqrt(jnp.mean(source * source, axis=-1, keepdims=True) + norm_eps)
    unit_rows = source * inverse
    normed = (unit_rows * gain).astype(jnp.bfloat16)
    scores = jax.nn.sigmoid(jnp.dot(normed, router, preferred_element_type=jnp.float32))
    picked = expert_ids[:, :, None] == jnp.arange(experts, dtype=jnp.int32)[None, None, :]
    chosen = jnp.sum(jnp.where(picked, scores[:, None, :], 0.0), axis=2)
    total = jnp.sum(chosen, axis=1, keepdims=True)
    gates = chosen / total
    slot_ids, sources, slots_occupied = slot_layout(expert_ids, experts, capacity)
    slot_pairs = slot_ids.reshape(tok_rows, 2)
    send_rows = jnp.where(
        slots_occupied[:, None], normed[sources // 2], jnp.zeros((), jnp.bfloat16)
    )
    arrived = lax.all_to_all(
        send_rows.reshape(experts, capacity, width),
        "expert",
        split_axis=0,
        concat_axis=0,
        tiled=True,
    )
    expert_in = arrived.reshape(experts * capacity, width)
    pieces = (
        lax.all_gather(gate_weight_matrix, "dp", axis=1, tiled=True),
        lax.all_gather(up_weight, "dp", axis=1, tiled=True),
    )
    columns = expert_in
    pre_gate = jnp.dot(columns, pieces[0][0], preferred_element_type=jnp.float32)
    pre_up = jnp.dot(columns, pieces[1][0], preferred_element_type=jnp.float32)
    sigma = jax.nn.sigmoid(pre_gate)
    active = pre_gate * sigma
    hidden = (active * pre_up).astype(jnp.bfloat16)
    expert_out = jnp.dot(
        hidden,
        lax.all_gather(down_weight, "dp", axis=2, tiled=True)[0],
        preferred_element_type=jnp.float32,
    ).astype(jnp.bfloat16)
    returned = lax.all_to_all(
        expert_out.reshape(experts, capacity, width),
        "expert",
        split_axis=0,
        concat_axis=0,
        tiled=True,
    )
    outputs = returned.reshape(experts * capacity, width)[slot_pairs].astype(jnp.float32)
    combined = gates[:, :, None] * outputs
    mixed = (source + combined[:, 0] + combined[:, 1]).astype(jnp.bfloat16)
    cotangent = upstream.astype(jnp.float32)
    d_gates = jnp.sum(cotangent[:, None, :] * outputs, axis=2)
    weight_rows = gates.reshape(-1)[sources]
    d_send = jnp.where(
        slots_occupied[:, None], weight_rows[:, None] * cotangent[sources // 2], 0.0
    ).astype(jnp.bfloat16)
    d_arrived = lax.all_to_all(
        d_send.reshape(experts, capacity, width), "expert", split_axis=0, concat_axis=0, tiled=True
    )
    d_out = d_arrived.reshape(experts * capacity, width)
    columns = d_out
    d_hidden = transposed_product(columns, lax.all_gather(down_weight, "dp", axis=2, tiled=True)[0])
    d_pre_gate = (d_hidden * pre_up * sigma * (1.0 + pre_gate * (1.0 - sigma))).astype(jnp.bfloat16)
    d_pre_up = (d_hidden * active).astype(jnp.bfloat16)
    pieces = (
        lax.all_gather(gate_weight_matrix, "dp", axis=1, tiled=True),
        lax.all_gather(up_weight, "dp", axis=1, tiled=True),
    )
    block = transposed_product(d_pre_gate, pieces[0][0]) + transposed_product(
        d_pre_up, pieces[1][0]
    )
    d_rows = block.astype(jnp.bfloat16)
    d_back = lax.all_to_all(
        d_rows.reshape(experts, capacity, width), "expert", split_axis=0, concat_axis=0, tiled=True
    )
    d_parts = d_back.reshape(experts * capacity, width)[slot_pairs].astype(jnp.float32)
    grad_rows = lax.psum_scatter(
        jnp.concatenate(
            [
                inner_product(expert_in, d_pre_gate),
                inner_product(expert_in, d_pre_up),
                inner_product(d_out, hidden),
            ],
            axis=1,
        ).astype(jnp.bfloat16),
        "dp",
        scatter_dimension=0,
        tiled=True,
    ).astype(jnp.float32)
    gate_weight_gradient = grad_rows[:, :feed].astype(jnp.bfloat16)[None]
    up_weight_gradient = grad_rows[:, feed : 2 * feed].astype(jnp.bfloat16)[None]
    down_weight_gradient = grad_rows[:, 2 * feed :].T.astype(jnp.bfloat16)[None]
    blended = jnp.sum(gates * d_gates, axis=1, keepdims=True)
    d_chosen = (d_gates - blended) / total
    d_logit = d_chosen * chosen * (1.0 - chosen)
    d_logits = jnp.sum(jnp.where(picked, d_logit[:, :, None], 0.0), axis=1)
    router_float = router.astype(jnp.float32)
    d_normed = (
        d_parts[:, 0]
        + d_parts[:, 1]
        + jnp.dot(d_logits, router_float.T, precision=lax.Precision.HIGHEST)
    )
    d_unit = d_normed * gain
    inner = jnp.mean(d_unit * unit_rows, axis=-1, keepdims=True)
    d_tokens = (cotangent + inverse * (d_unit - unit_rows * inner)).astype(jnp.bfloat16)
    part_router = jnp.dot(normed.astype(jnp.float32).T, d_logits, precision=lax.Precision.HIGHEST)
    part_gain = jnp.sum(d_normed * unit_rows, axis=0)
    d_router, d_gain = lax.psum((part_router, part_gain), ("dp", "expert"))
    return (
        mixed,
        d_tokens,
        gate_weight_gradient,
        up_weight_gradient,
        down_weight_gradient,
        d_router,
        d_gain,
    )


def solution(mesh):
    return jax.shard_map(
        on_device,
        mesh=mesh,
        in_specs=(
            P(("dp", "expert"), None),
            P(("dp", "expert"), None),
            P(("dp", "expert"), None),
            P(),
            P(),
            P("expert", "dp", None),
            P("expert", "dp", None),
            P("expert", None, "dp"),
        ),
        out_specs=(
            P(("dp", "expert"), None),
            P(("dp", "expert"), None),
            P("expert", "dp", None),
            P("expert", "dp", None),
            P("expert", None, "dp"),
            P(),
            P(),
        ),
        check_vma=False,
    )
```

profile of v0, /device:TPU:0, one launch (start us, length us, event | category | flops | bytes accessed | tf_op | source)
XLA Modules:
  0.0 484.3 jit_solution(9917308662178683942)
XLA Ops:
  13.0 2.5 gather_fusion
  15.8 44.1 %all_to_all.20 = bf16[8,48,2048]{2,1,0:T(8,128)(2,1)S(1)} all-to-all(bf16[8,48,2048]{2,1,0:T(8,128)(2,1)S(1)} %broadcast_select_fusion), channel_id=1, replica_groups=mesh['dp'=4,'expert'=8] {'expert'}, dimensions={0} | all-to-all | bytes 3145728 | tf_op jit(solution)/shard_map/all_to_all | solution.py:58
  59.8 5.7 %fusion.10 = f32[384,1024]{1,0:T(8,128)} fusion(bf16[384,2048]{1,0:T(8,128)(2,1)S(1)} %bitcast.82, bf16[1,2048,1024]{2,1,0:T(8,128)(2,1)} %all-gather.4.cloned.1.call-done), kind=kOutput, calls=%fused_computation.17 | convolution fusion | flops 1610612736 | bytes 7340032 | tf_op jit(solution)/shard_map/dot_general | solution.py:71
  65.5 17.4 %all-gather.6.cloned.1.call-done = bf16[1,2048,1024]{2,1,0:T(8,128)(2,1)} async-done(((bf16[1,512,1024]{2,1,0:T(8,128)(2,1)}), bf16[1,2048,1024]{2,1,0:T(8,128)(2,1)}) %all-gather.6.cloned.1.call-update) | async-done | bytes 4194320 | tf_op jit(solution)/shard_map/all_gather | solution.py:68
  82.9 5.8 %multiply_convert_fusion.2 = (bf16[384,1024]{1,0:T(8,128)(2,1)S(1)}, f32[384,1024]{1,0:T(8,128)}) fusion(f32[384,1024]{1,0:T(8,128)} %fusion.10, bf16[384,2048]{1,0:T(8,128)(2,1)S(1)} %bitcast.83, bf16[1,2048,1024]{2,1,0:T(8,128)(2,1)} %all-gather.6.cloned.1.call-done), kind=kOutput, calls=%fused_computation.30 | convolution fusion | flops 1612972032 | bytes 9699328 | tf_op jit(solution)/shard_map/dot_general | solution.py:72
  88.7 30.3 %all-gather.8.cloned.1.call-done = bf16[1,1024,2048]{2,1,0:T(8,128)(2,1)} async-done(((bf16[1,1024,512]{2,1,0:T(8,128)(2,1)}), bf16[1,1024,2048]{2,1,0:T(8,128)(2,1)}) %all-gather.8.cloned.1.call-update) | async-done | bytes 4194320 | tf_op jit(solution)/shard_map/all_gather | solution.py:78
  119.0 5.2 %fusion.14 = bf16[384,2048]{1,0:T(8,128)(2,1)} fusion(bf16[384,1024]{1,0:T(8,128)(2,1)S(1)} %get-tuple-element.56, bf16[1,1024,2048]{2,1,0:T(8,128)(2,1)} %all-gather.8.cloned.1.call-done), kind=kOutput, calls=%fused_computation.24 | convolution fusion | flops 1611399168 | bytes 6553600 | tf_op jit(solution)/shard_map/dot_general | solution.py:76
  124.2 5.5 %all-to-all-start.1 = ((bf16[8,48,2048]{2,1,0:T(8,128)(2,1)}), bf16[8,48,2048]{2,1,0:T(8,128)(2,1)S(1)}, u32[]{:S(2)}, u32[]{:S(2)}) async-start(bf16[8,48,2048]{2,1,0:T(8,128)(2,1)} %bitcast.87), calls=%async_computation.1 | async-start | bytes 3145728 | tf_op jit(solution)/shard_map/all_to_all | solution.py:81
  131.5 3.3 gather_fusion.3
  135.1 32.0 %all-to-all-done.1 = bf16[8,48,2048]{2,1,0:T(8,128)(2,1)S(1)} async-done(((bf16[8,48,2048]{2,1,0:T(8,128)(2,1)}), bf16[8,48,2048]{2,1,0:T(8,128)(2,1)S(1)}, u32[]{:S(2)}, u32[]{:S(2)}) %all-to-all-start.1) | async-done | bytes 1572896 | tf_op jit(solution)/shard_map/all_to_all | solution.py:81
  167.1 2.3 gather_fusion.1
  169.4 3.4 reshape.257
  172.9 2.7 multiply_reduce_fusion
  176.0 2.8 gather_fusion.2
  181.1 40.9 %all_to_all.21 = bf16[8,48,2048]{2,1,0:T(8,128)(2,1)S(1)} all-to-all(bf16[8,48,2048]{2,1,0:T(8,128)(2,1)S(1)} %select_convert_fusion), channel_id=1, replica_groups=mesh['dp'=4,'expert'=8] {'expert'}, dimensions={0} | all-to-all | bytes 3145728 | tf_op jit(solution)/shard_map/all_to_all | solution.py:97
  222.0 2.4 convolution_convert_fusion
  225.1 2.3 multiply_convert_fusion.1
  227.4 2.4 convolution_convert_fusion.2
  229.8 2.4 convolution_convert_fusion.1
  232.2 21.4 %pad_maximum_fusion = bf16[2048,3072]{0,1:T(8,128)(2,1)} fusion(bf16[2048,1024]{0,1:T(8,128)(2,1)S(1)} %convolution_convert_fusion, bf16[2048,1024]{0,1:T(8,128)(2,1)S(1)} %convolution_convert_fusion.1, bf16[2048,1024]{0,1:T(8,128)(2,1)S(1)} %convolution_convert_fusion.2), kind=kLoop, calls=%fused_computation.6 | loop fusion | flops 37748736 | bytes 25165824 | tf_op jit(solution)/shard_map/concatenate | solution.py:118
  253.7 4.2 fusion.4
  257.9 3.1 add_convert_fusion
  260.9 3.7 all-to-all-start.3
  265.7 4.7 copy_multiply_fusion
  270.4 30.8 %all-to-all-done.3 = bf16[8,48,2048]{2,1,0:T(8,128)(2,1)S(1)} async-done(((bf16[8,48,2048]{2,1,0:T(8,128)(2,1)}), bf16[8,48,2048]{2,1,0:T(8,128)(2,1)S(1)}, u32[]{:S(2)}, u32[]{:S(2)}) %all-to-all-start.3) | async-done | bytes 1572896 | tf_op jit(solution)/shard_map/all_to_all | solution.py:113
  301.2 2.3 gather_fusion.4
  303.6 2.6 reshape.258
  307.9 2.3 fusion.31
  310.2 37.4 %psum.15 = f32[2048]{0:T(1024)} all-reduce(f32[2048]{0:T(1024)S(1)} %get-tuple-element.35), channel_id=1, replica_groups=mesh['dp'=4,'expert'=8] {'dp','expert'}, use_global_device_ids=true, to_apply=%region_15.16 | all-reduce | flops 2048 | bytes 16384 | tf_op jit(solution)/shard_map/psum | solution.py:148
  347.6 2.7 fusion.30
  352.4 3.0 slice_bitcast_fusion
  358.1 118.0 %all-reduce.2.cloned.1.call-done = f32[2048,8]{0,1:T(8,128)} async-done(((f32[2048,8]{0,1:T(8,128)}), f32[2048,8]{0,1:T(8,128)}) %all-reduce.2.cloned.1.call-update) | async-done | bytes 65552 | tf_op jit(solution)/shard_map/psum | solution.py:148
  (84 shorter events, 20.3 us)
Async XLA Ops:
  7.2 127.7 %copy-start = (bf16[2048,8]{0,1:T(8,128)(2,1)S(1)}, bf16[2048,8]{0,1:T(8,128)(2,1)}, u32[]{:S(2)}) copy-start(bf16[2048,8]{0,1:T(8,128)(2,1)} %param.12) | copy-start | bytes 98308
  7.2 2.3 copy-start.8
  7.2 5.4 %copy-start.1 = (bf16[128,2048]{1,0:T(8,128)(2,1)S(1)}, bf16[128,2048]{1,0:T(8,128)(2,1)}, u32[]{:S(2)}) copy-start(bf16[128,2048]{1,0:T(8,128)(2,1)} %param.8) | copy-start | bytes 1572868
  7.2 5.6 %copy-start.7 = (f32[2048]{0:T(1024)S(1)}, f32[2048]{0:T(1024)}, u32[]{:S(2)}) copy-start(f32[2048]{0:T(1024)} %param.11) | copy-start | bytes 24580
  7.2 52.6 %all-gather.4.cloned.1.call-start = ((), (), s32[]{:S(2)}) async-start(), calls=%async_computation.5 | async-start | bytes 5242880 | tf_op jit(solution)/shard_map/all_gather | solution.py:67
  7.9 75.0 %all-gather.6.cloned.1.call-start = ((), (), s32[]{:S(2)}) async-start(), calls=%async_computation.6 | async-start | bytes 5242880 | tf_op jit(solution)/shard_map/all_gather | solution.py:68
  8.7 110.3 %all-gather.8.cloned.1.call-start = ((), (), s32[]{:S(2)}) async-start(), calls=%async_computation.7 | async-start | bytes 5242880 | tf_op jit(solution)/shard_map/all_gather | solution.py:78
  59.8 23.1 %copy-start.5 = (bf16[8,48,2048]{2,1,0:T(8,128)(2,1)}, bf16[8,48,2048]{2,1,0:T(8,128)(2,1)S(1)}, u32[]{:S(2)}) copy-start(bf16[8,48,2048]{2,1,0:T(8,128)(2,1)S(1)} %all_to_all.20) | copy-start | bytes 4718596
  88.7 35.5 %copy-start.11 = (bf16[384,1024]{1,0:T(8,128)(2,1)}, bf16[384,1024]{1,0:T(8,128)(2,1)S(1)}, u32[]{:S(2)}) copy-start(bf16[384,1024]{1,0:T(8,128)(2,1)S(1)} %get-tuple-element.56) | copy-start | bytes 2359300
  124.2 42.9 %all-to-all-start.1 = ((bf16[8,48,2048]{2,1,0:T(8,128)(2,1)}), bf16[8,48,2048]{2,1,0:T(8,128)(2,1)S(1)}, u32[]{:S(2)}, u32[]{:S(2)}) async-start(bf16[8,48,2048]{2,1,0:T(8,128)(2,1)} %bitcast.87), calls=%async_computation.1 | async-start | bytes 3145728 | tf_op jit(solution)/shard_map/all_to_all | solution.py:81
  129.7 222.7 %reduce-scatter.2.cloned.1.call-start = ((), (), s32[]{:S(2)}) async-start(), calls=%async_computation.8 | async-start | bytes 15728640 | tf_op jit(solution)/shard_map/reduce_scatter | solution.py:117
  181.1 40.9 %copy-start.12 = (bf16[384,1024]{1,0:T(8,128)(2,1)S(1)}, bf16[384,1024]{1,0:T(8,128)(2,1)}, u32[]{:S(2)}) copy-start(bf16[384,1024]{1,0:T(8,128)(2,1)} %copy-done.11) | copy-start | bytes 2359300
  222.0 2.4 copy-start.10
  222.0 2.7 copy-start.13
  222.0 3.1 copy-start.14
  225.1 2.3 copy-start.6
  253.7 4.2 copy-start.9
  260.9 40.3 %all-to-all-start.3 = ((bf16[8,48,2048]{2,1,0:T(8,128)(2,1)}), bf16[8,48,2048]{2,1,0:T(8,128)(2,1)S(1)}, u32[]{:S(2)}, u32[]{:S(2)}) async-start(bf16[8,48,2048]{2,1,0:T(8,128)(2,1)} %bitcast.86), calls=%async_computation.3 | async-start | bytes 3145728 | tf_op jit(solution)/shard_map/all_to_all | solution.py:113
  264.7 211.4 %all-reduce.2.cloned.1.call-start = ((), (), s32[]{:S(2)}) async-start(), calls=%async_computation.9 | async-start | bytes 131072 | tf_op jit(solution)/shard_map/psum | solution.py:148
  306.2 1.7 copy-start.2
  307.8 39.7 %copy-start.3 = (f32[128,2,2048]{2,0,1:T(8,128)S(1)}, f32[128,2,2048]{2,0,1:T(8,128)}, u32[]{:S(2)}) copy-start(f32[128,2,2048]{2,0,1:T(8,128)} %copy_multiply_fusion) | copy-start | bytes 6291460
  307.8 39.7 %copy-start.4 = (bf16[128,2048]{1,0:T(8,128)(2,1)S(1)}, bf16[128,2048]{1,0:T(8,128)(2,1)}, u32[]{:S(2)}) copy-start(bf16[128,2048]{1,0:T(8,128)(2,1)} %param.10) | copy-start | bytes 1572868
Sparse Core Ops, SparseCore 0:
  9.6 37.1 all-gather.3
  48.4 34.4 all-gather.5
  84.5 34.4 all-gather.7
  253.8 98.5 reduce-scatter.1
  358.4 117.5 all-reduce.1
where the time goes:
time: 492 us; the launch traced here: 484 us
  waiting for transfers between devices  233 us (47%)
  blocking collectives  122 us (25%)
  matrix products  36.9 us (8%)
  other arithmetic  36.5 us (7%)
  local copies, waits for them, and re-layouts  31.5 us (6%)
  between operations  14.4 us (3%)
  starting transfers between devices  9.92 us (2%)
    psum x1, waiting for transfers between devices, on_device(): d_router, d_gain = lax.psum((part_router, part_gain), ('dp', 'expert'))  118 us
    all_to_all x1, blocking collectives, on_device(): lax.all_to_all(send_rows.reshape(experts, capacity, width), 'expert', spl...  44.1 us
    all_to_all x1, blocking collectives, on_device(): lax.all_to_all(d_send.reshape(experts, capacity, width), 'expert', split_...  40.9 us
    psum x1, blocking collectives, on_device(): d_router, d_gain = lax.psum((part_router, part_gain), ('dp', 'expert'))  37.4 us
    all_to_all x1, waiting for transfers between devices, on_device(): lax.all_to_all(expert_out.reshape(experts, capacity, width), 'expert', sp...  32 us
    all_to_all x1, waiting for transfers between devices, on_device(): lax.all_to_all(d_rows.reshape(experts, capacity, width), 'expert', split_...  30.8 us
    all_gather x1, waiting for transfers between devices, on_device(): lax.all_gather(down_weight, 'dp', axis=2, tiled=True)[0]  30.3 us
    concatenate x1, other arithmetic, on_device(): jnp.concatenate([inner_product(expert_in, d_pre_gate), inner_product(expe...  21.4 us
  transfers between devices with their start and end apart: 7, of which 6 were waited for; matrix products, arithmetic and copies ran while one was open for 11% of the time, Pallas kernels for 0%

commit v1 on v0

v1 whole, which is shorter than its diff:
```python
import jax
import jax.numpy as jnp
from jax import lax
from jax.sharding import PartitionSpec as P

norm_eps = 1e-06


def product(left, right):
    return jnp.dot(left, right, preferred_element_type=jnp.float32)


def transposed_product(left, right):
    return lax.dot_general(
        left, right, (((1,), (1,)), ((), ())), preferred_element_type=jnp.float32
    )


def inner_product(left, right):
    return lax.dot_general(
        left, right, (((0,), (0,)), ((), ())), preferred_element_type=jnp.float32
    )


def slot_pairs_of(expert_ids, experts, capacity):
    flattened = expert_ids.reshape(-1)
    onehot = (flattened[:, None] == jnp.arange(experts, dtype=jnp.int32)[None, :]).astype(jnp.int32)
    ranking = jnp.sum(jnp.cumsum(onehot, axis=0) * onehot, axis=1) - 1
    return (flattened * capacity + ranking).reshape(expert_ids.shape)


def to_sibling(value):
    count = lax.axis_size("dp")
    return lax.ppermute(value, "dp", [(i, i ^ 1) for i in range(count)])


def to_chip(value, step):
    count = lax.axis_size("dp")
    return lax.ppermute(value, "dp", [(i, (i + 2 * step) % count) for i in range(count)])


def sum_over_all(value):
    for axis in ("dp", "expert"):
        count = lax.axis_size(axis)
        hop = 1
        while hop < count:
            value = value + lax.ppermute(value, axis, [(i, i ^ hop) for i in range(count)])
            hop *= 2
    return value


def on_device(
    tokens, expert_ids, upstream, gain, router, gate_weight_matrix, up_weight, down_weight
):
    experts = lax.axis_size("expert")
    dp_count = lax.axis_size("dp")
    chips = dp_count // 2
    me = lax.axis_index("dp")
    tok_rows, width = tokens.shape
    feed = gate_weight_matrix.shape[2]
    part = width // dp_count
    capacity = 3 * tok_rows // experts
    slots = experts * capacity

    shard = (gate_weight_matrix[0], up_weight[0], down_weight[0])
    pieces = []
    owners = []
    for k in range(chips):
        arrived = shard if k == 0 else tuple(to_chip(w, k) for w in shard)
        pieces.append(arrived)
        pieces.append(tuple(to_sibling(w) for w in arrived))
        owner = lax.rem(me - 2 * k + dp_count, dp_count)
        owners.append(owner)
        owners.append(owner + 1 - 2 * lax.rem(owner, 2))

    source = tokens.astype(jnp.float32)
    inverse = lax.rsqrt(jnp.mean(source * source, axis=-1, keepdims=True) + norm_eps)
    unit_rows = source * inverse
    normed = (unit_rows * gain).astype(jnp.bfloat16)
    scores = jax.nn.sigmoid(product(normed, router))
    picked = expert_ids[:, :, None] == jnp.arange(experts, dtype=jnp.int32)[None, None, :]
    chosen = jnp.sum(jnp.where(picked, scores[:, None, :], 0.0), axis=2)
    total = jnp.sum(chosen, axis=1, keepdims=True)
    gates = chosen / total

    slot_pairs = slot_pairs_of(expert_ids, experts, capacity)
    places = jnp.arange(slots, dtype=jnp.int32)
    first = places[:, None] == slot_pairs[None, :, 0]
    second = places[:, None] == slot_pairs[None, :, 1]
    fill = (first | second).astype(jnp.bfloat16)
    slot_gate = jnp.sum(
        jnp.where(first, gates[None, :, 0], jnp.where(second, gates[None, :, 1], 0.0)),
        axis=1,
        keepdims=True,
    )
    send_rows = product(fill, normed).astype(jnp.bfloat16)
    d_send = (slot_gate * product(fill, upstream)).astype(jnp.bfloat16)
    arrived = lax.all_to_all(
        jnp.concatenate(
            [
                send_rows.reshape(experts, capacity, width),
                d_send.reshape(experts, capacity, width),
            ],
            axis=1,
        ),
        "expert",
        split_axis=0,
        concat_axis=0,
        tiled=True,
    )
    expert_in = arrived[:, :capacity].reshape(slots, width)
    d_out = arrived[:, capacity:].reshape(slots, width)
    in_parts = [lax.dynamic_slice_in_dim(expert_in, o * part, part, 1) for o in owners]
    out_parts = [lax.dynamic_slice_in_dim(d_out, o * part, part, 1) for o in owners]

    pre_gate = sum(product(x, w[0]) for x, w in zip(in_parts, pieces))
    pre_up = sum(product(x, w[1]) for x, w in zip(in_parts, pieces))
    sigma = jax.nn.sigmoid(pre_gate)
    active = pre_gate * sigma
    hidden = (active * pre_up).astype(jnp.bfloat16)

    def in_order(parts):
        whole = jnp.zeros((slots, width), jnp.bfloat16)
        for o, value in zip(owners, parts):
            whole = lax.dynamic_update_slice_in_dim(whole, value, o * part, 1)
        return whole

    def send_back(rows):
        return lax.all_to_all(
            rows.reshape(experts, capacity, width),
            "expert",
            split_axis=0,
            concat_axis=0,
            tiled=True,
        ).reshape(slots, width)

    expert_out = in_order([product(hidden, w[2]).astype(jnp.bfloat16) for w in pieces])
    returned = send_back(expert_out)

    d_hidden = sum(transposed_product(x, w[2]) for x, w in zip(out_parts, pieces))
    d_pre_gate = (d_hidden * pre_up * sigma * (1.0 + pre_gate * (1.0 - sigma))).astype(jnp.bfloat16)
    d_pre_up = (d_hidden * active).astype(jnp.bfloat16)

    def shares(index):
        x, d = in_parts[index], out_parts[index]
        return (
            inner_product(x, d_pre_gate).astype(jnp.bfloat16),
            inner_product(x, d_pre_up).astype(jnp.bfloat16),
            inner_product(hidden, d).astype(jnp.bfloat16),
        )

    totals = None
    for k in list(range(1, chips)) + [0]:
        theirs = [to_sibling(v) for v in shares(2 * k + 1)]
        mine = shares(2 * k)
        both = [a.astype(jnp.float32) + b.astype(jnp.float32) for a, b in zip(mine, theirs)]
        if k:
            both = [
                to_chip(v.astype(jnp.bfloat16), chips - k).astype(jnp.float32) for v in both
            ]
        totals = both if totals is None else [a + b for a, b in zip(totals, both)]
    weight_gradients = [v.astype(jnp.bfloat16)[None] for v in totals]

    d_rows = in_order(
        [
            (transposed_product(d_pre_gate, w[0]) + transposed_product(d_pre_up, w[1])).astype(
                jnp.bfloat16
            )
            for w in pieces
        ]
    )
    d_back = send_back(d_rows)

    cotangent = upstream.astype(jnp.float32)
    first_out = inner_product(first.astype(jnp.bfloat16), returned)
    second_out = inner_product(second.astype(jnp.bfloat16), returned)
    mixed = (source + gates[:, :1] * first_out + gates[:, 1:] * second_out).astype(jnp.bfloat16)
    d_gates = jnp.concatenate(
        [
            jnp.sum(cotangent * first_out, axis=1, keepdims=True),
            jnp.sum(cotangent * second_out, axis=1, keepdims=True),
        ],
        axis=1,
    )
    blended = jnp.sum(gates * d_gates, axis=1, keepdims=True)
    d_chosen = (d_gates - blended) / total
    d_logit = d_chosen * chosen * (1.0 - chosen)
    d_logits = jnp.sum(jnp.where(picked, d_logit[:, :, None], 0.0), axis=1)
    part_router = lax.dot_general(
        d_logits,
        normed.astype(jnp.float32),
        (((0,), (0,)), ((), ())),
        precision=lax.Precision.HIGHEST,
    )
    d_router = sum_over_all(part_router).T
    through_router = jnp.dot(
        d_logits, router.astype(jnp.float32).T, precision=lax.Precision.HIGHEST
    )

    d_normed = inner_product(fill, d_back) + through_router
    d_unit = d_normed * gain
    inner = jnp.mean(d_unit * unit_rows, axis=-1, keepdims=True)
    d_tokens = (cotangent + inverse * (d_unit - unit_rows * inner)).astype(jnp.bfloat16)
    part_gain = jnp.sum(d_normed * unit_rows, axis=0)
    d_gain = sum_over_all(part_gain.reshape(-1, 128)).reshape(-1)
    return (mixed, d_tokens, *weight_gradients, d_router, d_gain)


def solution(mesh):
    return jax.shard_map(
        on_device,
        mesh=mesh,
        in_specs=(
            P(("dp", "expert"), None),
            P(("dp", "expert"), None),
            P(("dp", "expert"), None),
            P(),
            P(),
            P("expert", "dp", None),
            P("expert", "dp", None),
            P("expert", None, "dp"),
        ),
        out_specs=(
            P(("dp", "expert"), None),
            P(("dp", "expert"), None),
            P("expert", "dp", None),
            P("expert", "dp", None),
            P("expert", None, "dp"),
            P(),
            P(),
        ),
        check_vma=False,
    )
```

time: 492 us -> 263 us (0.53); the launches traced: 484 us -> 261 us
  blocking collectives: 122 us -> 0 us
  waiting for transfers between devices: 233 us -> 128 us
  matrix products: 36.9 us -> 70.1 us
  starting transfers between devices: 9.92 us -> 39.2 us
  local copies, waits for them, and re-layouts: 31.5 us -> 7.14 us
  other arithmetic: 36.5 us -> 15.3 us
  between operations: 14.4 us -> 1.25 us
    psum x1 -> x0, waiting for transfers between devices: 118 us -> none  [on_device(): d_router, d_gain = lax.psum((part_router, part_gain), ('dp', 'expert'))]
    all_to_all x2 -> x0, blocking collectives: 84.9 us -> none  [the longest x1 44.1 us: on_device(): lax.all_to_all(send_rows.reshape(experts, capacity, width), 'expert', spl...]
    all_gather x3 -> x0, waiting for transfers between devices: 47.7 us -> none  [the longest x1 30.3 us: on_device(): lax.all_gather(down_weight, 'dp', axis=2, tiled=True)[0]]
    ppermute x0 -> x28, waiting for transfers between devices: none -> 47.2 us  [the longest x6 25.9 us: to_chip(): lax.ppermute(value, 'dp', [(i, (i + 2 * step) % count) for i in range(cou...]
    psum x1 -> x0, blocking collectives: 37.4 us -> none  [on_device(): d_router, d_gain = lax.psum((part_router, part_gain), ('dp', 'expert'))]
    dot_general x3 -> x15, matrix products: 7.25 us -> 30.6 us  [inner_product(): lax.dot_general(left, right, (((0,), (0,)), ((), ())), preferred_element_...]
    ppermute x0 -> x28, starting transfers between devices: none -> 22.7 us  [the longest x10 12.8 us: sum_over_all(): lax.ppermute(value, axis, [(i, i ^ hop) for i in range(count)])]
    concatenate x1, other arithmetic: 21.4 us -> 2.03 us  [on_device(): jnp.concatenate([send_rows.reshape(experts, capacity, width), d_send.resh...]
  transfers between devices with their start and end apart: 7 -> 31, of which waited for: 6 -> 9; matrix products, arithmetic and copies ran while one was open for 11% -> 26% of each run, Pallas kernels for 0% -> 0%
where the time goes in v1:
time: 263 us; the launch traced here: 261 us
  waiting for transfers between devices  128 us (49%)
  matrix products  70.1 us (27%)
  starting transfers between devices  39.2 us (15%)
  other arithmetic  15.3 us (6%)
  local copies, waits for them, and re-layouts  7.14 us (3%)
    all_to_all x1, waiting for transfers between devices, on_device(): lax.all_to_all(jnp.concatenate([send_rows.reshape(experts, capacity, widt...  66.9 us
    dot_general x15, matrix products, inner_product(): lax.dot_general(left, right, (((0,), (0,)), ((), ())), preferred_element_...  30.6 us
    ppermute x6, waiting for transfers between devices, to_chip(): lax.ppermute(value, 'dp', [(i, (i + 2 * step) % count) for i in range(cou...  25.9 us
    ppermute x10, waiting for transfers between devices, sum_over_all(): lax.ppermute(value, axis, [(i, i ^ hop) for i in range(count)])  21.2 us
    dot_general x12, matrix products, transposed_product(): lax.dot_general(left, right, (((1,), (1,)), ((), ())), preferred_element_...  20 us
    dot_general x15, matrix products, product(): return jnp.dot(left, right, preferred_element_type=jnp.float32)  18.2 us
    all_to_all x2, waiting for transfers between devices, send_back(): lax.all_to_all(rows.reshape(experts, capacity, width), 'expert', split_ax...  14.2 us
    ppermute x10, starting transfers between devices, sum_over_all(): lax.ppermute(value, axis, [(i, i ^ hop) for i in range(count)])  12.8 us
  transfers between devices with their start and end apart: 31, of which 9 were waited for; matrix products, arithmetic and copies ran while one was open for 26% of the time, Pallas kernels for 0%

profile of v1, /device:TPU:0, one launch (start us, length us, event | category | flops | bytes accessed | tf_op | source)
XLA Modules:
  0.0 261.4 jit_solution(8983843219451211271)
XLA Ops:
  7.1 2.0 pad_maximum_fusion
  9.2 7.4 %all-to-all-start = ((bf16[8,96,2048]{2,1,0:T(8,128)(2,1)}), bf16[8,96,2048]{2,1,0:T(8,128)(2,1)}, u32[]{:S(2)}, u32[]{:S(2)}) async-start(bf16[8,96,2048]{2,1,0:T(8,128)(2,1)} %pad_maximum_fusion), calls=%async_computation | async-start | bytes 6291456 | tf_op jit(solution)/shard_map/all_to_all | solution.py:98
  20.4 66.9 %all-to-all-done = bf16[8,96,2048]{2,1,0:T(8,128)(2,1)} async-done(((bf16[8,96,2048]{2,1,0:T(8,128)(2,1)}), bf16[8,96,2048]{2,1,0:T(8,128)(2,1)}, u32[]{:S(2)}, u32[]{:S(2)}) %all-to-all-start) | async-done | bytes 3145760 | tf_op jit(solution)/shard_map/all_to_all | solution.py:98
  87.4 2.1 fusion.120
  91.9 1.8 fusion.43
  98.1 1.8 fusion.37
  102.3 1.8 fusion.59
  115.1 1.8 fusion.16
  121.1 4.5 %all-to-all-start.1 = ((bf16[8,48,2048]{2,1,0:T(8,128)(2,1)}), bf16[8,48,2048]{2,1,0:T(8,128)(2,1)}, u32[]{:S(2)}, u32[]{:S(2)}) async-start(bf16[8,48,2048]{2,1,0:T(8,128)(2,1)} %bitcast.119), calls=%async_computation.1 | async-start | bytes 3145728 | tf_op jit(solution)/shard_map/all_to_all | solution.py:129
  125.6 1.8 fusion.113
  130.3 1.8 fusion.121
  132.2 1.9 fusion.122
  137.5 2.7 %fusion.8 = bf16[384,2048]{1,0:T(8,128)(2,1)} fusion(bf16[384,2048]{1,0:T(8,128)(2,1)} %fusion.6, s32[]{:T(128)S(6)} %select_n.44, f32[384,512]{1,0:T(8,128)S(1)} %fusion.121, bf16[384,1024]{1,0:T(8,128)(2,1)S(1)} %get-tuple-element.14, bf16[512,1024]{1,0:T(8,128)(2,1)} %collective-permute-done), kind=kOutput, calls=%fused_computation.47 | convolution fusion | flops 403046400 | bytes 3014660 | tf_op jit(solution)/shard_map/dot_general | solution.py:14
  140.2 2.7 %convolution_convert_fusion.2 = bf16[1024,512]{1,0:T(8,128)(2,1)} fusion(bf16[384,1024]{1,0:T(8,128)(2,1)S(1)} %copy-done.19, bf16[384,2048]{1,0:T(8,128)(2,1)} %bitcast.128, s32[]{:T(128)S(6)} %select_n.43), kind=kOutput, calls=%fused_computation.29 | convolution fusion | flops 403177472 | bytes 2228228 | tf_op jit(solution)/shard_map/dot_general | solution.py:20
  142.9 2.7 %fusion.10 = bf16[384,2048]{1,0:T(8,128)(2,1)} fusion(bf16[384,2048]{1,0:T(8,128)(2,1)} %fusion.8, s32[]{:T(128)S(6)} %select_n.45, f32[384,512]{1,0:T(8,128)S(1)} %fusion.122, bf16[384,1024]{1,0:T(8,128)(2,1)S(1)} %get-tuple-element.14, bf16[512,1024]{1,0:T(8,128)(2,1)} %collective-permute-done.1), kind=kOutput, calls=%fused_computation.49 | convolution fusion | flops 403046400 | bytes 3014660 | tf_op jit(solution)/shard_map/dot_general | solution.py:14
  148.8 14.0 %all-to-all-done.1 = bf16[8,48,2048]{2,1,0:T(8,128)(2,1)} async-done(((bf16[8,48,2048]{2,1,0:T(8,128)(2,1)}), bf16[8,48,2048]{2,1,0:T(8,128)(2,1)}, u32[]{:S(2)}, u32[]{:S(2)}) %all-to-all-start.1) | async-done | bytes 1572896 | tf_op jit(solution)/shard_map/all_to_all | solution.py:129
  162.8 4.5 %all-to-all-start.2 = ((bf16[8,48,2048]{2,1,0:T(8,128)(2,1)}), bf16[8,48,2048]{2,1,0:T(8,128)(2,1)}, u32[]{:S(2)}, u32[]{:S(2)}) async-start(bf16[8,48,2048]{2,1,0:T(8,128)(2,1)} %bitcast.15), calls=%async_computation.2 | async-start | bytes 3145728 | tf_op jit(solution)/shard_map/all_to_all | solution.py:129
  167.4 2.3 add_convert_fusion.1
  174.7 2.9 %add_convert_fusion.3 = bf16[512,1024]{1,0:T(8,128)(2,1)} fusion(bf16[512,1024]{1,0:T(8,128)(2,1)} %collective-permute-done.12, bf16[384,1024]{1,0:T(8,128)(2,1)S(1)} %get-tuple-element.13, bf16[384,2048]{1,0:T(8,128)(2,1)S(1)} %bitcast.117, s32[]{:T(128)S(6)} %select_n.45), kind=kOutput, calls=%fused_computation.7 | convolution fusion | flops 405274624 | bytes 3276804 | tf_op jit(solution)/shard_map/dot_general | solution.py:20
  178.2 2.0 add_convert_fusion.5
  181.7 14.1 %collective-permute-done.16 = bf16[1024,512]{1,0:T(8,128)(2,1)S(1)} collective-permute-done((bf16[1024,512]{1,0:T(8,128)(2,1)S(1)}, bf16[1024,512]{1,0:T(8,128)(2,1)S(1)}, u32[]{:S(2)}, u32[]{:S(2)}) %collective-permute-start.16) | collective-permute-done | bytes 1048608 | tf_op jit(solution)/shard_map/ppermute | solution.py:39
  195.9 2.6 %fusion.33 = bf16[1,1024,512]{2,1,0:T(8,128)(2,1)} fusion(bf16[1024,512]{1,0:T(8,128)(2,1)} %collective-permute-done.17, bf16[1024,512]{1,0:T(8,128)(2,1)S(1)} %copy-done.15, bf16[1024,512]{1,0:T(8,128)(2,1)S(1)} %collective-permute-done.16), kind=kLoop, calls=%fused_computation.77 | loop fusion | flops 3145728 | bytes 4194304 | tf_op jit(solution)/shard_map/broadcast_in_dim | solution.py:162
  198.5 2.0 fusion.67
  200.5 3.0 %fusion.28 = (f32[128]{0:T(128)S(1)}, f32[128]{0:T(128)S(1)}, bf16[128,2048]{1,0:T(8,128)(2,1)}) fusion(bf16[128,2048]{1,0:T(8,128)(2,1)S(1)} %copy-done.6, f32[128,2048]{1,0:T(8,128)S(1)} %fusion.67, f32[128]{0:T(128)S(1)} %get-tuple-element.22, f32[128]{0:T(128)S(1)} %get-tuple-element.21, bf16[128,2048]{1,0:T(8,128)(2,1)S(1)} %copy-done.2, ...), kind=kOutput, calls=%fused_computation.72 | convolution fusion | flops 204259072 | bytes 4196864 | tf_op jit(solution)/shard_map/dot_general | solution.py:20
  203.7 1.9 fusion.70
  206.7 11.8 %collective-permute-done.13 = bf16[512,1024]{1,0:T(8,128)(2,1)} collective-permute-done((bf16[512,1024]{1,0:T(8,128)(2,1)}, bf16[512,1024]{1,0:T(8,128)(2,1)}, u32[]{:S(2)}, u32[]{:S(2)}) %collective-permute-start.13) | collective-permute-done | bytes 1048608 | tf_op jit(solution)/shard_map/ppermute | solution.py:39
  218.5 3.1 %fusion.32 = bf16[1,512,1024]{2,1,0:T(8,128)(2,1)} fusion(bf16[512,1024]{1,0:T(8,128)(2,1)} %collective-permute-done.14, bf16[512,1024]{1,0:T(8,128)(2,1)S(1)} %copy-done.12, bf16[512,1024]{1,0:T(8,128)(2,1)} %collective-permute-done.13), kind=kLoop, calls=%fused_computation.76 | loop fusion | flops 3145728 | bytes 4194304 | tf_op jit(solution)/shard_map/broadcast_in_dim | solution.py:162
  223.7 15.4 %collective-permute-done.24 = f32[16,128]{1,0:T(8,128)S(1)} collective-permute-done((f32[16,128]{1,0:T(8,128)S(1)}, f32[16,128]{1,0:T(8,128)S(1)}, u32[]{:S(2)}, u32[]{:S(2)}) %collective-permute-start.24) | collective-permute-done | bytes 8224 | tf_op jit(solution)/shard_map/ppermute | solution.py:47
  242.2 2.8 %fusion.31 = bf16[1,512,1024]{2,1,0:T(8,128)(2,1)} fusion(bf16[512,1024]{1,0:T(8,128)(2,1)} %collective-permute-done.11, bf16[512,1024]{1,0:T(8,128)(2,1)S(1)} %copy-done.11, bf16[512,1024]{1,0:T(8,128)(2,1)S(1)} %collective-permute-done.10), kind=kLoop, calls=%fused_computation.75 | loop fusion | flops 3145728 | bytes 4194304 | tf_op jit(solution)/shard_map/broadcast_in_dim | solution.py:162
  248.7 2.3 collective-permute-start.27
  255.5 2.0 collective-permute-start.22
  258.2 2.6 collective-permute-done.22
  (156 shorter events, 66.7 us)
Async XLA Ops:
  9.2 78.2 %all-to-all-start = ((bf16[8,96,2048]{2,1,0:T(8,128)(2,1)}), bf16[8,96,2048]{2,1,0:T(8,128)(2,1)}, u32[]{:S(2)}, u32[]{:S(2)}) async-start(bf16[8,96,2048]{2,1,0:T(8,128)(2,1)} %pad_maximum_fusion), calls=%async_computation | async-start | bytes 6291456 | tf_op jit(solution)/shard_map/all_to_all | solution.py:98
  16.6 83.4 %collective-permute-start.3 = (bf16[512,1024]{1,0:T(8,128)(2,1)S(1)}, bf16[512,1024]{1,0:T(8,128)(2,1)}, u32[]{:S(2)}, u32[]{:S(2)}) collective-permute-start(bf16[512,1024]{1,0:T(8,128)(2,1)S(1)} %bitcast.130), channel_id=1, source_target_pairs={{0,8},{8,0},{16,24},{24,16},{1,9},{9,1},{17,25},{25,17},{2,10},{10... | collective-permute-start | bytes 3145736 | tf_op jit(solution)/shard_map/ppermute | solution.py:34
  16.6 77.1 %collective-permute-start.4 = (bf16[512,1024]{1,0:T(8,128)(2,1)S(1)}, bf16[512,1024]{1,0:T(8,128)(2,1)}, u32[]{:S(2)}, u32[]{:S(2)}) collective-permute-start(bf16[512,1024]{1,0:T(8,128)(2,1)S(1)} %bitcast.131), channel_id=1, source_target_pairs={{0,16},{8,24},{16,0},{24,8},{1,17},{9,25},{17,1},{25,9},{2,18},{10... | collective-permute-start | bytes 3145736 | tf_op jit(solution)/shard_map/ppermute | solution.py:39
  18.2 84.1 %collective-permute-start = (bf16[512,1024]{1,0:T(8,128)(2,1)}, bf16[512,1024]{1,0:T(8,128)(2,1)}, u32[]{:S(2)}, u32[]{:S(2)}) collective-permute-start(bf16[512,1024]{1,0:T(8,128)(2,1)} %bitcast.9), channel_id=1, source_target_pairs={{0,8},{8,0},{16,24},{24,16},{1,9},{9,1},{17,25},{25,17},{2,10},{10... | collective-permute-start | bytes 3145736 | tf_op jit(solution)/shard_map/ppermute | solution.py:34
  18.4 77.2 %collective-permute-start.1 = (bf16[512,1024]{1,0:T(8,128)(2,1)}, bf16[512,1024]{1,0:T(8,128)(2,1)}, u32[]{:S(2)}, u32[]{:S(2)}) collective-permute-start(bf16[512,1024]{1,0:T(8,128)(2,1)} %bitcast.9), channel_id=1, source_target_pairs={{0,16},{8,24},{16,0},{24,8},{1,17},{9,25},{17,1},{25,9},{2,18},{10... | collective-permute-start | bytes 3145736 | tf_op jit(solution)/shard_map/ppermute | solution.py:39
  18.9 79.1 %collective-permute-start.7 = (bf16[1024,512]{1,0:T(8,128)(2,1)}, bf16[1024,512]{1,0:T(8,128)(2,1)}, u32[]{:S(2)}, u32[]{:S(2)}) collective-permute-start(bf16[1024,512]{1,0:T(8,128)(2,1)} %bitcast.11), channel_id=1, source_target_pairs={{0,16},{8,24},{16,0},{24,8},{1,17},{9,25},{17,1},{25,9},{2,18},{10... | collective-permute-start | bytes 3145736 | tf_op jit(solution)/shard_map/ppermute | solution.py:39
  93.7 10.4 %collective-permute-start.6 = (bf16[1024,512]{1,0:T(8,128)(2,1)}, bf16[1024,512]{1,0:T(8,128)(2,1)S(1)}, u32[]{:S(2)}, u32[]{:S(2)}) collective-permute-start(bf16[1024,512]{1,0:T(8,128)(2,1)} %bitcast.11), channel_id=1, source_target_pairs={{0,8},{8,0},{16,24},{24,16},{1,9},{9,1},{17,25},{25,17},{2,10},{10... | collective-permute-start | bytes 3145736 | tf_op jit(solution)/shard_map/ppermute | solution.py:34
  95.6 9.1 %collective-permute-start.5 = (bf16[512,1024]{1,0:T(8,128)(2,1)}, bf16[512,1024]{1,0:T(8,128)(2,1)S(1)}, u32[]{:S(2)}, u32[]{:S(2)}) collective-permute-start(bf16[512,1024]{1,0:T(8,128)(2,1)} %collective-permute-done.4), channel_id=1, source_target_pairs={{0,8},{8,0},{16,24},{24,16},{1,9},{9,1},{17,25},{25,17},{2,10},{10... | collective-permute-start | bytes 3145736 | tf_op jit(solution)/shard_map/ppermute | solution.py:34
  98.0 7.7 %collective-permute-start.2 = (bf16[512,1024]{1,0:T(8,128)(2,1)}, bf16[512,1024]{1,0:T(8,128)(2,1)S(1)}, u32[]{:S(2)}, u32[]{:S(2)}) collective-permute-start(bf16[512,1024]{1,0:T(8,128)(2,1)} %collective-permute-done.1), channel_id=1, source_target_pairs={{0,8},{8,0},{16,24},{24,16},{1,9},{9,1},{17,25},{25,17},{2,10},{10... | collective-permute-start | bytes 3145736 | tf_op jit(solution)/shard_map/ppermute | solution.py:34
  99.9 6.8 %collective-permute-start.8 = (bf16[1024,512]{1,0:T(8,128)(2,1)}, bf16[1024,512]{1,0:T(8,128)(2,1)S(1)}, u32[]{:S(2)}, u32[]{:S(2)}) collective-permute-start(bf16[1024,512]{1,0:T(8,128)(2,1)} %collective-permute-done.7), channel_id=1, source_target_pairs={{0,8},{8,0},{16,24},{24,16},{1,9},{9,1},{17,25},{25,17},{2,10},{10... | collective-permute-start | bytes 3145736 | tf_op jit(solution)/shard_map/ppermute | solution.py:34
  121.1 41.7 %all-to-all-start.1 = ((bf16[8,48,2048]{2,1,0:T(8,128)(2,1)}), bf16[8,48,2048]{2,1,0:T(8,128)(2,1)}, u32[]{:S(2)}, u32[]{:S(2)}) async-start(bf16[8,48,2048]{2,1,0:T(8,128)(2,1)} %bitcast.119), calls=%async_computation.1 | async-start | bytes 3145728 | tf_op jit(solution)/shard_map/all_to_all | solution.py:129
  127.4 39.9 %collective-permute-start.15 = (bf16[1024,512]{1,0:T(8,128)(2,1)}, bf16[1024,512]{1,0:T(8,128)(2,1)}, u32[]{:S(2)}, u32[]{:S(2)}) collective-permute-start(bf16[1024,512]{1,0:T(8,128)(2,1)} %convolution_convert_fusion.3), channel_id=1, source_target_pairs={{0,8},{8,0},{16,24},{24,16},{1,9},{9,1},{17,25},{25,17},{2,10},{10... | collective-permute-start | bytes 3145736 | tf_op jit(solution)/shard_map/ppermute | solution.py:34
  127.5 52.6 %collective-permute-start.17 = (bf16[1024,512]{1,0:T(8,128)(2,1)}, bf16[1024,512]{1,0:T(8,128)(2,1)}, u32[]{:S(2)}, u32[]{:S(2)}) collective-permute-start(bf16[1024,512]{1,0:T(8,128)(2,1)} %convolution_convert_fusion.1), channel_id=1, source_target_pairs={{0,8},{8,0},{16,24},{24,16},{1,9},{9,1},{17,25},{25,17},{2,10},{10... | collective-permute-start | bytes 3145736 | tf_op jit(solution)/shard_map/ppermute | solution.py:34
  128.0 46.7 %collective-permute-start.12 = (bf16[512,1024]{1,0:T(8,128)(2,1)}, bf16[512,1024]{1,0:T(8,128)(2,1)}, u32[]{:S(2)}, u32[]{:S(2)}) collective-permute-start(bf16[512,1024]{1,0:T(8,128)(2,1)} %convolution_convert_fusion.7), channel_id=1, source_target_pairs={{0,8},{8,0},{16,24},{24,16},{1,9},{9,1},{17,25},{25,17},{2,10},{10... | collective-permute-start | bytes 3145736 | tf_op jit(solution)/shard_map/ppermute | solution.py:34
  128.1 78.6 %collective-permute-start.14 = (bf16[512,1024]{1,0:T(8,128)(2,1)}, bf16[512,1024]{1,0:T(8,128)(2,1)}, u32[]{:S(2)}, u32[]{:S(2)}) collective-permute-start(bf16[512,1024]{1,0:T(8,128)(2,1)} %convolution_convert_fusion.5), channel_id=1, source_target_pairs={{0,8},{8,0},{16,24},{24,16},{1,9},{9,1},{17,25},{25,17},{2,10},{10... | collective-permute-start | bytes 3145736 | tf_op jit(solution)/shard_map/ppermute | solution.py:34
  130.3 47.4 %collective-permute-start.9 = (bf16[512,1024]{1,0:T(8,128)(2,1)}, bf16[512,1024]{1,0:T(8,128)(2,1)}, u32[]{:S(2)}, u32[]{:S(2)}) collective-permute-start(bf16[512,1024]{1,0:T(8,128)(2,1)} %convolution_convert_fusion.11), channel_id=1, source_target_pairs={{0,8},{8,0},{16,24},{24,16},{1,9},{9,1},{17,25},{25,17},{2,10},{10... | collective-permute-start | bytes 3145736 | tf_op jit(solution)/shard_map/ppermute | solution.py:34
  162.8 40.9 %all-to-all-start.2 = ((bf16[8,48,2048]{2,1,0:T(8,128)(2,1)}), bf16[8,48,2048]{2,1,0:T(8,128)(2,1)}, u32[]{:S(2)}, u32[]{:S(2)}) async-start(bf16[8,48,2048]{2,1,0:T(8,128)(2,1)} %bitcast.15), calls=%async_computation.2 | async-start | bytes 3145728 | tf_op jit(solution)/shard_map/all_to_all | solution.py:129
  169.7 26.2 %collective-permute-start.16 = (bf16[1024,512]{1,0:T(8,128)(2,1)S(1)}, bf16[1024,512]{1,0:T(8,128)(2,1)S(1)}, u32[]{:S(2)}, u32[]{:S(2)}) collective-permute-start(bf16[1024,512]{1,0:T(8,128)(2,1)S(1)} %add_convert_fusion.1), channel_id=1, source_target_pairs={{0,16},{8,24},{16,0},{24,8},{1,17},{9,25},{17,1},{25,9},{2,18},{10... | collective-permute-start | bytes 3145736 | tf_op jit(solution)/shard_map/ppermute | solution.py:39
  174.7 67.4 %collective-permute-start.11 = (bf16[512,1024]{1,0:T(8,128)(2,1)}, bf16[512,1024]{1,0:T(8,128)(2,1)}, u32[]{:S(2)}, u32[]{:S(2)}) collective-permute-start(bf16[512,1024]{1,0:T(8,128)(2,1)} %convolution_convert_fusion.9), channel_id=1, source_target_pairs={{0,8},{8,0},{16,24},{24,16},{1,9},{9,1},{17,25},{25,17},{2,10},{10... | collective-permute-start | bytes 3145736 | tf_op jit(solution)/shard_map/ppermute | solution.py:34
  177.7 40.8 %collective-permute-start.13 = (bf16[512,1024]{1,0:T(8,128)(2,1)}, bf16[512,1024]{1,0:T(8,128)(2,1)}, u32[]{:S(2)}, u32[]{:S(2)}) collective-permute-start(bf16[512,1024]{1,0:T(8,128)(2,1)} %add_convert_fusion.3), channel_id=1, source_target_pairs={{0,16},{8,24},{16,0},{24,8},{1,17},{9,25},{17,1},{25,9},{2,18},{10... | collective-permute-start | bytes 3145736 | tf_op jit(solution)/shard_map/ppermute | solution.py:39
  180.2 62.0 %collective-permute-start.10 = (bf16[512,1024]{1,0:T(8,128)(2,1)S(1)}, bf16[512,1024]{1,0:T(8,128)(2,1)S(1)}, u32[]{:S(2)}, u32[]{:S(2)}) collective-permute-start(bf16[512,1024]{1,0:T(8,128)(2,1)S(1)} %add_convert_fusion.5), channel_id=1, source_target_pairs={{0,16},{8,24},{16,0},{24,8},{1,17},{9,25},{17,1},{25,9},{2,18},{10... | collective-permute-start | bytes 3145736 | tf_op jit(solution)/shard_map/ppermute | solution.py:39
  206.6 15.0 %collective-permute-start.23 = (f32[16,128]{1,0:T(8,128)S(1)}, f32[16,128]{1,0:T(8,128)S(1)}, u32[]{:S(2)}, u32[]{:S(2)}) collective-permute-start(f32[16,128]{1,0:T(8,128)S(1)} %bitcast.132), channel_id=1, source_target_pairs={{0,8},{8,0},{16,24},{24,16},{1,9},{9,1},{17,25},{25,17},{2,10},{10... | collective-permute-start | bytes 24584 | tf_op jit(solution)/shard_map/ppermute | solution.py:47
  221.6 20.6 %copy-start.11 = (bf16[512,1024]{1,0:T(8,128)(2,1)S(1)}, bf16[512,1024]{1,0:T(8,128)(2,1)}, u32[]{:S(2)}) copy-start(bf16[512,1024]{1,0:T(8,128)(2,1)} %convolution_convert_fusion.10) | copy-start | bytes 3145732
  221.6 17.5 %collective-permute-start.24 = (f32[16,128]{1,0:T(8,128)S(1)}, f32[16,128]{1,0:T(8,128)S(1)}, u32[]{:S(2)}, u32[]{:S(2)}) collective-permute-start(f32[16,128]{1,0:T(8,128)S(1)} %bitcast_add_fusion), channel_id=1, source_target_pairs={{0,16},{8,24},{16,0},{24,8},{1,17},{9,25},{17,1},{25,9},{2,18},{10... | collective-permute-start | bytes 24584 | tf_op jit(solution)/shard_map/ppermute | solution.py:47
  223.6 16.9 %collective-permute-start.18 = (f32[8,2048]{1,0:T(8,128)S(1)}, f32[8,2048]{1,0:T(8,128)S(1)}, u32[]{:S(2)}, u32[]{:S(2)}) collective-permute-start(f32[8,2048]{1,0:T(8,128)S(1)} %fusion.116), channel_id=1, source_target_pairs={{0,8},{8,0},{16,24},{24,16},{1,9},{9,1},{17,25},{25,17},{2,10},{10... | collective-permute-start | bytes 196616 | tf_op jit(solution)/shard_map/ppermute | solution.py:47
  239.1 5.9 %collective-permute-start.25 = (f32[16,128]{1,0:T(8,128)S(1)}, f32[16,128]{1,0:T(8,128)S(1)}, u32[]{:S(2)}, u32[]{:S(2)}) collective-permute-start(f32[16,128]{1,0:T(8,128)S(1)} %fusion.174), channel_id=1, source_target_pairs={{0,1},{1,0},{2,3},{3,2},{4,5},{5,4},{6,7},{7,6},{8,9},{9,8},{10,11... | collective-permute-start | bytes 24584 | tf_op jit(solution)/shard_map/ppermute | solution.py:47
  240.6 5.9 %collective-permute-start.19 = (f32[8,2048]{1,0:T(8,128)S(1)}, f32[8,2048]{1,0:T(8,128)S(1)}, u32[]{:S(2)}, u32[]{:S(2)}) collective-permute-start(f32[8,2048]{1,0:T(8,128)S(1)} %add.214), channel_id=1, source_target_pairs={{0,16},{8,24},{16,0},{24,8},{1,17},{9,25},{17,1},{25,9},{2,18},{10... | collective-permute-start | bytes 196616 | tf_op jit(solution)/shard_map/ppermute | solution.py:47
  245.0 3.7 %collective-permute-start.26 = (f32[16,128]{1,0:T(8,128)S(1)}, f32[16,128]{1,0:T(8,128)S(1)}, u32[]{:S(2)}, u32[]{:S(2)}) collective-permute-start(f32[16,128]{1,0:T(8,128)S(1)} %add.221), channel_id=1, source_target_pairs={{0,2},{1,3},{2,0},{3,1},{4,6},{5,7},{6,4},{7,5},{8,10},{9,11},{10,... | collective-permute-start | bytes 24584 | tf_op jit(solution)/shard_map/ppermute | solution.py:47
  246.4 4.5 %collective-permute-start.20 = (f32[8,2048]{1,0:T(8,128)S(1)}, f32[8,2048]{1,0:T(8,128)S(1)}, u32[]{:S(2)}, u32[]{:S(2)}) collective-permute-start(f32[8,2048]{1,0:T(8,128)S(1)} %add.215), channel_id=1, source_target_pairs={{0,1},{1,0},{2,3},{3,2},{4,5},{5,4},{6,7},{7,6},{8,9},{9,8},{10,11... | collective-permute-start | bytes 196616 | tf_op jit(solution)/shard_map/ppermute | solution.py:47
  248.7 8.9 %collective-permute-start.27 = (f32[16,128]{1,0:T(8,128)S(1)}, f32[16,128]{1,0:T(8,128)S(1)}, u32[]{:S(2)}, u32[]{:S(2)}) collective-permute-start(f32[16,128]{1,0:T(8,128)S(1)} %add.222), channel_id=1, source_target_pairs={{0,4},{1,5},{2,6},{3,7},{4,0},{5,1},{6,2},{7,3},{8,12},{9,13},{10,... | collective-permute-start | bytes 24584 | tf_op jit(solution)/shard_map/ppermute | solution.py:47
  251.0 4.5 %collective-permute-start.21 = (f32[8,2048]{1,0:T(8,128)S(1)}, f32[8,2048]{1,0:T(8,128)S(1)}, u32[]{:S(2)}, u32[]{:S(2)}) collective-permute-start(f32[8,2048]{1,0:T(8,128)S(1)} %add.216), channel_id=1, source_target_pairs={{0,2},{1,3},{2,0},{3,1},{4,6},{5,7},{6,4},{7,5},{8,10},{9,11},{10,... | collective-permute-start | bytes 196616 | tf_op jit(solution)/shard_map/ppermute | solution.py:47
  255.5 5.2 %collective-permute-start.22 = (f32[8,2048]{1,0:T(8,128)S(1)}, f32[8,2048]{1,0:T(8,128)S(1)}, u32[]{:S(2)}, u32[]{:S(2)}) collective-permute-start(f32[8,2048]{1,0:T(8,128)S(1)} %add.217), channel_id=1, source_target_pairs={{0,4},{1,5},{2,6},{3,7},{4,0},{5,1},{6,2},{7,3},{8,12},{9,13},{10,... | collective-permute-start | bytes 196616 | tf_op jit(solution)/shard_map/ppermute | solution.py:47
  (19 other events, 106.4 us)

commit v2 on v1

--- a/solution.py
+++ b/solution.py
@@ -36,16 +36,24 @@
 
 def to_chip(value, step):
     count = lax.axis_size("dp")
-    return lax.ppermute(value, "dp", [(i, (i + 2 * step) % count) for i in range(count)])
+    return lax.ppermute(value, "dp", [(i, i ^ (2 * step)) for i in range(count)])
 
 
 def sum_over_all(value):
     for axis in ("dp", "expert"):
         count = lax.axis_size(axis)
+
+        def at(mask):
+            return lax.ppermute(value, axis, [(i, i ^ mask) for i in range(count)])
+
         hop = 1
         while hop < count:
-            value = value + lax.ppermute(value, axis, [(i, i ^ hop) for i in range(count)])
-            hop *= 2
+            if 4 * hop <= count:
+                value = (value + at(hop)) + (at(2 * hop) + at(3 * hop))
+                hop *= 4
+            else:
+                value = value + at(hop)
+                hop *= 2
     return value
 
 
@@ -64,14 +72,19 @@
 
     shard = (gate_weight_matrix[0], up_weight[0], down_weight[0])
     pieces = []
-    owners = []
     for k in range(chips):
         arrived = shard if k == 0 else tuple(to_chip(w, k) for w in shard)
         pieces.append(arrived)
         pieces.append(tuple(to_sibling(w) for w in arrived))
-        owner = lax.rem(me - 2 * k + dp_count, dp_count)
-        owners.append(owner)
-        owners.append(owner + 1 - 2 * lax.rem(owner, 2))
+
+    def reordered(value):
+        return jnp.concatenate(
+            [lax.dynamic_slice_in_dim(value, (me ^ p) * part, part, 1) for p in range(dp_count)],
+            axis=1,
+        )
+
+    def split(value):
+        return [value[:, p * part : (p + 1) * part] for p in range(dp_count)]
 
     source = tokens.astype(jnp.float32)
     inverse = lax.rsqrt(jnp.mean(source * source, axis=-1, keepdims=True) + norm_eps)
@@ -93,39 +106,7 @@
         axis=1,
         keepdims=True,
     )
-    send_rows = product(fill, normed).astype(jnp.bfloat16)
-    d_send = (slot_gate * product(fill, upstream)).astype(jnp.bfloat16)
-    arrived = lax.all_to_all(
-        jnp.concatenate(
-            [
-                send_rows.reshape(experts, capacity, width),
-                d_send.reshape(experts, capacity, width),
-            ],
-            axis=1,
-        ),
-        "expert",
-        split_axis=0,
-        concat_axis=0,
-        tiled=True,
-    )
-    expert_in = arrived[:, :capacity].reshape(slots, width)
-    d_out = arrived[:, capacity:].reshape(slots, width)
-    in_parts = [lax.dynamic_slice_in_dim(expert_in, o * part, part, 1) for o in owners]
-    out_parts = [lax.dynamic_slice_in_dim(d_out, o * part, part, 1) for o in owners]
-
-    pre_gate = sum(product(x, w[0]) for x, w in zip(in_parts, pieces))
-    pre_up = sum(product(x, w[1]) for x, w in zip(in_parts, pieces))
-    sigma = jax.nn.sigmoid(pre_gate)
-    active = pre_gate * sigma
-    hidden = (active * pre_up).astype(jnp.bfloat16)
-
-    def in_order(parts):
-        whole = jnp.zeros((slots, width), jnp.bfloat16)
-        for o, value in zip(owners, parts):
-            whole = lax.dynamic_update_slice_in_dim(whole, value, o * part, 1)
-        return whole
-
-    def send_back(rows):
+    def exchange(rows):
         return lax.all_to_all(
             rows.reshape(experts, capacity, width),
             "expert",
@@ -134,8 +115,22 @@
             tiled=True,
         ).reshape(slots, width)
 
-    expert_out = in_order([product(hidden, w[2]).astype(jnp.bfloat16) for w in pieces])
-    returned = send_back(expert_out)
+    expert_in = exchange(product(fill, reordered(normed)).astype(jnp.bfloat16))
+    d_out = exchange((slot_gate * product(fill, reordered(upstream))).astype(jnp.bfloat16))
+    in_parts = split(expert_in)
+
+    pre_gate = sum(product(x, w[0]) for x, w in zip(in_parts, pieces))
+    pre_up = sum(product(x, w[1]) for x, w in zip(in_parts, pieces))
+    sigma = jax.nn.sigmoid(pre_gate)
+    active = pre_gate * sigma
+    hidden = (active * pre_up).astype(jnp.bfloat16)
+
+    expert_out = jnp.concatenate(
+        [product(hidden, w[2]).astype(jnp.bfloat16) for w in pieces], axis=1
+    )
+    expert_out, d_out, hidden = lax.optimization_barrier((expert_out, d_out, hidden))
+    returned = exchange(expert_out)
+    out_parts = split(d_out)
 
     d_hidden = sum(transposed_product(x, w[2]) for x, w in zip(out_parts, pieces))
     d_pre_gate = (d_hidden * pre_up * sigma * (1.0 + pre_gate * (1.0 - sigma))).astype(jnp.bfloat16)
@@ -149,31 +144,33 @@
             inner_product(hidden, d).astype(jnp.bfloat16),
         )
 
-    totals = None
-    for k in list(range(1, chips)) + [0]:
+    def pair_sum(k):
         theirs = [to_sibling(v) for v in shares(2 * k + 1)]
-        mine = shares(2 * k)
-        both = [a.astype(jnp.float32) + b.astype(jnp.float32) for a, b in zip(mine, theirs)]
-        if k:
-            both = [
-                to_chip(v.astype(jnp.bfloat16), chips - k).astype(jnp.float32) for v in both
-            ]
-        totals = both if totals is None else [a + b for a, b in zip(totals, both)]
-    weight_gradients = [v.astype(jnp.bfloat16)[None] for v in totals]
-
-    d_rows = in_order(
+        return [
+            a.astype(jnp.float32) + b.astype(jnp.float32) for a, b in zip(shares(2 * k), theirs)
+        ]
+
+    away = [[v.astype(jnp.bfloat16) for v in pair_sum(k)] for k in range(1, chips)]
+    totals = pair_sum(0)
+    away, d_pre_gate, d_pre_up = lax.optimization_barrier((away, d_pre_gate, d_pre_up))
+    d_rows = jnp.concatenate(
         [
             (transposed_product(d_pre_gate, w[0]) + transposed_product(d_pre_up, w[1])).astype(
                 jnp.bfloat16
             )
             for w in pieces
-        ]
-    )
-    d_back = send_back(d_rows)
+        ],
+        axis=1,
+    )
+    d_back = exchange(d_rows)
+    for k in range(1, chips):
+        landed = [to_chip(v, k).astype(jnp.float32) for v in away[k - 1]]
+        totals = [a + b for a, b in zip(totals, landed)]
+    weight_gradients = [v.astype(jnp.bfloat16)[None] for v in totals]
 
     cotangent = upstream.astype(jnp.float32)
-    first_out = inner_product(first.astype(jnp.bfloat16), returned)
-    second_out = inner_product(second.astype(jnp.bfloat16), returned)
+    first_out = reordered(inner_product(first.astype(jnp.bfloat16), returned))
+    second_out = reordered(inner_product(second.astype(jnp.bfloat16), returned))
     mixed = (source + gates[:, :1] * first_out + gates[:, 1:] * second_out).astype(jnp.bfloat16)
     d_gates = jnp.concatenate(
         [
@@ -192,17 +189,18 @@
         (((0,), (0,)), ((), ())),
         precision=lax.Precision.HIGHEST,
     )
-    d_router = sum_over_all(part_router).T
     through_router = jnp.dot(
         d_logits, router.astype(jnp.float32).T, precision=lax.Precision.HIGHEST
     )
 
-    d_normed = inner_product(fill, d_back) + through_router
+    d_normed = reordered(inner_product(fill, d_back)) + through_router
     d_unit = d_normed * gain
     inner = jnp.mean(d_unit * unit_rows, axis=-1, keepdims=True)
     d_tokens = (cotangent + inverse * (d_unit - unit_rows * inner)).astype(jnp.bfloat16)
     part_gain = jnp.sum(d_normed * unit_rows, axis=0)
-    d_gain = sum_over_all(part_gain.reshape(-1, 128)).reshape(-1)
+    summed = sum_over_all(jnp.concatenate([part_router, part_gain[None]], axis=0))
+    d_router = summed[:experts].T
+    d_gain = summed[experts]
     return (mixed, d_tokens, *weight_gradients, d_router, d_gain)
 
 

time: 263 us -> 266 us (1.011)
  matrix products: 70.1 us -> 72.8 us
    ppermute x16 -> x13, waiting for transfers between devices: 47.2 us -> 111 us  [the longest x6 99 us: to_chip(): return lax.ppermute(value, 'dp', [(i, i ^ 2 * step) for i in range(count)])]
    all_to_all x3 -> x4, waiting for transfers between devices: 81.1 us -> 18.4 us  [exchange(): lax.all_to_all(rows.reshape(experts, capacity, width), 'expert', split_ax...]
    all_to_all x3 -> x4, starting transfers between devices: 16.4 us -> 22.4 us  [exchange(): lax.all_to_all(rows.reshape(experts, capacity, width), 'expert', split_ax...]
    ppermute x16 -> x13, starting transfers between devices: 20.1 us -> 15.3 us  [the longest x7 8.11 us: at(): return lax.ppermute(value, axis, [(i, i ^ mask) for i in range(count)])]
    dot_general x15, matrix products: 18.2 us -> 22.6 us  [product(): return jnp.dot(left, right, preferred_element_type=jnp.float32)]
  transfers between devices with their start and end apart: 31 -> 29, of which waited for: 9 -> 13; matrix products, arithmetic and copies ran while one was open for 26% -> 30% of each run, Pallas kernels for 0% -> 0%
where the time goes in v2:
time: 266 us; the launch traced here: 265 us
  waiting for transfers between devices  129 us (48%)
  matrix products  72.8 us (27%)
  starting transfers between devices  39 us (15%)
  other arithmetic  16 us (6%)
  local copies, waits for them, and re-layouts  6.3 us (2%)
    ppermute x6, waiting for transfers between devices, to_chip(): return lax.ppermute(value, 'dp', [(i, i ^ 2 * step) for i in range(count)])  99 us
    dot_general x15, matrix products, inner_product(): lax.dot_general(left, right, (((0,), (0,)), ((), ())), preferred_element_...  29.5 us
    dot_general x15, matrix products, product(): return jnp.dot(left, right, preferred_element_type=jnp.float32)  22.6 us
    all_to_all x4, starting transfers between devices, exchange(): lax.all_to_all(rows.reshape(experts, capacity, width), 'expert', split_ax...  22.4 us
    dot_general x12, matrix products, transposed_product(): lax.dot_general(left, right, (((1,), (1,)), ((), ())), preferred_element_...  19.4 us
    all_to_all x4, waiting for transfers between devices, exchange(): lax.all_to_all(rows.reshape(experts, capacity, width), 'expert', split_ax...  18.4 us
    ppermute x7, waiting for transfers between devices, at(): return lax.ppermute(value, axis, [(i, i ^ mask) for i in range(count)])  12 us
    ppermute x7, starting transfers between devices, at(): return lax.ppermute(value, axis, [(i, i ^ mask) for i in range(count)])  8.11 us
  transfers between devices with their start and end apart: 29, of which 13 were waited for; matrix products, arithmetic and copies ran while one was open for 30% of the time, Pallas kernels for 0%

profile of v2, /device:TPU:0, one launch (start us, length us, event | category | flops | bytes accessed | tf_op | source)
XLA Modules:
  0.0 264.8 jit_solution(11649927158854340112)
XLA Ops:
  7.9 7.4 %all-to-all-start = ((bf16[8,48,2048]{2,1,0:T(8,128)(2,1)}), bf16[8,48,2048]{2,1,0:T(8,128)(2,1)S(1)}, u32[]{:S(2)}, u32[]{:S(2)}) async-start(bf16[8,48,2048]{2,1,0:T(8,128)(2,1)} %bitcast.131), calls=%async_computation | async-start | bytes 3145728 | tf_op jit(solution)/shard_map/all_to_all | solution.py:110
  21.2 20.5 %collective-permute-done.1 = bf16[512,1024]{1,0:T(8,128)(2,1)} collective-permute-done((bf16[512,1024]{1,0:T(8,128)(2,1)}, bf16[512,1024]{1,0:T(8,128)(2,1)}, u32[]{:S(2)}, u32[]{:S(2)}) %collective-permute-start.1) | collective-permute-done | bytes 1048608 | tf_op jit(solution)/shard_map/ppermute | solution.py:39
  41.6 22.5 %collective-permute-done.4 = bf16[512,1024]{1,0:T(8,128)(2,1)} collective-permute-done((bf16[512,1024]{1,0:T(8,128)(2,1)}, bf16[512,1024]{1,0:T(8,128)(2,1)}, u32[]{:S(2)}, u32[]{:S(2)}) %collective-permute-start.4) | collective-permute-done | bytes 1048608 | tf_op jit(solution)/shard_map/ppermute | solution.py:39
  64.1 5.9 %all-to-all-start.1 = ((bf16[8,48,2048]{2,1,0:T(8,128)(2,1)}), bf16[8,48,2048]{2,1,0:T(8,128)(2,1)S(1)}, u32[]{:S(2)}, u32[]{:S(2)}) async-start(bf16[8,48,2048]{2,1,0:T(8,128)(2,1)} %bitcast.130), calls=%async_computation.1 | async-start | bytes 3145728 | tf_op jit(solution)/shard_map/all_to_all | solution.py:110
  70.0 1.9 fusion.71
  76.5 9.6 %collective-permute-done.7 = bf16[1024,512]{1,0:T(8,128)(2,1)} collective-permute-done((bf16[1024,512]{1,0:T(8,128)(2,1)}, bf16[1024,512]{1,0:T(8,128)(2,1)}, u32[]{:S(2)}, u32[]{:S(2)}) %collective-permute-start.7) | collective-permute-done | bytes 1048608 | tf_op jit(solution)/shard_map/ppermute | solution.py:39
  91.6 3.8 %multiply_convert_fusion.3 = (bf16[384,1024]{1,0:T(8,128)(2,1)S(1)}, f32[384,1024]{1,0:T(8,128)}) fusion(f32[384,1024]{1,0:T(8,128)S(1)} %add_add_fusion.2, bf16[512,1024]{1,0:T(8,128)(2,1)} %collective-permute-done.5, bf16[384,2048]{1,0:T(8,128)(2,1)S(1)} %bitcast.107, f32[384,1024]{1,0:T(8,128)S(1)} %fusion.57, f32[384,1024]{1,0:T(8,128)S(1)} %fusion.69, ...), kind=kOutput, calls=%fused_computation.17 | convolution fusion | flops 406192128 | bytes 10092544 | tf_op jit(solution)/shard_map/dot_general | solution.py:10
  100.7 7.0 %all-to-all-done.1 = bf16[8,48,2048]{2,1,0:T(8,128)(2,1)S(1)} async-done(((bf16[8,48,2048]{2,1,0:T(8,128)(2,1)}), bf16[8,48,2048]{2,1,0:T(8,128)(2,1)S(1)}, u32[]{:S(2)}, u32[]{:S(2)}) %all-to-all-start.1) | async-done | bytes 1572896 | tf_op jit(solution)/shard_map/all_to_all | solution.py:110
  107.7 2.4 fusion.49
  111.9 2.0 fusion.43
  115.6 2.2 multiply_convert_fusion.1
  121.7 4.5 %all-to-all-start.2 = ((bf16[8,48,2048]{2,1,0:T(8,128)(2,1)}), bf16[8,48,2048]{2,1,0:T(8,128)(2,1)}, u32[]{:S(2)}, u32[]{:S(2)}) async-start(bf16[8,48,2048]{2,1,0:T(8,128)(2,1)} %bitcast.116), calls=%async_computation.2 | async-start | bytes 3145728 | tf_op jit(solution)/shard_map/all_to_all | solution.py:110
  126.2 3.0 %convolution_convert_fusion.1 = bf16[1024,512]{1,0:T(8,128)(2,1)} fusion(bf16[384,1024]{1,0:T(8,128)(2,1)} %copy-done.24, bf16[384,2048]{1,0:T(8,128)(2,1)} %bitcast.123), kind=kOutput, calls=%fused_computation.29 | convolution fusion | flops 403177472 | bytes 2228224 | tf_op jit(solution)/shard_map/dot_general | solution.py:20
  129.7 3.1 %add_convert_fusion.3 = bf16[1024,512]{1,0:T(8,128)(2,1)} fusion(bf16[1024,512]{1,0:T(8,128)(2,1)} %collective-permute-done.11, bf16[384,1024]{1,0:T(8,128)(2,1)S(1)} %copy-done.26, bf16[384,2048]{1,0:T(8,128)(2,1)} %bitcast.124), kind=kOutput, calls=%fused_computation.6 | convolution fusion | flops 405274624 | bytes 3276800 | tf_op jit(solution)/shard_map/dot_general | solution.py:20
  132.8 2.9 %add_convert_fusion.4 = bf16[512,1024]{1,0:T(8,128)(2,1)} fusion(bf16[512,1024]{1,0:T(8,128)(2,1)} %collective-permute-done.10, bf16[384,1024]{1,0:T(8,128)(2,1)S(1)} %get-tuple-element.19, bf16[384,2048]{1,0:T(8,128)(2,1)S(1)} %bitcast.110), kind=kOutput, calls=%fused_computation.7 | convolution fusion | flops 405274624 | bytes 3276800 | tf_op jit(solution)/shard_map/dot_general | solution.py:20
  135.7 3.0 %add_convert_fusion.5 = bf16[512,1024]{1,0:T(8,128)(2,1)} fusion(bf16[512,1024]{1,0:T(8,128)(2,1)} %collective-permute-done.9, bf16[384,1024]{1,0:T(8,128)(2,1)S(1)} %get-tuple-element.18, bf16[384,2048]{1,0:T(8,128)(2,1)S(1)} %bitcast.111), kind=kOutput, calls=%fused_computation.8 | convolution fusion | flops 405274624 | bytes 3276800 | tf_op jit(solution)/shard_map/dot_general | solution.py:20
  143.0 1.9 fusion.102
  152.5 11.4 %all-to-all-done.2 = bf16[8,48,2048]{2,1,0:T(8,128)(2,1)} async-done(((bf16[8,48,2048]{2,1,0:T(8,128)(2,1)}), bf16[8,48,2048]{2,1,0:T(8,128)(2,1)}, u32[]{:S(2)}, u32[]{:S(2)}) %all-to-all-start.2) | async-done | bytes 1572896 | tf_op jit(solution)/shard_map/all_to_all | solution.py:110
  163.9 4.6 %all-to-all-start.3 = ((bf16[8,48,2048]{2,1,0:T(8,128)(2,1)}), bf16[8,48,2048]{2,1,0:T(8,128)(2,1)}, u32[]{:S(2)}, u32[]{:S(2)}) async-start(bf16[8,48,2048]{2,1,0:T(8,128)(2,1)} %bitcast.117), calls=%async_computation.3 | async-start | bytes 3145728 | tf_op jit(solution)/shard_map/all_to_all | solution.py:110
  179.2 16.5 %collective-permute-done.17 = bf16[1024,512]{1,0:T(8,128)(2,1)S(1)} collective-permute-done((bf16[1024,512]{1,0:T(8,128)(2,1)S(1)}, bf16[1024,512]{1,0:T(8,128)(2,1)S(1)}, u32[]{:S(2)}, u32[]{:S(2)}) %collective-permute-start.17) | collective-permute-done | bytes 1048608 | tf_op jit(solution)/shard_map/ppermute | solution.py:39
  195.7 2.6 fusion.25
  198.3 19.9 %collective-permute-done.15 = bf16[512,1024]{1,0:T(8,128)(2,1)S(1)} collective-permute-done((bf16[512,1024]{1,0:T(8,128)(2,1)S(1)}, bf16[512,1024]{1,0:T(8,128)(2,1)S(1)}, u32[]{:S(2)}, u32[]{:S(2)}) %collective-permute-start.15) | collective-permute-done | bytes 1048608 | tf_op jit(solution)/shard_map/ppermute | solution.py:39
  219.8 1.9 fusion.75
  221.8 1.9 fusion.73
  223.7 1.9 fusion.76
  230.7 10.1 %collective-permute-done.13 = bf16[512,1024]{1,0:T(8,128)(2,1)} collective-permute-done((bf16[512,1024]{1,0:T(8,128)(2,1)S(1)}, bf16[512,1024]{1,0:T(8,128)(2,1)}, u32[]{:S(2)}, u32[]{:S(2)}) %collective-permute-start.13) | collective-permute-done | bytes 1048608 | tf_op jit(solution)/shard_map/ppermute | solution.py:39
  240.7 3.1 %fusion.23 = bf16[1,512,1024]{2,1,0:T(8,128)(2,1)} fusion(bf16[512,1024]{1,0:T(8,128)(2,1)} %collective-permute-done.13, bf16[512,1024]{1,0:T(8,128)(2,1)} %collective-permute-done.12, bf16[512,1024]{1,0:T(8,128)(2,1)S(1)} %copy-done.17), kind=kLoop, calls=%fused_computation.68 | loop fusion | flops 3145728 | bytes 4194304 | tf_op jit(solution)/shard_map/broadcast_in_dim | solution.py:169
  248.2 2.5 collective-permute-done.21
  250.8 1.9 collective-permute-done.22
  252.6 2.1 collective-permute-done.23
  254.8 2.6 collective-permute-start.24
  258.8 4.8 %collective-permute-done.24 = f32[9,2048]{1,0:T(8,128)S(1)} collective-permute-done((f32[9,2048]{1,0:T(8,128)S(1)}, f32[9,2048]{1,0:T(8,128)S(1)}, u32[]{:S(2)}, u32[]{:S(2)}) %collective-permute-start.24) | collective-permute-done | bytes 73760 | tf_op jit(solution)/shard_map/ppermute | solution.py:47
  (168 shorter events, 72.2 us)
Async XLA Ops:
  0.6 18.3 %copy-start = (bf16[2048,8]{0,1:T(8,128)(2,1)S(1)}, bf16[2048,8]{0,1:T(8,128)(2,1)}, u32[]{:S(2)}) copy-start(bf16[2048,8]{0,1:T(8,128)(2,1)} %param.12) | copy-start | bytes 98308
  6.1 12.8 %copy-start.1 = (bf16[128,2048]{1,0:T(8,128)(2,1)}, bf16[128,2048]{1,0:T(8,128)(2,1)S(1)}, u32[]{:S(2)}) copy-start(bf16[128,2048]{1,0:T(8,128)(2,1)S(1)} %fusion.12) | copy-start | bytes 1572868
  7.9 56.2 %all-to-all-start = ((bf16[8,48,2048]{2,1,0:T(8,128)(2,1)}), bf16[8,48,2048]{2,1,0:T(8,128)(2,1)S(1)}, u32[]{:S(2)}, u32[]{:S(2)}) async-start(bf16[8,48,2048]{2,1,0:T(8,128)(2,1)} %bitcast.131), calls=%async_computation | async-start | bytes 3145728 | tf_op jit(solution)/shard_map/all_to_all | solution.py:110
  15.3 60.9 %collective-permute-start = (bf16[512,1024]{1,0:T(8,128)(2,1)}, bf16[512,1024]{1,0:T(8,128)(2,1)}, u32[]{:S(2)}, u32[]{:S(2)}) collective-permute-start(bf16[512,1024]{1,0:T(8,128)(2,1)} %bitcast.128), channel_id=1, source_target_pairs={{0,8},{8,0},{16,24},{24,16},{1,9},{9,1},{17,25},{25,17},{2,10},{10... | collective-permute-start | bytes 3145736 | tf_op jit(solution)/shard_map/ppermute | solution.py:34
  15.3 26.3 %collective-permute-start.1 = (bf16[512,1024]{1,0:T(8,128)(2,1)}, bf16[512,1024]{1,0:T(8,128)(2,1)}, u32[]{:S(2)}, u32[]{:S(2)}) collective-permute-start(bf16[512,1024]{1,0:T(8,128)(2,1)} %bitcast.129), channel_id=1, source_target_pairs={{0,16},{8,24},{16,0},{24,8},{1,17},{9,25},{17,1},{25,9},{2,18},{10... | collective-permute-start | bytes 3145736 | tf_op jit(solution)/shard_map/ppermute | solution.py:39
  16.9 47.2 %collective-permute-start.4 = (bf16[512,1024]{1,0:T(8,128)(2,1)}, bf16[512,1024]{1,0:T(8,128)(2,1)}, u32[]{:S(2)}, u32[]{:S(2)}) collective-permute-start(bf16[512,1024]{1,0:T(8,128)(2,1)} %bitcast.126), channel_id=1, source_target_pairs={{0,16},{8,24},{16,0},{24,8},{1,17},{9,25},{17,1},{25,9},{2,18},{10... | collective-permute-start | bytes 3145736 | tf_op jit(solution)/shard_map/ppermute | solution.py:39
  17.4 70.5 %collective-permute-start.3 = (bf16[512,1024]{1,0:T(8,128)(2,1)}, bf16[512,1024]{1,0:T(8,128)(2,1)}, u32[]{:S(2)}, u32[]{:S(2)}) collective-permute-start(bf16[512,1024]{1,0:T(8,128)(2,1)} %bitcast.127), channel_id=1, source_target_pairs={{0,8},{8,0},{16,24},{24,16},{1,9},{9,1},{17,25},{25,17},{2,10},{10... | collective-permute-start | bytes 3145736 | tf_op jit(solution)/shard_map/ppermute | solution.py:34
  17.4 68.7 %collective-permute-start.7 = (bf16[1024,512]{1,0:T(8,128)(2,1)}, bf16[1024,512]{1,0:T(8,128)(2,1)}, u32[]{:S(2)}, u32[]{:S(2)}) collective-permute-start(bf16[1024,512]{1,0:T(8,128)(2,1)} %bitcast.132), channel_id=1, source_target_pairs={{0,16},{8,24},{16,0},{24,8},{1,17},{9,25},{17,1},{25,9},{2,18},{10... | collective-permute-start | bytes 3145736 | tf_op jit(solution)/shard_map/ppermute | solution.py:39
  41.6 48.1 %collective-permute-start.2 = (bf16[512,1024]{1,0:T(8,128)(2,1)}, bf16[512,1024]{1,0:T(8,128)(2,1)}, u32[]{:S(2)}, u32[]{:S(2)}) collective-permute-start(bf16[512,1024]{1,0:T(8,128)(2,1)} %collective-permute-done.1), channel_id=1, source_target_pairs={{0,8},{8,0},{16,24},{24,16},{1,9},{9,1},{17,25},{25,17},{2,10},{10... | collective-permute-start | bytes 3145736 | tf_op jit(solution)/shard_map/ppermute | solution.py:34
  64.1 27.5 %collective-permute-start.5 = (bf16[512,1024]{1,0:T(8,128)(2,1)}, bf16[512,1024]{1,0:T(8,128)(2,1)}, u32[]{:S(2)}, u32[]{:S(2)}) collective-permute-start(bf16[512,1024]{1,0:T(8,128)(2,1)} %collective-permute-done.4), channel_id=1, source_target_pairs={{0,8},{8,0},{16,24},{24,16},{1,9},{9,1},{17,25},{25,17},{2,10},{10... | collective-permute-start | bytes 3145736 | tf_op jit(solution)/shard_map/ppermute | solution.py:34
  64.1 43.6 %all-to-all-start.1 = ((bf16[8,48,2048]{2,1,0:T(8,128)(2,1)}), bf16[8,48,2048]{2,1,0:T(8,128)(2,1)S(1)}, u32[]{:S(2)}, u32[]{:S(2)}) async-start(bf16[8,48,2048]{2,1,0:T(8,128)(2,1)} %bitcast.130), calls=%async_computation.1 | async-start | bytes 3145728 | tf_op jit(solution)/shard_map/all_to_all | solution.py:110
  76.2 22.2 %collective-permute-start.6 = (bf16[1024,512]{1,0:T(8,128)(2,1)S(1)}, bf16[1024,512]{1,0:T(8,128)(2,1)S(1)}, u32[]{:S(2)}, u32[]{:S(2)}) collective-permute-start(bf16[1024,512]{1,0:T(8,128)(2,1)S(1)} %bitcast.133), channel_id=1, source_target_pairs={{0,8},{8,0},{16,24},{24,16},{1,9},{9,1},{17,25},{25,17},{2,10},{10... | collective-permute-start | bytes 3145736 | tf_op jit(solution)/shard_map/ppermute | solution.py:34
  86.1 11.7 %collective-permute-start.8 = (bf16[1024,512]{1,0:T(8,128)(2,1)}, bf16[1024,512]{1,0:T(8,128)(2,1)S(1)}, u32[]{:S(2)}, u32[]{:S(2)}) collective-permute-start(bf16[1024,512]{1,0:T(8,128)(2,1)} %collective-permute-done.7), channel_id=1, source_target_pairs={{0,8},{8,0},{16,24},{24,16},{1,9},{9,1},{17,25},{25,17},{2,10},{10... | collective-permute-start | bytes 3145736 | tf_op jit(solution)/shard_map/ppermute | solution.py:34
  111.9 17.8 %collective-permute-start.11 = (bf16[1024,512]{1,0:T(8,128)(2,1)}, bf16[1024,512]{1,0:T(8,128)(2,1)}, u32[]{:S(2)}, u32[]{:S(2)}) collective-permute-start(bf16[1024,512]{1,0:T(8,128)(2,1)} %convolution_convert_fusion.7), channel_id=1, source_target_pairs={{0,8},{8,0},{16,24},{24,16},{1,9},{9,1},{17,25},{25,17},{2,10},{10... | collective-permute-start | bytes 3145736 | tf_op jit(solution)/shard_map/ppermute | solution.py:34
  119.5 13.3 %collective-permute-start.10 = (bf16[512,1024]{1,0:T(8,128)(2,1)}, bf16[512,1024]{1,0:T(8,128)(2,1)}, u32[]{:S(2)}, u32[]{:S(2)}) collective-permute-start(bf16[512,1024]{1,0:T(8,128)(2,1)} %convolution_convert_fusion.9), channel_id=1, source_target_pairs={{0,8},{8,0},{16,24},{24,16},{1,9},{9,1},{17,25},{25,17},{2,10},{10... | collective-permute-start | bytes 3145736 | tf_op jit(solution)/shard_map/ppermute | solution.py:34
  121.6 14.1 %collective-permute-start.9 = (bf16[512,1024]{1,0:T(8,128)(2,1)}, bf16[512,1024]{1,0:T(8,128)(2,1)}, u32[]{:S(2)}, u32[]{:S(2)}) collective-permute-start(bf16[512,1024]{1,0:T(8,128)(2,1)} %convolution_convert_fusion.11), channel_id=1, source_target_pairs={{0,8},{8,0},{16,24},{24,16},{1,9},{9,1},{17,25},{25,17},{2,10},{10... | collective-permute-start | bytes 3145736 | tf_op jit(solution)/shard_map/ppermute | solution.py:34
  121.7 42.2 %all-to-all-start.2 = ((bf16[8,48,2048]{2,1,0:T(8,128)(2,1)}), bf16[8,48,2048]{2,1,0:T(8,128)(2,1)}, u32[]{:S(2)}, u32[]{:S(2)}) async-start(bf16[8,48,2048]{2,1,0:T(8,128)(2,1)} %bitcast.116), calls=%async_computation.2 | async-start | bytes 3145728 | tf_op jit(solution)/shard_map/all_to_all | solution.py:110
  129.2 48.4 %collective-permute-start.16 = (bf16[1024,512]{1,0:T(8,128)(2,1)}, bf16[1024,512]{1,0:T(8,128)(2,1)}, u32[]{:S(2)}, u32[]{:S(2)}) collective-permute-start(bf16[1024,512]{1,0:T(8,128)(2,1)} %convolution_convert_fusion.1), channel_id=1, source_target_pairs={{0,8},{8,0},{16,24},{24,16},{1,9},{9,1},{17,25},{25,17},{2,10},{10... | collective-permute-start | bytes 3145736 | tf_op jit(solution)/shard_map/ppermute | solution.py:34
  163.9 59.8 %all-to-all-start.3 = ((bf16[8,48,2048]{2,1,0:T(8,128)(2,1)}), bf16[8,48,2048]{2,1,0:T(8,128)(2,1)}, u32[]{:S(2)}, u32[]{:S(2)}) async-start(bf16[8,48,2048]{2,1,0:T(8,128)(2,1)} %bitcast.117), calls=%async_computation.3 | async-start | bytes 3145728 | tf_op jit(solution)/shard_map/all_to_all | solution.py:110
  169.2 29.1 %collective-permute-start.14 = (bf16[512,1024]{1,0:T(8,128)(2,1)S(1)}, bf16[512,1024]{1,0:T(8,128)(2,1)S(1)}, u32[]{:S(2)}, u32[]{:S(2)}) collective-permute-start(bf16[512,1024]{1,0:T(8,128)(2,1)S(1)} %convolution_convert_fusion.3), channel_id=1, source_target_pairs={{0,8},{8,0},{16,24},{24,16},{1,9},{9,1},{17,25},{25,17},{2,10},{10... | collective-permute-start | bytes 3145736 | tf_op jit(solution)/shard_map/ppermute | solution.py:34
  169.7 26.0 %collective-permute-start.17 = (bf16[1024,512]{1,0:T(8,128)(2,1)S(1)}, bf16[1024,512]{1,0:T(8,128)(2,1)S(1)}, u32[]{:S(2)}, u32[]{:S(2)}) collective-permute-start(bf16[1024,512]{1,0:T(8,128)(2,1)S(1)} %copy-done.20), channel_id=1, source_target_pairs={{0,16},{8,24},{16,0},{24,8},{1,17},{9,25},{17,1},{25,9},{2,18},{10... | collective-permute-start | bytes 3145736 | tf_op jit(solution)/shard_map/ppermute | solution.py:39
  172.9 57.8 %collective-permute-start.12 = (bf16[512,1024]{1,0:T(8,128)(2,1)}, bf16[512,1024]{1,0:T(8,128)(2,1)}, u32[]{:S(2)}, u32[]{:S(2)}) collective-permute-start(bf16[512,1024]{1,0:T(8,128)(2,1)} %convolution_convert_fusion.5), channel_id=1, source_target_pairs={{0,8},{8,0},{16,24},{24,16},{1,9},{9,1},{17,25},{25,17},{2,10},{10... | collective-permute-start | bytes 3145736 | tf_op jit(solution)/shard_map/ppermute | solution.py:34
  172.9 45.2 %collective-permute-start.15 = (bf16[512,1024]{1,0:T(8,128)(2,1)S(1)}, bf16[512,1024]{1,0:T(8,128)(2,1)S(1)}, u32[]{:S(2)}, u32[]{:S(2)}) collective-permute-start(bf16[512,1024]{1,0:T(8,128)(2,1)S(1)} %copy-done.14), channel_id=1, source_target_pairs={{0,16},{8,24},{16,0},{24,8},{1,17},{9,25},{17,1},{25,9},{2,18},{10... | collective-permute-start | bytes 3145736 | tf_op jit(solution)/shard_map/ppermute | solution.py:39
  177.6 63.1 %collective-permute-start.13 = (bf16[512,1024]{1,0:T(8,128)(2,1)S(1)}, bf16[512,1024]{1,0:T(8,128)(2,1)}, u32[]{:S(2)}, u32[]{:S(2)}) collective-permute-start(bf16[512,1024]{1,0:T(8,128)(2,1)S(1)} %copy-done.13), channel_id=1, source_target_pairs={{0,16},{8,24},{16,0},{24,8},{1,17},{9,25},{17,1},{25,9},{2,18},{10... | collective-permute-start | bytes 3145736 | tf_op jit(solution)/shard_map/ppermute | solution.py:39
  227.7 13.0 %copy-start.17 = (bf16[512,1024]{1,0:T(8,128)(2,1)S(1)}, bf16[512,1024]{1,0:T(8,128)(2,1)}, u32[]{:S(2)}) copy-start(bf16[512,1024]{1,0:T(8,128)(2,1)} %convolution_convert_fusion.6) | copy-start | bytes 3145732
  228.7 15.2 %collective-permute-start.18 = (f32[9,2048]{1,0:T(8,128)S(1)}, f32[9,2048]{1,0:T(8,128)S(1)}, u32[]{:S(2)}, u32[]{:S(2)}) collective-permute-start(f32[9,2048]{1,0:T(8,128)S(1)} %pad_maximum_fusion.4), channel_id=1, source_target_pairs={{0,8},{8,0},{16,24},{24,16},{1,9},{9,1},{17,25},{25,17},{2,10},{10... | collective-permute-start | bytes 221192 | tf_op jit(solution)/shard_map/ppermute | solution.py:47
  228.8 15.1 %collective-permute-start.19 = (f32[9,2048]{1,0:T(8,128)S(1)}, f32[9,2048]{1,0:T(8,128)S(1)}, u32[]{:S(2)}, u32[]{:S(2)}) collective-permute-start(f32[9,2048]{1,0:T(8,128)S(1)} %pad_maximum_fusion.4), channel_id=1, source_target_pairs={{0,16},{8,24},{16,0},{24,8},{1,17},{9,25},{17,1},{25,9},{2,18},{10... | collective-permute-start | bytes 221192 | tf_op jit(solution)/shard_map/ppermute | solution.py:47
  230.4 14.2 %collective-permute-start.20 = (f32[9,2048]{1,0:T(8,128)S(1)}, f32[9,2048]{1,0:T(8,128)S(1)}, u32[]{:S(2)}, u32[]{:S(2)}) collective-permute-start(f32[9,2048]{1,0:T(8,128)S(1)} %pad_maximum_fusion.4), channel_id=1, source_target_pairs={{0,24},{8,16},{16,8},{24,0},{1,25},{9,17},{17,9},{25,1},{2,26},{10... | collective-permute-start | bytes 221192 | tf_op jit(solution)/shard_map/ppermute | solution.py:47
  244.6 6.1 %collective-permute-start.21 = (f32[9,2048]{1,0:T(8,128)S(1)}, f32[9,2048]{1,0:T(8,128)S(1)}, u32[]{:S(2)}, u32[]{:S(2)}) collective-permute-start(f32[9,2048]{1,0:T(8,128)S(1)} %add_add_fusion.4), channel_id=1, source_target_pairs={{0,1},{1,0},{2,3},{3,2},{4,5},{5,4},{6,7},{7,6},{8,9},{9,8},{10,11... | collective-permute-start | bytes 221192 | tf_op jit(solution)/shard_map/ppermute | solution.py:47
  246.3 6.3 %collective-permute-start.22 = (f32[9,2048]{1,0:T(8,128)S(1)}, f32[9,2048]{1,0:T(8,128)S(1)}, u32[]{:S(2)}, u32[]{:S(2)}) collective-permute-start(f32[9,2048]{1,0:T(8,128)S(1)} %add_add_fusion.4), channel_id=1, source_target_pairs={{0,2},{1,3},{2,0},{3,1},{4,6},{5,7},{6,4},{7,5},{8,10},{9,11},{10,... | collective-permute-start | bytes 221192 | tf_op jit(solution)/shard_map/ppermute | solution.py:47
  247.8 6.9 %collective-permute-start.23 = (f32[9,2048]{1,0:T(8,128)S(1)}, f32[9,2048]{1,0:T(8,128)S(1)}, u32[]{:S(2)}, u32[]{:S(2)}) collective-permute-start(f32[9,2048]{1,0:T(8,128)S(1)} %add_add_fusion.4), channel_id=1, source_target_pairs={{0,3},{1,2},{2,1},{3,0},{4,7},{5,6},{6,5},{7,4},{8,11},{9,10},{10,... | collective-permute-start | bytes 221192 | tf_op jit(solution)/shard_map/ppermute | solution.py:47
  254.8 8.8 %collective-permute-start.24 = (f32[9,2048]{1,0:T(8,128)S(1)}, f32[9,2048]{1,0:T(8,128)S(1)}, u32[]{:S(2)}, u32[]{:S(2)}) collective-permute-start(f32[9,2048]{1,0:T(8,128)S(1)} %add_add_fusion.3), channel_id=1, source_target_pairs={{0,4},{1,5},{2,6},{3,7},{4,0},{5,1},{6,2},{7,3},{8,12},{9,13},{10,... | collective-permute-start | bytes 221192 | tf_op jit(solution)/shard_map/ppermute | solution.py:47
  (25 other events, 75.6 us)

commit v3 on v2

--- a/solution.py
+++ b/solution.py
@@ -1,9 +1,14 @@
+import functools
+
 import jax
 import jax.numpy as jnp
 from jax import lax
+from jax.experimental import pallas as pl
+from jax.experimental.pallas import tpu as pltpu
 from jax.sharding import PartitionSpec as P
 
 norm_eps = 1e-06
+MESH = pl.DeviceIdType.MESH
 
 
 def product(left, right):
@@ -39,22 +44,81 @@
     return lax.ppermute(value, "dp", [(i, i ^ (2 * step)) for i in range(count)])
 
 
+def exchange_sum_kernel(n, m, v_ref, o_ref, near, far, mine, send_sem, recv_sem):
+    d, e = lax.axis_index("dp"), lax.axis_index("expert")
+    cols = v_ref.shape[1] // n
+    barrier = pltpu.get_barrier_semaphore()
+    dp_peers = [lax.rem(d + p, n) for p in range(1, n)]
+    ex_peers = [lax.rem(e + p, m) for p in range(1, m)]
+    for peer in dp_peers:
+        pl.semaphore_signal(barrier, inc=1, device_id=(peer, e), device_id_type=MESH)
+    for peer in ex_peers:
+        pl.semaphore_signal(barrier, inc=1, device_id=(d, peer), device_id_type=MESH)
+    pl.semaphore_wait(barrier, n + m - 2)
+
+    def chunk(ref, index):
+        return ref.at[:, pl.ds(pl.multiple_of(index * cols, cols), cols)]
+
+    def send(src, dst, sem, device):
+        copy = pltpu.make_async_remote_copy(
+            src_ref=src,
+            dst_ref=dst,
+            send_sem=send_sem.at[sem],
+            recv_sem=recv_sem.at[sem],
+            device_id=device,
+            device_id_type=MESH,
+        )
+        copy.start()
+        return copy
+
+    copies = [
+        send(chunk(v_ref, peer), near.at[i], i, (peer, e)) for i, peer in enumerate(dp_peers)
+    ]
+    value = v_ref[:, pl.ds(pl.multiple_of(d * cols, cols), cols)]
+    for i, copy in enumerate(copies):
+        copy.wait()
+        value = value + near[i]
+    mine[...] = value
+    far[e] = value
+    copies = [
+        send(mine, far.at[e], n - 1 + i, (d, peer)) for i, peer in enumerate(ex_peers)
+    ]
+    for copy in copies:
+        copy.wait()
+    value = far[0]
+    for i in range(1, m):
+        value = value + far[i]
+    mine[...] = value
+    o_ref[:, pl.ds(pl.multiple_of(d * cols, cols), cols)] = value
+    copies = [
+        send(mine, chunk(o_ref, d), n + m - 2 + i, (peer, e)) for i, peer in enumerate(dp_peers)
+    ]
+    for copy in copies:
+        copy.wait()
+
+
 def sum_over_all(value):
-    for axis in ("dp", "expert"):
-        count = lax.axis_size(axis)
-
-        def at(mask):
-            return lax.ppermute(value, axis, [(i, i ^ mask) for i in range(count)])
-
-        hop = 1
-        while hop < count:
-            if 4 * hop <= count:
-                value = (value + at(hop)) + (at(2 * hop) + at(3 * hop))
-                hop *= 4
-            else:
-                value = value + at(hop)
-                hop *= 2
-    return value
+    n, m = lax.axis_size("dp"), lax.axis_size("expert")
+    rows, width = value.shape
+    part = width // n
+    flights = 2 * (n - 1) + m - 1
+    return pl.pallas_call(
+        functools.partial(exchange_sum_kernel, n, m),
+        out_shape=jax.ShapeDtypeStruct((rows, width), jnp.float32),
+        in_specs=[pl.BlockSpec(memory_space=pltpu.VMEM)],
+        out_specs=pl.BlockSpec(memory_space=pltpu.VMEM),
+        scratch_shapes=[
+            pltpu.VMEM((n - 1, rows, part), jnp.float32),
+            pltpu.VMEM((m, rows, part), jnp.float32),
+            pltpu.VMEM((rows, part), jnp.float32),
+            pltpu.SemaphoreType.DMA((flights,)),
+            pltpu.SemaphoreType.DMA((flights,)),
+        ],
+        compiler_params=pltpu.CompilerParams(collective_id=0, has_side_effects=True),
+        cost_estimate=pl.CostEstimate(
+            flops=rows * width * (n + m), bytes_accessed=8 * rows * width * n, transcendentals=0
+        ),
+    )(value)
 
 
 def on_device(
@@ -117,6 +181,7 @@
 
     expert_in = exchange(product(fill, reordered(normed)).astype(jnp.bfloat16))
     d_out = exchange((slot_gate * product(fill, reordered(upstream))).astype(jnp.bfloat16))
+    d_out, pieces[2:] = lax.optimization_barrier((d_out, pieces[2:]))
     in_parts = split(expert_in)
 
     pre_gate = sum(product(x, w[0]) for x, w in zip(in_parts, pieces))
@@ -152,7 +217,10 @@
 
     away = [[v.astype(jnp.bfloat16) for v in pair_sum(k)] for k in range(1, chips)]
     totals = pair_sum(0)
-    away, d_pre_gate, d_pre_up = lax.optimization_barrier((away, d_pre_gate, d_pre_up))
+    landed = [[to_chip(v, k) for v in away[k - 1]] for k in range(1, chips)]
+    away, returned, d_pre_gate, d_pre_up = lax.optimization_barrier(
+        (away, returned, d_pre_gate, d_pre_up)
+    )
     d_rows = jnp.concatenate(
         [
             (transposed_product(d_pre_gate, w[0]) + transposed_product(d_pre_up, w[1])).astype(
@@ -162,10 +230,14 @@
         ],
         axis=1,
     )
+    if chips > 1:
+        d_rows, landed[0][0] = lax.optimization_barrier((d_rows, landed[0][0]))
+        returned, landed[0][2] = lax.optimization_barrier((returned, landed[0][2]))
     d_back = exchange(d_rows)
-    for k in range(1, chips):
-        landed = [to_chip(v, k).astype(jnp.float32) for v in away[k - 1]]
-        totals = [a + b for a, b in zip(totals, landed)]
+    if chips > 1:
+        d_back, landed[0][1] = lax.optimization_barrier((d_back, landed[0][1]))
+    for shares_landed in landed:
+        totals = [a + b.astype(jnp.float32) for a, b in zip(totals, shares_landed)]
     weight_gradients = [v.astype(jnp.bfloat16)[None] for v in totals]
 
     cotangent = upstream.astype(jnp.float32)
@@ -197,10 +269,10 @@
     d_unit = d_normed * gain
     inner = jnp.mean(d_unit * unit_rows, axis=-1, keepdims=True)
     d_tokens = (cotangent + inverse * (d_unit - unit_rows * inner)).astype(jnp.bfloat16)
-    part_gain = jnp.sum(d_normed * unit_rows, axis=0)
-    summed = sum_over_all(jnp.concatenate([part_router, part_gain[None]], axis=0))
+    part_gain = jnp.sum((d_normed * unit_rows).reshape(-1, 8, width), axis=0)
+    summed = sum_over_all(jnp.concatenate([part_router, part_gain], axis=0))
     d_router = summed[:experts].T
-    d_gain = summed[experts]
+    d_gain = jnp.sum(summed[experts:], axis=0)
     return (mixed, d_tokens, *weight_gradients, d_router, d_gain)
 
 

time: 266 us -> 302 us (1.14)
  waiting for transfers between devices: 129 us -> 150 us
  Pallas kernels: 0 us -> 17.6 us
  starting transfers between devices: 39 us -> 31.7 us
  other arithmetic: 16 us -> 21.3 us
    all_to_all x4, waiting for transfers between devices: 18.4 us -> 54.6 us  [exchange(): lax.all_to_all(rows.reshape(experts, capacity, width), 'expert', split_ax...]
    pallas_call x0 -> x1, Pallas kernels: none -> 17.6 us  [sum_over_all(): pl.pallas_call(functools.partial(exchange_sum_kernel, n, m), out_shape=ja...]
    ppermute x7 -> x0, waiting for transfers between devices: 12 us -> none  [at(): return lax.ppermute(value, axis, [(i, i ^ mask) for i in range(count)])]
    ppermute x7 -> x0, starting transfers between devices: 8.11 us -> none  [at(): return lax.ppermute(value, axis, [(i, i ^ mask) for i in range(count)])]
    ppermute x6, waiting for transfers between devices: 99 us -> 94.9 us  [to_chip(): return lax.ppermute(value, 'dp', [(i, i ^ 2 * step) for i in range(count)])]
    dot_general x12, matrix products: 19.4 us -> 23.2 us  [transposed_product(): lax.dot_general(left, right, (((1,), (1,)), ((), ())), preferred_element_...]
    dot_general x15, matrix products: 29.5 us -> 25.7 us  [inner_product(): lax.dot_general(left, right, (((0,), (0,)), ((), ())), preferred_element_...]
  transfers between devices with their start and end apart: 29 -> 22, of which waited for: 13 -> 7; matrix products, arithmetic and copies ran while one was open for 30% -> 25% of each run, Pallas kernels for 0% -> 6%
where the time goes in v3:
time: 302 us; the launch traced here: 300 us
  waiting for transfers between devices  150 us (50%)
  matrix products  72 us (24%)
  starting transfers between devices  31.7 us (10%)
  other arithmetic  21.3 us (7%)
  Pallas kernels  17.6 us (6%)
  local copies, waits for them, and re-layouts  6.85 us (2%)
    ppermute x6, waiting for transfers between devices, to_chip(): return lax.ppermute(value, 'dp', [(i, i ^ 2 * step) for i in range(count)])  94.9 us
    all_to_all x4, waiting for transfers between devices, exchange(): lax.all_to_all(rows.reshape(experts, capacity, width), 'expert', split_ax...  54.6 us
    dot_general x15, matrix products, inner_product(): lax.dot_general(left, right, (((0,), (0,)), ((), ())), preferred_element_...  25.7 us
    dot_general x12, matrix products, transposed_product(): lax.dot_general(left, right, (((1,), (1,)), ((), ())), preferred_element_...  23.2 us
    all_to_all x4, starting transfers between devices, exchange(): lax.all_to_all(rows.reshape(experts, capacity, width), 'expert', split_ax...  21.9 us
    dot_general x15, matrix products, product(): return jnp.dot(left, right, preferred_element_type=jnp.float32)  21.9 us
    pallas_call x1, Pallas kernels, sum_over_all(): pl.pallas_call(functools.partial(exchange_sum_kernel, n, m), out_shape=ja...  17.6 us
    broadcast_in_dim x3, other arithmetic, on_device(): weight_gradients = [v.astype(jnp.bfloat16)[None] for v in totals]  8.59 us
  transfers between devices with their start and end apart: 22, of which 7 were waited for; matrix products, arithmetic and copies ran while one was open for 25% of the time, Pallas kernels for 6%

profile of v3, /device:TPU:0, one launch (start us, length us, event | category | flops | bytes accessed | tf_op | source)
XLA Modules:
  0.0 300.3 jit_solution(11626966659972904120)
XLA Ops:
  7.9 7.4 %all-to-all-start = ((bf16[8,48,2048]{2,1,0:T(8,128)(2,1)}), bf16[8,48,2048]{2,1,0:T(8,128)(2,1)S(1)}, u32[]{:S(2)}, u32[]{:S(2)}) async-start(bf16[8,48,2048]{2,1,0:T(8,128)(2,1)} %bitcast.119), calls=%async_computation | async-start | bytes 3145728 | tf_op jit(solution)/shard_map/all_to_all | solution.py:174
  17.6 34.8 %all-to-all-done = bf16[8,48,2048]{2,1,0:T(8,128)(2,1)S(1)} async-done(((bf16[8,48,2048]{2,1,0:T(8,128)(2,1)}), bf16[8,48,2048]{2,1,0:T(8,128)(2,1)S(1)}, u32[]{:S(2)}, u32[]{:S(2)}) %all-to-all-start) | async-done | bytes 1572896 | tf_op jit(solution)/shard_map/all_to_all | solution.py:174
  52.3 4.3 %all-to-all-start.1 = ((bf16[8,48,2048]{2,1,0:T(8,128)(2,1)}), bf16[8,48,2048]{2,1,0:T(8,128)(2,1)}, u32[]{:S(2)}, u32[]{:S(2)}) async-start(bf16[8,48,2048]{2,1,0:T(8,128)(2,1)} %bitcast.9), calls=%async_computation.1 | async-start | bytes 3145728 | tf_op jit(solution)/shard_map/all_to_all | solution.py:174
  60.2 22.8 %collective-permute-done.1 = bf16[512,1024]{1,0:T(8,128)(2,1)S(1)} collective-permute-done((bf16[512,1024]{1,0:T(8,128)(2,1)}, bf16[512,1024]{1,0:T(8,128)(2,1)S(1)}, u32[]{:S(2)}, u32[]{:S(2)}) %collective-permute-start.1) | collective-permute-done | bytes 1048608 | tf_op jit(solution)/shard_map/ppermute | solution.py:44
  83.0 22.5 %collective-permute-done.2 = bf16[512,1024]{1,0:T(8,128)(2,1)S(1)} collective-permute-done((bf16[512,1024]{1,0:T(8,128)(2,1)}, bf16[512,1024]{1,0:T(8,128)(2,1)S(1)}, u32[]{:S(2)}, u32[]{:S(2)}) %collective-permute-start.2) | collective-permute-done | bytes 1048608 | tf_op jit(solution)/shard_map/ppermute | solution.py:44
  105.5 20.4 %collective-permute-done.3 = bf16[1024,512]{1,0:T(8,128)(2,1)S(1)} collective-permute-done((bf16[1024,512]{1,0:T(8,128)(2,1)}, bf16[1024,512]{1,0:T(8,128)(2,1)S(1)}, u32[]{:S(2)}, u32[]{:S(2)}) %collective-permute-start.3) | collective-permute-done | bytes 1048608 | tf_op jit(solution)/shard_map/ppermute | solution.py:44
  136.5 2.4 fusion.67
  138.9 2.1 multiply_convert_fusion.3
  141.0 2.1 convolution_convert_fusion.16
  148.8 2.7 fusion.47
  151.5 3.2 %fusion.53 = f32[384,1024]{1,0:T(8,128)} fusion(bf16[384,2048]{1,0:T(8,128)(2,1)} %bitcast.10, bf16[1,1024,512]{2,1,0:T(8,128)(2,1)} %param.15), kind=kOutput, calls=%fused_computation.98 | convolution fusion | flops 402653184 | bytes 3014656 | tf_op jit(solution)/shard_map/dot_general | solution.py:19
  154.8 5.7 %all-to-all-start.2 = ((bf16[8,48,2048]{2,1,0:T(8,128)(2,1)}), bf16[8,48,2048]{2,1,0:T(8,128)(2,1)}, u32[]{:S(2)}, u32[]{:S(2)}) async-start(bf16[8,48,2048]{2,1,0:T(8,128)(2,1)} %bitcast.13), calls=%async_computation.2 | async-start | bytes 3145728 | tf_op jit(solution)/shard_map/all_to_all | solution.py:174
  160.5 2.1 fusion.50
  162.6 4.0 %multiply_convert_fusion.1 = (bf16[384,1024]{1,0:T(8,128)(2,1)S(1)}, bf16[384,1024]{1,0:T(8,128)(2,1)S(1)}) fusion(f32[384,1024]{1,0:T(8,128)} %copy-done.19, f32[384,1024]{1,0:T(8,128)} %get-tuple-element.80, bf16[1024,512]{1,0:T(8,128)(2,1)} %collective-permute-done.6, bf16[384,2048]{1,0:T(8,128)(2,1)} %bitcast.10, f32[384,1024]{1,0:T(8,128)S(1)} %copy-done.18, ...), kind=kOutput, calls=%fused_computation.14 | convolution fusion | flops 408944640 | bytes 10878976 | tf_op jit(solution)/shard_map/dot_general | solution.py:19
  175.7 2.7 add_convert_fusion.3
  178.4 19.8 %all-to-all-done.2 = bf16[8,48,2048]{2,1,0:T(8,128)(2,1)} async-done(((bf16[8,48,2048]{2,1,0:T(8,128)(2,1)}), bf16[8,48,2048]{2,1,0:T(8,128)(2,1)}, u32[]{:S(2)}, u32[]{:S(2)}) %all-to-all-start.2) | async-done | bytes 1572896 | tf_op jit(solution)/shard_map/all_to_all | solution.py:174
  198.3 1.9 fusion.112
  200.8 1.9 fusion.107
  211.5 4.5 %all-to-all-start.3 = ((bf16[8,48,2048]{2,1,0:T(8,128)(2,1)}), bf16[8,48,2048]{2,1,0:T(8,128)(2,1)}, u32[]{:S(2)}, u32[]{:S(2)}) async-start(bf16[8,48,2048]{2,1,0:T(8,128)(2,1)} %bitcast.118), calls=%async_computation.3 | async-start | bytes 3145728 | tf_op jit(solution)/shard_map/all_to_all | solution.py:174
  222.9 2.7 convolution_convert_fusion.1
  226.1 2.7 convolution_convert_fusion.2
  229.3 14.6 %collective-permute-done.12 = bf16[1024,512]{1,0:T(8,128)(2,1)S(1)} collective-permute-done((bf16[1024,512]{1,0:T(8,128)(2,1)S(1)}, bf16[1024,512]{1,0:T(8,128)(2,1)S(1)}, u32[]{:S(2)}, u32[]{:S(2)}) %collective-permute-start.12) | collective-permute-done | bytes 1048608 | tf_op jit(solution)/shard_map/ppermute | solution.py:44
  243.9 2.3 fusion.85
  246.3 1.9 fusion.83
  248.2 2.8 fusion.24
  251.1 14.7 %collective-permute-done.14 = bf16[512,1024]{1,0:T(8,128)(2,1)} collective-permute-done((bf16[512,1024]{1,0:T(8,128)(2,1)S(1)}, bf16[512,1024]{1,0:T(8,128)(2,1)}, u32[]{:S(2)}, u32[]{:S(2)}) %collective-permute-start.14) | collective-permute-done | bytes 1048608 | tf_op jit(solution)/shard_map/ppermute | solution.py:44
  265.8 1.9 fusion.86
  272.2 2.6 fusion.26
  274.9 17.6 %shard_map.135 = f32[16,2048]{1,0:T(8,128)} custom-call(f32[16,2048]{1,0:T(8,128)} %pad_maximum_fusion.4.v_ref), custom_call_target="tpu_custom_call" | custom-call | flops 393216 | bytes 1048576 | tf_op jit(solution)/shard_map/pallas_call | solution.py:105
  292.4 2.1 slice_reduce_fusion
  294.6 2.6 fusion.23
  297.2 3.1 %fusion.25 = bf16[1,512,1024]{2,1,0:T(8,128)(2,1)} fusion(bf16[512,1024]{1,0:T(8,128)(2,1)} %collective-permute-done.14, bf16[512,1024]{1,0:T(8,128)(2,1)} %collective-permute-done.16, bf16[512,1024]{1,0:T(8,128)(2,1)S(1)} %copy-done.25), kind=kLoop, calls=%fused_computation.70 | loop fusion | flops 3145728 | bytes 4194304 | tf_op jit(solution)/shard_map/broadcast_in_dim | solution.py:241
  (166 shorter events, 60.0 us)
Async XLA Ops:
  0.6 14.7 %copy-start = (bf16[2048,8]{0,1:T(8,128)(2,1)S(1)}, bf16[2048,8]{0,1:T(8,128)(2,1)}, u32[]{:S(2)}) copy-start(bf16[2048,8]{0,1:T(8,128)(2,1)} %param.12) | copy-start | bytes 98308
  6.1 9.2 %copy-start.2 = (bf16[128,2048]{1,0:T(8,128)(2,1)}, bf16[128,2048]{1,0:T(8,128)(2,1)S(1)}, u32[]{:S(2)}) copy-start(bf16[128,2048]{1,0:T(8,128)(2,1)S(1)} %fusion.12) | copy-start | bytes 1572868
  7.9 7.6 %copy-start.30 = (s32[128,2]{0,1:T(2,128)S(1)}, s32[128,2]{0,1:T(2,128)}, u32[]{:S(2)}) copy-start(s32[128,2]{0,1:T(2,128)} %param.9) | copy-start | bytes 3076
  7.9 7.9 %copy-start.4 = (bf16[128,2048]{1,0:T(8,128)(2,1)S(1)}, bf16[128,2048]{1,0:T(8,128)(2,1)}, u32[]{:S(2)}) copy-start(bf16[128,2048]{1,0:T(8,128)(2,1)} %param.10) | copy-start | bytes 1572868
  7.9 44.4 %all-to-all-start = ((bf16[8,48,2048]{2,1,0:T(8,128)(2,1)}), bf16[8,48,2048]{2,1,0:T(8,128)(2,1)S(1)}, u32[]{:S(2)}, u32[]{:S(2)}) async-start(bf16[8,48,2048]{2,1,0:T(8,128)(2,1)} %bitcast.119), calls=%async_computation | async-start | bytes 3145728 | tf_op jit(solution)/shard_map/all_to_all | solution.py:174
  52.3 77.9 %all-to-all-start.1 = ((bf16[8,48,2048]{2,1,0:T(8,128)(2,1)}), bf16[8,48,2048]{2,1,0:T(8,128)(2,1)}, u32[]{:S(2)}, u32[]{:S(2)}) async-start(bf16[8,48,2048]{2,1,0:T(8,128)(2,1)} %bitcast.9), calls=%async_computation.1 | async-start | bytes 3145728 | tf_op jit(solution)/shard_map/all_to_all | solution.py:174
  56.6 26.4 %collective-permute-start.1 = (bf16[512,1024]{1,0:T(8,128)(2,1)}, bf16[512,1024]{1,0:T(8,128)(2,1)S(1)}, u32[]{:S(2)}, u32[]{:S(2)}) collective-permute-start(bf16[512,1024]{1,0:T(8,128)(2,1)} %bitcast.7), channel_id=1, source_target_pairs={{0,16},{8,24},{16,0},{24,8},{1,17},{9,25},{17,1},{25,9},{2,18},{10... | collective-permute-start | bytes 3145736 | tf_op jit(solution)/shard_map/ppermute | solution.py:44
  58.2 47.3 %collective-permute-start.2 = (bf16[512,1024]{1,0:T(8,128)(2,1)}, bf16[512,1024]{1,0:T(8,128)(2,1)S(1)}, u32[]{:S(2)}, u32[]{:S(2)}) collective-permute-start(bf16[512,1024]{1,0:T(8,128)(2,1)} %bitcast.11), channel_id=1, source_target_pairs={{0,16},{8,24},{16,0},{24,8},{1,17},{9,25},{17,1},{25,9},{2,18},{10... | collective-permute-start | bytes 3145736 | tf_op jit(solution)/shard_map/ppermute | solution.py:44
  58.7 67.2 %collective-permute-start.3 = (bf16[1024,512]{1,0:T(8,128)(2,1)}, bf16[1024,512]{1,0:T(8,128)(2,1)S(1)}, u32[]{:S(2)}, u32[]{:S(2)}) collective-permute-start(bf16[1024,512]{1,0:T(8,128)(2,1)} %bitcast.12), channel_id=1, source_target_pairs={{0,16},{8,24},{16,0},{24,8},{1,17},{9,25},{17,1},{25,9},{2,18},{10... | collective-permute-start | bytes 3145736 | tf_op jit(solution)/shard_map/ppermute | solution.py:44
  83.0 43.4 %copy-start.6 = (bf16[512,1024]{1,0:T(8,128)(2,1)}, bf16[512,1024]{1,0:T(8,128)(2,1)S(1)}, u32[]{:S(2)}) copy-start(bf16[512,1024]{1,0:T(8,128)(2,1)S(1)} %collective-permute-done.1) | copy-start | bytes 3145732
  83.0 45.2 %collective-permute-start.4 = (bf16[512,1024]{1,0:T(8,128)(2,1)S(1)}, bf16[512,1024]{1,0:T(8,128)(2,1)S(1)}, u32[]{:S(2)}, u32[]{:S(2)}) collective-permute-start(bf16[512,1024]{1,0:T(8,128)(2,1)S(1)} %collective-permute-done.1), channel_id=1, source_target_pairs={{0,8},{8,0},{16,24},{24,16},{1,9},{9,1},{17,25},{25,17},{2,10},{10... | collective-permute-start | bytes 3145736 | tf_op jit(solution)/shard_map/ppermute | solution.py:39
  105.5 22.8 %copy-start.9 = (bf16[512,1024]{1,0:T(8,128)(2,1)}, bf16[512,1024]{1,0:T(8,128)(2,1)S(1)}, u32[]{:S(2)}) copy-start(bf16[512,1024]{1,0:T(8,128)(2,1)S(1)} %collective-permute-done.2) | copy-start | bytes 3145732
  105.5 23.4 %collective-permute-start.5 = (bf16[512,1024]{1,0:T(8,128)(2,1)S(1)}, bf16[512,1024]{1,0:T(8,128)(2,1)S(1)}, u32[]{:S(2)}, u32[]{:S(2)}) collective-permute-start(bf16[512,1024]{1,0:T(8,128)(2,1)S(1)} %collective-permute-done.2), channel_id=1, source_target_pairs={{0,8},{8,0},{16,24},{24,16},{1,9},{9,1},{17,25},{25,17},{2,10},{10... | collective-permute-start | bytes 3145736 | tf_op jit(solution)/shard_map/ppermute | solution.py:39
  125.9 4.3 %collective-permute-start.6 = (bf16[1024,512]{1,0:T(8,128)(2,1)S(1)}, bf16[1024,512]{1,0:T(8,128)(2,1)}, u32[]{:S(2)}, u32[]{:S(2)}) collective-permute-start(bf16[1024,512]{1,0:T(8,128)(2,1)S(1)} %collective-permute-done.3), channel_id=1, source_target_pairs={{0,8},{8,0},{16,24},{24,16},{1,9},{9,1},{17,25},{25,17},{2,10},{10... | collective-permute-start | bytes 3145736 | tf_op jit(solution)/shard_map/ppermute | solution.py:39
  125.9 8.0 %collective-permute-start = (bf16[512,1024]{1,0:T(8,128)(2,1)}, bf16[512,1024]{1,0:T(8,128)(2,1)}, u32[]{:S(2)}, u32[]{:S(2)}) collective-permute-start(bf16[512,1024]{1,0:T(8,128)(2,1)} %bitcast.7), channel_id=1, source_target_pairs={{0,8},{8,0},{16,24},{24,16},{1,9},{9,1},{17,25},{25,17},{2,10},{10... | collective-permute-start | bytes 3145736 | tf_op jit(solution)/shard_map/ppermute | solution.py:39
  126.4 10.1 %collective-permute-start.7 = (bf16[512,1024]{1,0:T(8,128)(2,1)}, bf16[512,1024]{1,0:T(8,128)(2,1)}, u32[]{:S(2)}, u32[]{:S(2)}) collective-permute-start(bf16[512,1024]{1,0:T(8,128)(2,1)} %bitcast.11), channel_id=1, source_target_pairs={{0,8},{8,0},{16,24},{24,16},{1,9},{9,1},{17,25},{25,17},{2,10},{10... | collective-permute-start | bytes 3145736 | tf_op jit(solution)/shard_map/ppermute | solution.py:39
  128.3 17.4 %collective-permute-start.8 = (bf16[1024,512]{1,0:T(8,128)(2,1)}, bf16[1024,512]{1,0:T(8,128)(2,1)}, u32[]{:S(2)}, u32[]{:S(2)}) collective-permute-start(bf16[1024,512]{1,0:T(8,128)(2,1)} %bitcast.12), channel_id=1, source_target_pairs={{0,8},{8,0},{16,24},{24,16},{1,9},{9,1},{17,25},{25,17},{2,10},{10... | collective-permute-start | bytes 3145736 | tf_op jit(solution)/shard_map/ppermute | solution.py:39
  136.5 4.5 %copy-start.19 = (f32[384,1024]{1,0:T(8,128)}, f32[384,1024]{1,0:T(8,128)S(1)}, u32[]{:S(2)}) copy-start(f32[384,1024]{1,0:T(8,128)S(1)} %add_add_fusion.2) | copy-start | bytes 4718596
  141.0 4.6 %copy-start.32 = (bf16[384,1024]{1,0:T(8,128)(2,1)}, bf16[384,1024]{1,0:T(8,128)(2,1)S(1)}, u32[]{:S(2)}) copy-start(bf16[384,1024]{1,0:T(8,128)(2,1)S(1)} %get-tuple-element.34) | copy-start | bytes 2359300
  154.8 43.5 %all-to-all-start.2 = ((bf16[8,48,2048]{2,1,0:T(8,128)(2,1)}), bf16[8,48,2048]{2,1,0:T(8,128)(2,1)}, u32[]{:S(2)}, u32[]{:S(2)}) async-start(bf16[8,48,2048]{2,1,0:T(8,128)(2,1)} %bitcast.13), calls=%async_computation.2 | async-start | bytes 3145728 | tf_op jit(solution)/shard_map/all_to_all | solution.py:174
  167.3 3.4 %collective-permute-start.9 = (bf16[512,1024]{1,0:T(8,128)(2,1)S(1)}, bf16[512,1024]{1,0:T(8,128)(2,1)S(1)}, u32[]{:S(2)}, u32[]{:S(2)}) collective-permute-start(bf16[512,1024]{1,0:T(8,128)(2,1)S(1)} %convolution_convert_fusion.11), channel_id=1, source_target_pairs={{0,8},{8,0},{16,24},{24,16},{1,9},{9,1},{17,25},{25,17},{2,10},{10... | collective-permute-start | bytes 3145736 | tf_op jit(solution)/shard_map/ppermute | solution.py:39
  168.3 5.7 %collective-permute-start.10 = (bf16[512,1024]{1,0:T(8,128)(2,1)S(1)}, bf16[512,1024]{1,0:T(8,128)(2,1)S(1)}, u32[]{:S(2)}, u32[]{:S(2)}) collective-permute-start(bf16[512,1024]{1,0:T(8,128)(2,1)S(1)} %convolution_convert_fusion.9), channel_id=1, source_target_pairs={{0,8},{8,0},{16,24},{24,16},{1,9},{9,1},{17,25},{25,17},{2,10},{10... | collective-permute-start | bytes 3145736 | tf_op jit(solution)/shard_map/ppermute | solution.py:39
  170.4 5.3 %collective-permute-start.11 = (bf16[1024,512]{1,0:T(8,128)(2,1)S(1)}, bf16[1024,512]{1,0:T(8,128)(2,1)S(1)}, u32[]{:S(2)}, u32[]{:S(2)}) collective-permute-start(bf16[1024,512]{1,0:T(8,128)(2,1)S(1)} %convolution_convert_fusion.7), channel_id=1, source_target_pairs={{0,8},{8,0},{16,24},{24,16},{1,9},{9,1},{17,25},{25,17},{2,10},{10... | collective-permute-start | bytes 3145736 | tf_op jit(solution)/shard_map/ppermute | solution.py:39
  172.5 39.0 %collective-permute-start.13 = (bf16[512,1024]{1,0:T(8,128)(2,1)}, bf16[512,1024]{1,0:T(8,128)(2,1)}, u32[]{:S(2)}, u32[]{:S(2)}) collective-permute-start(bf16[512,1024]{1,0:T(8,128)(2,1)} %add_convert_fusion.5), channel_id=1, source_target_pairs={{0,16},{8,24},{16,0},{24,8},{1,17},{9,25},{17,1},{25,9},{2,18},{10... | collective-permute-start | bytes 3145736 | tf_op jit(solution)/shard_map/ppermute | solution.py:44
  211.5 54.3 %all-to-all-start.3 = ((bf16[8,48,2048]{2,1,0:T(8,128)(2,1)}), bf16[8,48,2048]{2,1,0:T(8,128)(2,1)}, u32[]{:S(2)}, u32[]{:S(2)}) async-start(bf16[8,48,2048]{2,1,0:T(8,128)(2,1)} %bitcast.118), calls=%async_computation.3 | async-start | bytes 3145728 | tf_op jit(solution)/shard_map/all_to_all | solution.py:174
  216.7 31.5 %collective-permute-start.15 = (bf16[512,1024]{1,0:T(8,128)(2,1)S(1)}, bf16[512,1024]{1,0:T(8,128)(2,1)S(1)}, u32[]{:S(2)}, u32[]{:S(2)}) collective-permute-start(bf16[512,1024]{1,0:T(8,128)(2,1)S(1)} %convolution_convert_fusion.5), channel_id=1, source_target_pairs={{0,8},{8,0},{16,24},{24,16},{1,9},{9,1},{17,25},{25,17},{2,10},{10... | collective-permute-start | bytes 3145736 | tf_op jit(solution)/shard_map/ppermute | solution.py:39
  217.9 26.0 %collective-permute-start.12 = (bf16[1024,512]{1,0:T(8,128)(2,1)S(1)}, bf16[1024,512]{1,0:T(8,128)(2,1)S(1)}, u32[]{:S(2)}, u32[]{:S(2)}) collective-permute-start(bf16[1024,512]{1,0:T(8,128)(2,1)S(1)} %copy-done.31), channel_id=1, source_target_pairs={{0,16},{8,24},{16,0},{24,8},{1,17},{9,25},{17,1},{25,9},{2,18},{10... | collective-permute-start | bytes 3145736 | tf_op jit(solution)/shard_map/ppermute | solution.py:44
  225.6 3.3 %copy-start.20 = (bf16[512,1024]{1,0:T(8,128)(2,1)S(1)}, bf16[512,1024]{1,0:T(8,128)(2,1)}, u32[]{:S(2)}) copy-start(bf16[512,1024]{1,0:T(8,128)(2,1)} %add_convert_fusion.4) | copy-start | bytes 3145732
  225.6 71.6 %collective-permute-start.16 = (bf16[512,1024]{1,0:T(8,128)(2,1)}, bf16[512,1024]{1,0:T(8,128)(2,1)}, u32[]{:S(2)}, u32[]{:S(2)}) collective-permute-start(bf16[512,1024]{1,0:T(8,128)(2,1)} %convolution_convert_fusion.3), channel_id=1, source_target_pairs={{0,8},{8,0},{16,24},{24,16},{1,9},{9,1},{17,25},{25,17},{2,10},{10... | collective-permute-start | bytes 3145736 | tf_op jit(solution)/shard_map/ppermute | solution.py:39
  225.6 46.7 %collective-permute-start.17 = (bf16[1024,512]{1,0:T(8,128)(2,1)}, bf16[1024,512]{1,0:T(8,128)(2,1)}, u32[]{:S(2)}, u32[]{:S(2)}) collective-permute-start(bf16[1024,512]{1,0:T(8,128)(2,1)} %convolution_convert_fusion.1), channel_id=1, source_target_pairs={{0,8},{8,0},{16,24},{24,16},{1,9},{9,1},{17,25},{25,17},{2,10},{10... | collective-permute-start | bytes 3145736 | tf_op jit(solution)/shard_map/ppermute | solution.py:39
  228.8 36.9 %collective-permute-start.14 = (bf16[512,1024]{1,0:T(8,128)(2,1)S(1)}, bf16[512,1024]{1,0:T(8,128)(2,1)}, u32[]{:S(2)}, u32[]{:S(2)}) collective-permute-start(bf16[512,1024]{1,0:T(8,128)(2,1)S(1)} %copy-done.20), channel_id=1, source_target_pairs={{0,16},{8,24},{16,0},{24,8},{1,17},{9,25},{17,1},{25,9},{2,18},{10... | collective-permute-start | bytes 3145736 | tf_op jit(solution)/shard_map/ppermute | solution.py:44
  269.3 3.0 copy-start.28
  (25 other events, 44.4 us)

commit v4 on v3

--- a/solution.py
+++ b/solution.py
@@ -179,9 +179,24 @@
             tiled=True,
         ).reshape(slots, width)
 
-    expert_in = exchange(product(fill, reordered(normed)).astype(jnp.bfloat16))
-    d_out = exchange((slot_gate * product(fill, reordered(upstream))).astype(jnp.bfloat16))
-    d_out, pieces[2:] = lax.optimization_barrier((d_out, pieces[2:]))
+    arrived = lax.all_to_all(
+        jnp.concatenate(
+            [
+                rows.reshape(experts, capacity, width)
+                for rows in (
+                    product(fill, reordered(normed)).astype(jnp.bfloat16),
+                    (slot_gate * product(fill, reordered(upstream))).astype(jnp.bfloat16),
+                )
+            ],
+            axis=1,
+        ),
+        "expert",
+        split_axis=0,
+        concat_axis=0,
+        tiled=True,
+    )
+    expert_in = arrived[:, :capacity].reshape(slots, width)
+    d_out = arrived[:, capacity:].reshape(slots, width)
     in_parts = split(expert_in)
 
     pre_gate = sum(product(x, w[0]) for x, w in zip(in_parts, pieces))
@@ -201,43 +216,42 @@
     d_pre_gate = (d_hidden * pre_up * sigma * (1.0 + pre_gate * (1.0 - sigma))).astype(jnp.bfloat16)
     d_pre_up = (d_hidden * active).astype(jnp.bfloat16)
 
-    def shares(index):
-        x, d = in_parts[index], out_parts[index]
-        return (
-            inner_product(x, d_pre_gate).astype(jnp.bfloat16),
-            inner_product(x, d_pre_up).astype(jnp.bfloat16),
-            inner_product(hidden, d).astype(jnp.bfloat16),
+    def pair_sum(lefts, rights, k, waited=()):
+        theirs = to_sibling(inner_product(lefts[2 * k + 1], rights[2 * k + 1]).astype(jnp.bfloat16))
+        theirs, waited = lax.optimization_barrier((theirs, waited))
+        mine = inner_product(lefts[2 * k], rights[2 * k]).astype(jnp.bfloat16)
+        return mine.astype(jnp.float32) + theirs.astype(jnp.float32)
+
+    def from_chips(lefts, rights, waited=()):
+        return [
+            to_chip(pair_sum(lefts, rights, k, waited).astype(jnp.bfloat16), k)
+            for k in range(1, chips)
+        ]
+
+    hiddens, d_gates_in, d_ups_in = ([v] * dp_count for v in (hidden, d_pre_gate, d_pre_up))
+    landed_down = from_chips(hiddens, out_parts)
+    landed_gate = from_chips(in_parts, d_gates_in, landed_down)
+    landed_up = from_chips(in_parts, d_ups_in, landed_down)
+
+    def d_rows_of(w, d_gate, d_up):
+        return (transposed_product(d_gate, w[0]) + transposed_product(d_up, w[1])).astype(
+            jnp.bfloat16
         )
 
-    def pair_sum(k):
-        theirs = [to_sibling(v) for v in shares(2 * k + 1)]
-        return [
-            a.astype(jnp.float32) + b.astype(jnp.float32) for a, b in zip(shares(2 * k), theirs)
-        ]
-
-    away = [[v.astype(jnp.bfloat16) for v in pair_sum(k)] for k in range(1, chips)]
-    totals = pair_sum(0)
-    landed = [[to_chip(v, k) for v in away[k - 1]] for k in range(1, chips)]
-    away, returned, d_pre_gate, d_pre_up = lax.optimization_barrier(
-        (away, returned, d_pre_gate, d_pre_up)
-    )
-    d_rows = jnp.concatenate(
-        [
-            (transposed_product(d_pre_gate, w[0]) + transposed_product(d_pre_up, w[1])).astype(
-                jnp.bfloat16
-            )
-            for w in pieces
-        ],
-        axis=1,
-    )
-    if chips > 1:
-        d_rows, landed[0][0] = lax.optimization_barrier((d_rows, landed[0][0]))
-        returned, landed[0][2] = lax.optimization_barrier((returned, landed[0][2]))
-    d_back = exchange(d_rows)
-    if chips > 1:
-        d_back, landed[0][1] = lax.optimization_barrier((d_back, landed[0][1]))
-    for shares_landed in landed:
-        totals = [a + b.astype(jnp.float32) for a, b in zip(totals, shares_landed)]
+    d_rows = [d_rows_of(pieces[0], d_pre_gate, d_pre_up)]
+    returned, late_gate, late_up = lax.optimization_barrier((returned, d_pre_gate, d_pre_up))
+    d_rows += [d_rows_of(w, late_gate, late_up) for w in pieces[1:]]
+    d_rows, landed_gate = lax.optimization_barrier((d_rows, landed_gate))
+    d_back = exchange(jnp.concatenate(d_rows, axis=1))
+    d_back, landed_up = lax.optimization_barrier((d_back, landed_up))
+    totals = [
+        sum((v.astype(jnp.float32) for v in landed), pair_sum(lefts, rights, 0))
+        for landed, lefts, rights in (
+            (landed_gate, in_parts, d_gates_in),
+            (landed_up, in_parts, d_ups_in),
+            (landed_down, hiddens, out_parts),
+        )
+    ]
     weight_gradients = [v.astype(jnp.bfloat16)[None] for v in totals]
 
     cotangent = upstream.astype(jnp.float32)

time: 302 us -> 264 us (0.87)
  waiting for transfers between devices: 150 us -> 116 us
  matrix products: 72 us -> 61.3 us
  other arithmetic: 21.3 us -> 28 us
  starting transfers between devices: 31.7 us -> 28 us
    all_to_all x4 -> x2, waiting for transfers between devices: 54.6 us -> 0.02 us  [exchange(): lax.all_to_all(rows.reshape(experts, capacity, width), 'expert', split_ax...]
    all_to_all x0 -> x1, waiting for transfers between devices: none -> 21.8 us  [on_device(): lax.all_to_all(jnp.concatenate([rows.reshape(experts, capacity, width) fo...]
    all_to_all x4 -> x2, starting transfers between devices: 21.9 us -> 10.2 us  [exchange(): lax.all_to_all(rows.reshape(experts, capacity, width), 'expert', split_ax...]
    all_to_all x0 -> x1, starting transfers between devices: none -> 7.25 us  [on_device(): lax.all_to_all(jnp.concatenate([rows.reshape(experts, capacity, width) fo...]
    dot_general x15, matrix products: 25.7 us -> 19.7 us  [inner_product(): lax.dot_general(left, right, (((0,), (0,)), ((), ())), preferred_element_...]
    convert_element_type x0 -> x3, other arithmetic: none -> 4.53 us  [from_chips(): pair_sum(lefts, rights, k, waited).astype(jnp.bfloat16)]
    unnamed x71 -> x85, local copies, waits for them, and re-layouts: 5.74 us -> 7.39 us
  transfers between devices with their start and end apart: 22 -> 21, of which waited for: 7 -> 6; matrix products, arithmetic and copies ran while one was open for 25% -> 24% of each run, Pallas kernels for 6% -> 0%
where the time goes in v4:
time: 264 us; the launch traced here: 262 us
  waiting for transfers between devices  116 us (44%)
  matrix products  61.3 us (23%)
  other arithmetic  28 us (11%)
  starting transfers between devices  28 us (11%)
  Pallas kernels  17.9 us (7%)
  local copies, waits for them, and re-layouts  9.43 us (4%)
    ppermute x6, waiting for transfers between devices, to_chip(): return lax.ppermute(value, 'dp', [(i, i ^ 2 * step) for i in range(count)])  94.4 us
    all_to_all x1, waiting for transfers between devices, on_device(): lax.all_to_all(jnp.concatenate([rows.reshape(experts, capacity, width) fo...  21.8 us
    dot_general x12, matrix products, transposed_product(): lax.dot_general(left, right, (((1,), (1,)), ((), ())), preferred_element_...  21.4 us
    dot_general x15, matrix products, inner_product(): lax.dot_general(left, right, (((0,), (0,)), ((), ())), preferred_element_...  19.7 us
    dot_general x15, matrix products, product(): return jnp.dot(left, right, preferred_element_type=jnp.float32)  19 us
    pallas_call x1, Pallas kernels, sum_over_all(): pl.pallas_call(functools.partial(exchange_sum_kernel, n, m), out_shape=ja...  17.9 us
    all_to_all x2, starting transfers between devices, exchange(): lax.all_to_all(rows.reshape(experts, capacity, width), 'expert', split_ax...  10.2 us
    broadcast_in_dim x3, other arithmetic, on_device(): weight_gradients = [v.astype(jnp.bfloat16)[None] for v in totals]  8.65 us
  transfers between devices with their start and end apart: 21, of which 6 were waited for; matrix products, arithmetic and copies ran while one was open for 24% of the time, Pallas kernels for 0%

profile of v4, /device:TPU:0, one launch (start us, length us, event | category | flops | bytes accessed | tf_op | source)
XLA Modules:
  0.0 262.2 jit_solution(16281531390656627062)
XLA Ops:
  8.5 2.1 pad_maximum_fusion
  10.6 7.2 %all-to-all-start = ((bf16[8,96,2048]{2,1,0:T(8,128)(2,1)}), bf16[8,96,2048]{2,1,0:T(8,128)(2,1)S(1)}, u32[]{:S(2)}, u32[]{:S(2)}) async-start(bf16[8,96,2048]{2,1,0:T(8,128)(2,1)} %pad_maximum_fusion), calls=%async_computation | async-start | bytes 6291456 | tf_op jit(solution)/shard_map/all_to_all | solution.py:182
  21.9 22.3 %collective-permute-done.1 = bf16[512,1024]{1,0:T(8,128)(2,1)} collective-permute-done((bf16[512,1024]{1,0:T(8,128)(2,1)}, bf16[512,1024]{1,0:T(8,128)(2,1)}, u32[]{:S(2)}, u32[]{:S(2)}) %collective-permute-start.1) | collective-permute-done | bytes 1048608 | tf_op jit(solution)/shard_map/ppermute | solution.py:44
  44.3 22.5 %collective-permute-done.4 = bf16[512,1024]{1,0:T(8,128)(2,1)} collective-permute-done((bf16[512,1024]{1,0:T(8,128)(2,1)}, bf16[512,1024]{1,0:T(8,128)(2,1)}, u32[]{:S(2)}, u32[]{:S(2)}) %collective-permute-start.4) | collective-permute-done | bytes 1048608 | tf_op jit(solution)/shard_map/ppermute | solution.py:44
  66.7 21.8 %all-to-all-done = bf16[8,96,2048]{2,1,0:T(8,128)(2,1)S(1)} async-done(((bf16[8,96,2048]{2,1,0:T(8,128)(2,1)}), bf16[8,96,2048]{2,1,0:T(8,128)(2,1)S(1)}, u32[]{:S(2)}, u32[]{:S(2)}) %all-to-all-start) | async-done | bytes 3145760 | tf_op jit(solution)/shard_map/all_to_all | solution.py:182
  91.7 1.8 fusion.60
  93.5 1.9 fusion.58
  99.6 1.8 add_add_fusion.2
  101.5 3.9 %multiply_convert_fusion.3 = (bf16[384,1024]{1,0:T(8,128)(2,1)S(1)}, f32[384,1024]{1,0:T(8,128)}) fusion(f32[384,1024]{1,0:T(8,128)S(1)} %add_add_fusion.2, bf16[512,1024]{1,0:T(8,128)(2,1)} %collective-permute-done.5, bf16[384,2048]{1,0:T(8,128)(2,1)S(1)} %bitcast.111, f32[384,1024]{1,0:T(8,128)S(1)} %fusion.58, f32[384,1024]{1,0:T(8,128)S(1)} %fusion.70, ...), kind=kOutput, calls=%fused_computation.18 | convolution fusion | flops 406192128 | bytes 10092544 | tf_op jit(solution)/shard_map/dot_general | solution.py:15
  106.0 1.8 convolution_convert_fusion.14
  113.9 3.9 %all-to-all-start.1 = ((bf16[8,48,2048]{2,1,0:T(8,128)(2,1)}), bf16[8,48,2048]{2,1,0:T(8,128)(2,1)S(1)}, u32[]{:S(2)}, u32[]{:S(2)}) async-start(bf16[8,48,2048]{2,1,0:T(8,128)(2,1)} %bitcast.13), calls=%async_computation.1 | async-start | bytes 3145728 | tf_op jit(solution)/shard_map/all_to_all | solution.py:174
  117.8 2.0 fusion.47
  119.8 2.0 fusion.44
  121.9 2.7 %multiply_convert_fusion.1 = (bf16[384,1024]{1,0:T(8,128)(2,1)S(1)}, bf16[384,1024]{1,0:T(8,128)(2,1)S(1)}) fusion(f32[384,1024]{1,0:T(8,128)S(1)} %copy-done.26, f32[384,1024]{1,0:T(8,128)} %get-tuple-element.74, bf16[1024,512]{1,0:T(8,128)(2,1)S(1)} %copy-done.38, bf16[384,2048]{1,0:T(8,128)(2,1)S(1)} %bitcast.126, f32[384,1024]{1,0:T(8,128)S(1)} %fusion.44, ...), kind=kOutput, calls=%fused_computation.15 | convolution fusion | flops 408944640 | bytes 10878976 | tf_op jit(solution)/shard_map/dot_general | solution.py:19
  139.2 18.1 %collective-permute-done.11 = bf16[1024,512]{1,0:T(8,128)(2,1)S(1)} collective-permute-done((bf16[1024,512]{1,0:T(8,128)(2,1)S(1)}, bf16[1024,512]{1,0:T(8,128)(2,1)S(1)}, u32[]{:S(2)}, u32[]{:S(2)}) %collective-permute-start.11) | collective-permute-done | bytes 1048608 | tf_op jit(solution)/shard_map/ppermute | solution.py:44
  160.2 1.8 fusion.104
  162.0 1.8 fusion.103
  163.9 1.8 fusion.102
  165.7 1.8 fusion.8
  167.6 1.8 fusion.7
  169.4 1.9 fusion.6
  171.3 12.0 %collective-permute-done.12 = bf16[512,1024]{1,0:T(8,128)(2,1)} collective-permute-done((bf16[512,1024]{1,0:T(8,128)(2,1)}, bf16[512,1024]{1,0:T(8,128)(2,1)}, u32[]{:S(2)}, u32[]{:S(2)}) %collective-permute-start.12) | collective-permute-done | bytes 1048608 | tf_op jit(solution)/shard_map/ppermute | solution.py:44
  184.7 6.3 %all-to-all-start.2 = ((bf16[8,48,2048]{2,1,0:T(8,128)(2,1)}), bf16[8,48,2048]{2,1,0:T(8,128)(2,1)}, u32[]{:S(2)}, u32[]{:S(2)}) async-start(bf16[8,48,2048]{2,1,0:T(8,128)(2,1)} %bitcast.120), calls=%async_computation.2 | async-start | bytes 3145728 | tf_op jit(solution)/shard_map/all_to_all | solution.py:174
  191.0 1.8 convolution_convert_fusion.5
  203.3 2.6 fusion.26
  207.8 19.4 %collective-permute-done.14 = bf16[512,1024]{1,0:T(8,128)(2,1)} collective-permute-done((bf16[512,1024]{1,0:T(8,128)(2,1)S(1)}, bf16[512,1024]{1,0:T(8,128)(2,1)}, u32[]{:S(2)}, u32[]{:S(2)}) %collective-permute-start.14) | collective-permute-done | bytes 1048608 | tf_op jit(solution)/shard_map/ppermute | solution.py:44
  227.2 1.9 fusion.77
  233.6 2.9 %fusion.24 = bf16[1,512,1024]{2,1,0:T(8,128)(2,1)} fusion(bf16[512,1024]{1,0:T(8,128)(2,1)} %collective-permute-done.12, bf16[512,1024]{1,0:T(8,128)(2,1)S(1)} %copy-done.31, bf16[512,1024]{1,0:T(8,128)(2,1)S(1)} %copy-done.32), kind=kLoop, calls=%fused_computation.70 | loop fusion | flops 3145728 | bytes 4194304 | tf_op jit(solution)/shard_map/broadcast_in_dim | solution.py:255
  236.5 17.9 %shard_map.135 = f32[16,2048]{1,0:T(8,128)} custom-call(f32[16,2048]{1,0:T(8,128)} %pad_maximum_fusion.5.v_ref), custom_call_target="tpu_custom_call" | custom-call | flops 393216 | bytes 1048576 | tf_op jit(solution)/shard_map/pallas_call | solution.py:105
  254.3 2.1 slice_reduce_fusion
  256.5 2.6 fusion.23
  259.1 3.1 %fusion.25 = bf16[1,512,1024]{2,1,0:T(8,128)(2,1)} fusion(bf16[512,1024]{1,0:T(8,128)(2,1)} %collective-permute-done.14, bf16[512,1024]{1,0:T(8,128)(2,1)} %collective-permute-done.16, bf16[512,1024]{1,0:T(8,128)(2,1)S(1)} %copy-done.29), kind=kLoop, calls=%fused_computation.71 | loop fusion | flops 3145728 | bytes 4194304 | tf_op jit(solution)/shard_map/broadcast_in_dim | solution.py:255
  (183 shorter events, 61.1 us)
Async XLA Ops:
  0.6 6.3 %copy-start = (bf16[2048,8]{0,1:T(8,128)(2,1)S(1)}, bf16[2048,8]{0,1:T(8,128)(2,1)}, u32[]{:S(2)}) copy-start(bf16[2048,8]{0,1:T(8,128)(2,1)} %param.12) | copy-start | bytes 98308
  0.6 5.6 %copy-start.10 = (bf16[128,2048]{1,0:T(8,128)(2,1)S(1)}, bf16[128,2048]{1,0:T(8,128)(2,1)}, u32[]{:S(2)}) copy-start(bf16[128,2048]{1,0:T(8,128)(2,1)} %param.10) | copy-start | bytes 1572868
  10.6 78.0 %all-to-all-start = ((bf16[8,96,2048]{2,1,0:T(8,128)(2,1)}), bf16[8,96,2048]{2,1,0:T(8,128)(2,1)S(1)}, u32[]{:S(2)}, u32[]{:S(2)}) async-start(bf16[8,96,2048]{2,1,0:T(8,128)(2,1)} %pad_maximum_fusion), calls=%async_computation | async-start | bytes 6291456 | tf_op jit(solution)/shard_map/all_to_all | solution.py:182
  17.9 26.4 %collective-permute-start.1 = (bf16[512,1024]{1,0:T(8,128)(2,1)}, bf16[512,1024]{1,0:T(8,128)(2,1)}, u32[]{:S(2)}, u32[]{:S(2)}) collective-permute-start(bf16[512,1024]{1,0:T(8,128)(2,1)} %bitcast.131), channel_id=1, source_target_pairs={{0,16},{8,24},{16,0},{24,8},{1,17},{9,25},{17,1},{25,9},{2,18},{10... | collective-permute-start | bytes 3145736 | tf_op jit(solution)/shard_map/ppermute | solution.py:44
  19.4 47.4 %collective-permute-start.4 = (bf16[512,1024]{1,0:T(8,128)(2,1)}, bf16[512,1024]{1,0:T(8,128)(2,1)}, u32[]{:S(2)}, u32[]{:S(2)}) collective-permute-start(bf16[512,1024]{1,0:T(8,128)(2,1)} %bitcast.129), channel_id=1, source_target_pairs={{0,16},{8,24},{16,0},{24,8},{1,17},{9,25},{17,1},{25,9},{2,18},{10... | collective-permute-start | bytes 3145736 | tf_op jit(solution)/shard_map/ppermute | solution.py:44
  19.9 75.5 %collective-permute-start = (bf16[512,1024]{1,0:T(8,128)(2,1)}, bf16[512,1024]{1,0:T(8,128)(2,1)}, u32[]{:S(2)}, u32[]{:S(2)}) collective-permute-start(bf16[512,1024]{1,0:T(8,128)(2,1)} %bitcast.132), channel_id=1, source_target_pairs={{0,8},{8,0},{16,24},{24,16},{1,9},{9,1},{17,25},{25,17},{2,10},{10... | collective-permute-start | bytes 3145736 | tf_op jit(solution)/shard_map/ppermute | solution.py:39
  19.9 77.9 %collective-permute-start.3 = (bf16[512,1024]{1,0:T(8,128)(2,1)}, bf16[512,1024]{1,0:T(8,128)(2,1)}, u32[]{:S(2)}, u32[]{:S(2)}) collective-permute-start(bf16[512,1024]{1,0:T(8,128)(2,1)} %bitcast.130), channel_id=1, source_target_pairs={{0,8},{8,0},{16,24},{24,16},{1,9},{9,1},{17,25},{25,17},{2,10},{10... | collective-permute-start | bytes 3145736 | tf_op jit(solution)/shard_map/ppermute | solution.py:39
  20.4 75.1 %collective-permute-start.7 = (bf16[1024,512]{1,0:T(8,128)(2,1)}, bf16[1024,512]{1,0:T(8,128)(2,1)}, u32[]{:S(2)}, u32[]{:S(2)}) collective-permute-start(bf16[1024,512]{1,0:T(8,128)(2,1)} %bitcast.135), channel_id=1, source_target_pairs={{0,16},{8,24},{16,0},{24,8},{1,17},{9,25},{17,1},{25,9},{2,18},{10... | collective-permute-start | bytes 3145736 | tf_op jit(solution)/shard_map/ppermute | solution.py:44
  44.3 55.4 %collective-permute-start.2 = (bf16[512,1024]{1,0:T(8,128)(2,1)}, bf16[512,1024]{1,0:T(8,128)(2,1)}, u32[]{:S(2)}, u32[]{:S(2)}) collective-permute-start(bf16[512,1024]{1,0:T(8,128)(2,1)} %collective-permute-done.1), channel_id=1, source_target_pairs={{0,8},{8,0},{16,24},{24,16},{1,9},{9,1},{17,25},{25,17},{2,10},{10... | collective-permute-start | bytes 3145736 | tf_op jit(solution)/shard_map/ppermute | solution.py:39
  66.7 34.8 %collective-permute-start.5 = (bf16[512,1024]{1,0:T(8,128)(2,1)}, bf16[512,1024]{1,0:T(8,128)(2,1)}, u32[]{:S(2)}, u32[]{:S(2)}) collective-permute-start(bf16[512,1024]{1,0:T(8,128)(2,1)} %collective-permute-done.4), channel_id=1, source_target_pairs={{0,8},{8,0},{16,24},{24,16},{1,9},{9,1},{17,25},{25,17},{2,10},{10... | collective-permute-start | bytes 3145736 | tf_op jit(solution)/shard_map/ppermute | solution.py:39
  88.8 12.7 %copy-start.1 = (bf16[8,48,2048]{2,1,0:T(8,128)(2,1)}, bf16[8,48,2048]{2,1,0:T(8,128)(2,1)S(1)}, u32[]{:S(2)}) copy-start(bf16[8,48,2048]{2,1,0:T(8,128)(2,1)S(1)} %get-tuple-element.44) | copy-start | bytes 4718596
  88.8 23.3 %copy-start.7 = (bf16[8,48,2048]{2,1,0:T(8,128)(2,1)}, bf16[8,48,2048]{2,1,0:T(8,128)(2,1)S(1)}, u32[]{:S(2)}) copy-start(bf16[8,48,2048]{2,1,0:T(8,128)(2,1)S(1)} %get-tuple-element.43) | copy-start | bytes 4718596
  95.4 13.0 %collective-permute-start.6 = (bf16[1024,512]{1,0:T(8,128)(2,1)S(1)}, bf16[1024,512]{1,0:T(8,128)(2,1)S(1)}, u32[]{:S(2)}, u32[]{:S(2)}) collective-permute-start(bf16[1024,512]{1,0:T(8,128)(2,1)S(1)} %bitcast.136), channel_id=1, source_target_pairs={{0,8},{8,0},{16,24},{24,16},{1,9},{9,1},{17,25},{25,17},{2,10},{10... | collective-permute-start | bytes 3145736 | tf_op jit(solution)/shard_map/ppermute | solution.py:39
  95.5 12.3 %collective-permute-start.8 = (bf16[1024,512]{1,0:T(8,128)(2,1)}, bf16[1024,512]{1,0:T(8,128)(2,1)S(1)}, u32[]{:S(2)}, u32[]{:S(2)}) collective-permute-start(bf16[1024,512]{1,0:T(8,128)(2,1)} %collective-permute-done.7), channel_id=1, source_target_pairs={{0,8},{8,0},{16,24},{24,16},{1,9},{9,1},{17,25},{25,17},{2,10},{10... | collective-permute-start | bytes 3145736 | tf_op jit(solution)/shard_map/ppermute | solution.py:39
  105.4 6.7 %copy-start.39 = (bf16[384,1024]{1,0:T(8,128)(2,1)}, bf16[384,1024]{1,0:T(8,128)(2,1)S(1)}, u32[]{:S(2)}) copy-start(bf16[384,1024]{1,0:T(8,128)(2,1)S(1)} %get-tuple-element.27) | copy-start | bytes 2359300
  113.8 16.7 %collective-permute-start.10 = (bf16[1024,512]{1,0:T(8,128)(2,1)}, bf16[1024,512]{1,0:T(8,128)(2,1)}, u32[]{:S(2)}, u32[]{:S(2)}) collective-permute-start(bf16[1024,512]{1,0:T(8,128)(2,1)} %convolution_convert_fusion.9), channel_id=1, source_target_pairs={{0,8},{8,0},{16,24},{24,16},{1,9},{9,1},{17,25},{25,17},{2,10},{10... | collective-permute-start | bytes 3145736 | tf_op jit(solution)/shard_map/ppermute | solution.py:39
  113.9 46.3 %all-to-all-start.1 = ((bf16[8,48,2048]{2,1,0:T(8,128)(2,1)}), bf16[8,48,2048]{2,1,0:T(8,128)(2,1)S(1)}, u32[]{:S(2)}, u32[]{:S(2)}) async-start(bf16[8,48,2048]{2,1,0:T(8,128)(2,1)} %bitcast.13), calls=%async_computation.1 | async-start | bytes 3145728 | tf_op jit(solution)/shard_map/all_to_all | solution.py:174
  117.8 4.0 %copy-start.23 = (f32[384,1024]{1,0:T(8,128)S(1)}, f32[384,1024]{1,0:T(8,128)}, u32[]{:S(2)}) copy-start(f32[384,1024]{1,0:T(8,128)} %fusion.50) | copy-start | bytes 4718596
  117.8 4.0 %copy-start.26 = (f32[384,1024]{1,0:T(8,128)S(1)}, f32[384,1024]{1,0:T(8,128)}, u32[]{:S(2)}) copy-start(f32[384,1024]{1,0:T(8,128)} %copy-done.25) | copy-start | bytes 4718596
  126.3 73.8 %collective-permute-start.13 = (bf16[512,1024]{1,0:T(8,128)(2,1)}, bf16[512,1024]{1,0:T(8,128)(2,1)}, u32[]{:S(2)}, u32[]{:S(2)}) collective-permute-start(bf16[512,1024]{1,0:T(8,128)(2,1)} %convolution_convert_fusion.7), channel_id=1, source_target_pairs={{0,8},{8,0},{16,24},{24,16},{1,9},{9,1},{17,25},{25,17},{2,10},{10... | collective-permute-start | bytes 3145736 | tf_op jit(solution)/shard_map/ppermute | solution.py:39
  127.5 11.7 %collective-permute-start.9 = (bf16[512,1024]{1,0:T(8,128)(2,1)S(1)}, bf16[512,1024]{1,0:T(8,128)(2,1)S(1)}, u32[]{:S(2)}, u32[]{:S(2)}) collective-permute-start(bf16[512,1024]{1,0:T(8,128)(2,1)S(1)} %convolution_convert_fusion.11), channel_id=1, source_target_pairs={{0,8},{8,0},{16,24},{24,16},{1,9},{9,1},{17,25},{25,17},{2,10},{10... | collective-permute-start | bytes 3145736 | tf_op jit(solution)/shard_map/ppermute | solution.py:39
  129.4 69.8 %collective-permute-start.17 = (bf16[1024,512]{1,0:T(8,128)(2,1)}, bf16[1024,512]{1,0:T(8,128)(2,1)}, u32[]{:S(2)}, u32[]{:S(2)}) collective-permute-start(bf16[1024,512]{1,0:T(8,128)(2,1)} %convolution_convert_fusion.1), channel_id=1, source_target_pairs={{0,8},{8,0},{16,24},{24,16},{1,9},{9,1},{17,25},{25,17},{2,10},{10... | collective-permute-start | bytes 3145736 | tf_op jit(solution)/shard_map/ppermute | solution.py:39
  132.1 25.2 %collective-permute-start.11 = (bf16[1024,512]{1,0:T(8,128)(2,1)S(1)}, bf16[1024,512]{1,0:T(8,128)(2,1)S(1)}, u32[]{:S(2)}, u32[]{:S(2)}) collective-permute-start(bf16[1024,512]{1,0:T(8,128)(2,1)S(1)} %add_convert_fusion.5), channel_id=1, source_target_pairs={{0,16},{8,24},{16,0},{24,8},{1,17},{9,25},{17,1},{25,9},{2,18},{10... | collective-permute-start | bytes 3145736 | tf_op jit(solution)/shard_map/ppermute | solution.py:44
  135.4 63.8 %collective-permute-start.16 = (bf16[512,1024]{1,0:T(8,128)(2,1)}, bf16[512,1024]{1,0:T(8,128)(2,1)}, u32[]{:S(2)}, u32[]{:S(2)}) collective-permute-start(bf16[512,1024]{1,0:T(8,128)(2,1)} %convolution_convert_fusion.3), channel_id=1, source_target_pairs={{0,8},{8,0},{16,24},{24,16},{1,9},{9,1},{17,25},{25,17},{2,10},{10... | collective-permute-start | bytes 3145736 | tf_op jit(solution)/shard_map/ppermute | solution.py:39
  158.7 24.6 %collective-permute-start.12 = (bf16[512,1024]{1,0:T(8,128)(2,1)}, bf16[512,1024]{1,0:T(8,128)(2,1)}, u32[]{:S(2)}, u32[]{:S(2)}) collective-permute-start(bf16[512,1024]{1,0:T(8,128)(2,1)} %add_convert_fusion.4), channel_id=1, source_target_pairs={{0,16},{8,24},{16,0},{24,8},{1,17},{9,25},{17,1},{25,9},{2,18},{10... | collective-permute-start | bytes 3145736 | tf_op jit(solution)/shard_map/ppermute | solution.py:44
  169.4 13.9 %copy-start.24 = (bf16[384,512]{1,0:T(8,128)(2,1)S(1)}, bf16[384,512]{1,0:T(8,128)(2,1)}, u32[]{:S(2)}) copy-start(bf16[384,512]{1,0:T(8,128)(2,1)} %fusion.5) | copy-start | bytes 1179652
  184.7 42.6 %all-to-all-start.2 = ((bf16[8,48,2048]{2,1,0:T(8,128)(2,1)}), bf16[8,48,2048]{2,1,0:T(8,128)(2,1)}, u32[]{:S(2)}, u32[]{:S(2)}) async-start(bf16[8,48,2048]{2,1,0:T(8,128)(2,1)} %bitcast.120), calls=%async_computation.2 | async-start | bytes 3145728 | tf_op jit(solution)/shard_map/all_to_all | solution.py:174
  192.8 6.3 %collective-permute-start.15 = (bf16[512,1024]{1,0:T(8,128)(2,1)S(1)}, bf16[512,1024]{1,0:T(8,128)(2,1)S(1)}, u32[]{:S(2)}, u32[]{:S(2)}) collective-permute-start(bf16[512,1024]{1,0:T(8,128)(2,1)S(1)} %convolution_convert_fusion.5), channel_id=1, source_target_pairs={{0,8},{8,0},{16,24},{24,16},{1,9},{9,1},{17,25},{25,17},{2,10},{10... | collective-permute-start | bytes 3145736 | tf_op jit(solution)/shard_map/ppermute | solution.py:39
  199.1 4.2 %copy-start.34 = (bf16[1024,512]{1,0:T(8,128)(2,1)S(1)}, bf16[1024,512]{1,0:T(8,128)(2,1)}, u32[]{:S(2)}) copy-start(bf16[1024,512]{1,0:T(8,128)(2,1)} %copy-done.33) | copy-start | bytes 3145732
  201.8 25.4 %collective-permute-start.14 = (bf16[512,1024]{1,0:T(8,128)(2,1)S(1)}, bf16[512,1024]{1,0:T(8,128)(2,1)}, u32[]{:S(2)}, u32[]{:S(2)}) collective-permute-start(bf16[512,1024]{1,0:T(8,128)(2,1)S(1)} %add_convert_fusion.3), channel_id=1, source_target_pairs={{0,16},{8,24},{16,0},{24,8},{1,17},{9,25},{17,1},{25,9},{2,18},{10... | collective-permute-start | bytes 3145736 | tf_op jit(solution)/shard_map/ppermute | solution.py:44
  233.6 22.9 %copy-start.17 = (f32[128,512]{1,0:T(8,128)S(1)}, f32[128,512]{1,0:T(8,128)}, u32[]{:S(2)}) copy-start(f32[128,512]{1,0:T(8,128)} %get-tuple-element.52) | copy-start | bytes 786436
  233.6 22.9 %copy-start.19 = (f32[128,512]{1,0:T(8,128)S(1)}, f32[128,512]{1,0:T(8,128)}, u32[]{:S(2)}) copy-start(f32[128,512]{1,0:T(8,128)} %copy-done.18) | copy-start | bytes 786436
  (31 other events, 53.2 us)

commit v5 on v4

--- a/solution.py
+++ b/solution.py
@@ -216,22 +216,20 @@
     d_pre_gate = (d_hidden * pre_up * sigma * (1.0 + pre_gate * (1.0 - sigma))).astype(jnp.bfloat16)
     d_pre_up = (d_hidden * active).astype(jnp.bfloat16)
 
-    def pair_sum(lefts, rights, k, waited=()):
+    def pair_sum(lefts, rights, k):
         theirs = to_sibling(inner_product(lefts[2 * k + 1], rights[2 * k + 1]).astype(jnp.bfloat16))
-        theirs, waited = lax.optimization_barrier((theirs, waited))
         mine = inner_product(lefts[2 * k], rights[2 * k]).astype(jnp.bfloat16)
         return mine.astype(jnp.float32) + theirs.astype(jnp.float32)
 
-    def from_chips(lefts, rights, waited=()):
+    def from_chips(lefts, rights):
         return [
-            to_chip(pair_sum(lefts, rights, k, waited).astype(jnp.bfloat16), k)
-            for k in range(1, chips)
+            to_chip(pair_sum(lefts, rights, k).astype(jnp.bfloat16), k) for k in range(1, chips)
         ]
 
     hiddens, d_gates_in, d_ups_in = ([v] * dp_count for v in (hidden, d_pre_gate, d_pre_up))
     landed_down = from_chips(hiddens, out_parts)
-    landed_gate = from_chips(in_parts, d_gates_in, landed_down)
-    landed_up = from_chips(in_parts, d_ups_in, landed_down)
+    landed_gate = from_chips(in_parts, d_gates_in)
+    landed_up = from_chips(in_parts, d_ups_in)
 
     def d_rows_of(w, d_gate, d_up):
         return (transposed_product(d_gate, w[0]) + transposed_product(d_up, w[1])).astype(
@@ -241,7 +239,8 @@
     d_rows = [d_rows_of(pieces[0], d_pre_gate, d_pre_up)]
     returned, late_gate, late_up = lax.optimization_barrier((returned, d_pre_gate, d_pre_up))
     d_rows += [d_rows_of(w, late_gate, late_up) for w in pieces[1:]]
-    d_rows, landed_gate = lax.optimization_barrier((d_rows, landed_gate))
+    d_rows, landed_down = lax.optimization_barrier((d_rows, landed_down))
+    returned, landed_gate = lax.optimization_barrier((returned, landed_gate))
     d_back = exchange(jnp.concatenate(d_rows, axis=1))
     d_back, landed_up = lax.optimization_barrier((d_back, landed_up))
     totals = [

time: 264 us -> 263 us (level)
  matrix products: 61.3 us -> 75.5 us
  waiting for transfers between devices: 116 us -> 111 us
  other arithmetic: 28 us -> 23.6 us
  local copies, waits for them, and re-layouts: 9.43 us -> 6.67 us
    ppermute x6, waiting for transfers between devices: 94.4 us -> 74.7 us  [to_chip(): return lax.ppermute(value, 'dp', [(i, i ^ 2 * step) for i in range(count)])]
    all_to_all x2, waiting for transfers between devices: 0.02 us -> 14.6 us  [exchange(): lax.all_to_all(rows.reshape(experts, capacity, width), 'expert', split_ax...]
    dot_general x15, matrix products: 19.7 us -> 26.3 us  [inner_product(): lax.dot_general(left, right, (((0,), (0,)), ((), ())), preferred_element_...]
    convert_element_type x3 -> x0, other arithmetic: 4.53 us -> none  [from_chips(): pair_sum(lefts, rights, k, waited).astype(jnp.bfloat16)]
    dot_general x15, matrix products: 19 us -> 23.4 us  [product(): return jnp.dot(left, right, preferred_element_type=jnp.float32)]
    unnamed x85 -> x57, local copies, waits for them, and re-layouts: 7.39 us -> 3.46 us
    dot_general x12, matrix products: 21.4 us -> 24.6 us  [transposed_product(): lax.dot_general(left, right, (((1,), (1,)), ((), ())), preferred_element_...]
  transfers between devices with their start and end apart: 21 -> 21, of which waited for: 6 -> 6; matrix products, arithmetic and copies ran while one was open for 24% -> 33% of each run, Pallas kernels for 0% -> 7%
where the time goes in v5:
time: 263 us; the launch traced here: 262 us
  waiting for transfers between devices  111 us (42%)
  matrix products  75.5 us (29%)
  starting transfers between devices  26.2 us (10%)
  other arithmetic  23.6 us (9%)
  Pallas kernels  17.3 us (7%)
  local copies, waits for them, and re-layouts  6.67 us (3%)
    ppermute x6, waiting for transfers between devices, to_chip(): return lax.ppermute(value, 'dp', [(i, i ^ 2 * step) for i in range(count)])  74.7 us
    dot_general x15, matrix products, inner_product(): lax.dot_general(left, right, (((0,), (0,)), ((), ())), preferred_element_...  26.3 us
    dot_general x12, matrix products, transposed_product(): lax.dot_general(left, right, (((1,), (1,)), ((), ())), preferred_element_...  24.6 us
    dot_general x15, matrix products, product(): return jnp.dot(left, right, preferred_element_type=jnp.float32)  23.4 us
    all_to_all x1, waiting for transfers between devices, on_device(): lax.all_to_all(jnp.concatenate([rows.reshape(experts, capacity, width) fo...  21.9 us
    pallas_call x1, Pallas kernels, sum_over_all(): pl.pallas_call(functools.partial(exchange_sum_kernel, n, m), out_shape=ja...  17.3 us
    all_to_all x2, waiting for transfers between devices, exchange(): lax.all_to_all(rows.reshape(experts, capacity, width), 'expert', split_ax...  14.6 us
    all_to_all x2, starting transfers between devices, exchange(): lax.all_to_all(rows.reshape(experts, capacity, width), 'expert', split_ax...  8.99 us
  transfers between devices with their start and end apart: 21, of which 6 were waited for; matrix products, arithmetic and copies ran while one was open for 33% of the time, Pallas kernels for 7%

profile of v5, /device:TPU:0, one launch (start us, length us, event | category | flops | bytes accessed | tf_op | source)
XLA Modules:
  0.0 261.9 jit_solution(6795139499296795387)
XLA Ops:
  8.5 2.0 pad_maximum_fusion
  10.6 7.3 %all-to-all-start = ((bf16[8,96,2048]{2,1,0:T(8,128)(2,1)}), bf16[8,96,2048]{2,1,0:T(8,128)(2,1)}, u32[]{:S(2)}, u32[]{:S(2)}) async-start(bf16[8,96,2048]{2,1,0:T(8,128)(2,1)} %pad_maximum_fusion), calls=%async_computation | async-start | bytes 6291456 | tf_op jit(solution)/shard_map/all_to_all | solution.py:182
  21.9 22.3 %collective-permute-done.1 = bf16[512,1024]{1,0:T(8,128)(2,1)} collective-permute-done((bf16[512,1024]{1,0:T(8,128)(2,1)}, bf16[512,1024]{1,0:T(8,128)(2,1)}, u32[]{:S(2)}, u32[]{:S(2)}) %collective-permute-start.1) | collective-permute-done | bytes 1048608 | tf_op jit(solution)/shard_map/ppermute | solution.py:44
  44.2 22.5 %collective-permute-done.4 = bf16[512,1024]{1,0:T(8,128)(2,1)} collective-permute-done((bf16[512,1024]{1,0:T(8,128)(2,1)}, bf16[512,1024]{1,0:T(8,128)(2,1)}, u32[]{:S(2)}, u32[]{:S(2)}) %collective-permute-start.4) | collective-permute-done | bytes 1048608 | tf_op jit(solution)/shard_map/ppermute | solution.py:44
  66.7 21.9 %all-to-all-done = bf16[8,96,2048]{2,1,0:T(8,128)(2,1)} async-done(((bf16[8,96,2048]{2,1,0:T(8,128)(2,1)}), bf16[8,96,2048]{2,1,0:T(8,128)(2,1)}, u32[]{:S(2)}, u32[]{:S(2)}) %all-to-all-start) | async-done | bytes 3145760 | tf_op jit(solution)/shard_map/all_to_all | solution.py:182
  88.6 2.1 fusion.101
  90.7 2.4 fusion.72
  102.7 1.8 add_add_fusion.2
  104.6 3.9 %multiply_convert_fusion.3 = (bf16[384,1024]{1,0:T(8,128)(2,1)S(1)}, f32[384,1024]{1,0:T(8,128)}) fusion(f32[384,1024]{1,0:T(8,128)S(1)} %add_add_fusion.2, bf16[512,1024]{1,0:T(8,128)(2,1)} %collective-permute-done.5, bf16[384,2048]{1,0:T(8,128)(2,1)S(1)} %bitcast.109, f32[384,1024]{1,0:T(8,128)S(1)} %fusion.58, f32[384,1024]{1,0:T(8,128)S(1)} %fusion.70, ...), kind=kOutput, calls=%fused_computation.18 | convolution fusion | flops 406192128 | bytes 10092544 | tf_op jit(solution)/shard_map/dot_general | solution.py:15
  108.5 2.1 convolution_convert_fusion.16
  114.9 3.0 %fusion.50 = f32[384,1024]{1,0:T(8,128)} fusion(bf16[384,2048]{1,0:T(8,128)(2,1)S(1)} %bitcast.119, bf16[1,1024,512]{2,1,0:T(8,128)(2,1)} %param.15), kind=kOutput, calls=%fused_computation.98 | convolution fusion | flops 402653184 | bytes 3014656 | tf_op jit(solution)/shard_map/dot_general | solution.py:19
  117.9 4.5 %all-to-all-start.1 = ((bf16[8,48,2048]{2,1,0:T(8,128)(2,1)}), bf16[8,48,2048]{2,1,0:T(8,128)(2,1)}, u32[]{:S(2)}, u32[]{:S(2)}) async-start(bf16[8,48,2048]{2,1,0:T(8,128)(2,1)} %bitcast.13), calls=%async_computation.1 | async-start | bytes 3145728 | tf_op jit(solution)/shard_map/all_to_all | solution.py:174
  122.4 2.0 fusion.47
  124.4 2.0 fusion.44
  126.5 2.2 multiply_convert_fusion.1
  139.3 2.6 fusion.5
  145.2 14.6 %all-to-all-done.1 = bf16[8,48,2048]{2,1,0:T(8,128)(2,1)} async-done(((bf16[8,48,2048]{2,1,0:T(8,128)(2,1)}), bf16[8,48,2048]{2,1,0:T(8,128)(2,1)}, u32[]{:S(2)}, u32[]{:S(2)}) %all-to-all-start.1) | async-done | bytes 1572896 | tf_op jit(solution)/shard_map/all_to_all | solution.py:174
  168.9 1.9 fusion.6
  172.2 4.5 %all-to-all-start.2 = ((bf16[8,48,2048]{2,1,0:T(8,128)(2,1)}), bf16[8,48,2048]{2,1,0:T(8,128)(2,1)}, u32[]{:S(2)}, u32[]{:S(2)}) async-start(bf16[8,48,2048]{2,1,0:T(8,128)(2,1)} %bitcast.118), calls=%async_computation.2 | async-start | bytes 3145728 | tf_op jit(solution)/shard_map/all_to_all | solution.py:174
  178.4 2.0 add_convert_fusion.5
  187.6 2.0 add_convert_fusion.3
  190.1 16.4 %collective-permute-done.10 = bf16[512,1024]{1,0:T(8,128)(2,1)S(1)} collective-permute-done((bf16[512,1024]{1,0:T(8,128)(2,1)S(1)}, bf16[512,1024]{1,0:T(8,128)(2,1)S(1)}, u32[]{:S(2)}, u32[]{:S(2)}) %collective-permute-start.10) | collective-permute-done | bytes 1048608 | tf_op jit(solution)/shard_map/ppermute | solution.py:44
  206.6 2.3 fusion.76
  209.0 2.0 fusion.74
  211.0 2.9 %fusion.26 = bf16[1,1024,512]{2,1,0:T(8,128)(2,1)} fusion(bf16[1024,512]{1,0:T(8,128)(2,1)} %collective-permute-done.12, bf16[1024,512]{1,0:T(8,128)(2,1)} %collective-permute-done.17, bf16[1024,512]{1,0:T(8,128)(2,1)S(1)} %copy-done.20), kind=kLoop, calls=%fused_computation.72 | loop fusion | flops 3145728 | bytes 4194304 | tf_op jit(solution)/shard_map/broadcast_in_dim | solution.py:254
  213.9 13.4 %collective-permute-done.14 = bf16[512,1024]{1,0:T(8,128)(2,1)} collective-permute-done((bf16[512,1024]{1,0:T(8,128)(2,1)S(1)}, bf16[512,1024]{1,0:T(8,128)(2,1)}, u32[]{:S(2)}, u32[]{:S(2)}) %collective-permute-start.14) | collective-permute-done | bytes 1048608 | tf_op jit(solution)/shard_map/ppermute | solution.py:44
  227.3 1.9 fusion.77
  233.8 2.8 %fusion.24 = bf16[1,512,1024]{2,1,0:T(8,128)(2,1)} fusion(bf16[512,1024]{1,0:T(8,128)(2,1)S(1)} %copy-done.18, bf16[512,1024]{1,0:T(8,128)(2,1)} %collective-permute-done.15, bf16[512,1024]{1,0:T(8,128)(2,1)S(1)} %copy-done.19), kind=kLoop, calls=%fused_computation.70 | loop fusion | flops 3145728 | bytes 4194304 | tf_op jit(solution)/shard_map/broadcast_in_dim | solution.py:254
  236.7 17.3 %shard_map.135 = f32[16,2048]{1,0:T(8,128)} custom-call(f32[16,2048]{1,0:T(8,128)} %pad_maximum_fusion.5.v_ref), custom_call_target="tpu_custom_call" | custom-call | flops 393216 | bytes 1048576 | tf_op jit(solution)/shard_map/pallas_call | solution.py:105
  254.0 2.1 slice_reduce_fusion
  256.1 2.6 fusion.23
  258.7 3.1 %fusion.25 = bf16[1,512,1024]{2,1,0:T(8,128)(2,1)} fusion(bf16[512,1024]{1,0:T(8,128)(2,1)} %collective-permute-done.14, bf16[512,1024]{1,0:T(8,128)(2,1)} %collective-permute-done.16, bf16[512,1024]{1,0:T(8,128)(2,1)S(1)} %copy-done.16), kind=kLoop, calls=%fused_computation.71 | loop fusion | flops 3145728 | bytes 4194304 | tf_op jit(solution)/shard_map/broadcast_in_dim | solution.py:254
  (152 shorter events, 64.2 us)
Async XLA Ops:
  0.6 6.3 %copy-start = (bf16[2048,8]{0,1:T(8,128)(2,1)S(1)}, bf16[2048,8]{0,1:T(8,128)(2,1)}, u32[]{:S(2)}) copy-start(bf16[2048,8]{0,1:T(8,128)(2,1)} %param.12) | copy-start | bytes 98308
  0.6 5.6 %copy-start.6 = (bf16[128,2048]{1,0:T(8,128)(2,1)S(1)}, bf16[128,2048]{1,0:T(8,128)(2,1)}, u32[]{:S(2)}) copy-start(bf16[128,2048]{1,0:T(8,128)(2,1)} %param.10) | copy-start | bytes 1572868
  10.6 78.1 %all-to-all-start = ((bf16[8,96,2048]{2,1,0:T(8,128)(2,1)}), bf16[8,96,2048]{2,1,0:T(8,128)(2,1)}, u32[]{:S(2)}, u32[]{:S(2)}) async-start(bf16[8,96,2048]{2,1,0:T(8,128)(2,1)} %pad_maximum_fusion), calls=%async_computation | async-start | bytes 6291456 | tf_op jit(solution)/shard_map/all_to_all | solution.py:182
  17.8 26.4 %collective-permute-start.1 = (bf16[512,1024]{1,0:T(8,128)(2,1)}, bf16[512,1024]{1,0:T(8,128)(2,1)}, u32[]{:S(2)}, u32[]{:S(2)}) collective-permute-start(bf16[512,1024]{1,0:T(8,128)(2,1)} %bitcast.9), channel_id=1, source_target_pairs={{0,16},{8,24},{16,0},{24,8},{1,17},{9,25},{17,1},{25,9},{2,18},{10... | collective-permute-start | bytes 3145736 | tf_op jit(solution)/shard_map/ppermute | solution.py:44
  19.3 47.3 %collective-permute-start.4 = (bf16[512,1024]{1,0:T(8,128)(2,1)}, bf16[512,1024]{1,0:T(8,128)(2,1)}, u32[]{:S(2)}, u32[]{:S(2)}) collective-permute-start(bf16[512,1024]{1,0:T(8,128)(2,1)} %bitcast.10), channel_id=1, source_target_pairs={{0,16},{8,24},{16,0},{24,8},{1,17},{9,25},{17,1},{25,9},{2,18},{10... | collective-permute-start | bytes 3145736 | tf_op jit(solution)/shard_map/ppermute | solution.py:44
  19.8 78.7 %collective-permute-start = (bf16[512,1024]{1,0:T(8,128)(2,1)}, bf16[512,1024]{1,0:T(8,128)(2,1)}, u32[]{:S(2)}, u32[]{:S(2)}) collective-permute-start(bf16[512,1024]{1,0:T(8,128)(2,1)} %bitcast.9), channel_id=1, source_target_pairs={{0,8},{8,0},{16,24},{24,16},{1,9},{9,1},{17,25},{25,17},{2,10},{10... | collective-permute-start | bytes 3145736 | tf_op jit(solution)/shard_map/ppermute | solution.py:39
  19.8 81.1 %collective-permute-start.3 = (bf16[512,1024]{1,0:T(8,128)(2,1)}, bf16[512,1024]{1,0:T(8,128)(2,1)}, u32[]{:S(2)}, u32[]{:S(2)}) collective-permute-start(bf16[512,1024]{1,0:T(8,128)(2,1)} %bitcast.10), channel_id=1, source_target_pairs={{0,8},{8,0},{16,24},{24,16},{1,9},{9,1},{17,25},{25,17},{2,10},{10... | collective-permute-start | bytes 3145736 | tf_op jit(solution)/shard_map/ppermute | solution.py:39
  20.3 78.3 %collective-permute-start.7 = (bf16[1024,512]{1,0:T(8,128)(2,1)}, bf16[1024,512]{1,0:T(8,128)(2,1)}, u32[]{:S(2)}, u32[]{:S(2)}) collective-permute-start(bf16[1024,512]{1,0:T(8,128)(2,1)} %bitcast.11), channel_id=1, source_target_pairs={{0,16},{8,24},{16,0},{24,8},{1,17},{9,25},{17,1},{25,9},{2,18},{10... | collective-permute-start | bytes 3145736 | tf_op jit(solution)/shard_map/ppermute | solution.py:44
  44.2 58.5 %collective-permute-start.2 = (bf16[512,1024]{1,0:T(8,128)(2,1)}, bf16[512,1024]{1,0:T(8,128)(2,1)}, u32[]{:S(2)}, u32[]{:S(2)}) collective-permute-start(bf16[512,1024]{1,0:T(8,128)(2,1)} %collective-permute-done.1), channel_id=1, source_target_pairs={{0,8},{8,0},{16,24},{24,16},{1,9},{9,1},{17,25},{25,17},{2,10},{10... | collective-permute-start | bytes 3145736 | tf_op jit(solution)/shard_map/ppermute | solution.py:39
  66.7 37.9 %collective-permute-start.5 = (bf16[512,1024]{1,0:T(8,128)(2,1)}, bf16[512,1024]{1,0:T(8,128)(2,1)}, u32[]{:S(2)}, u32[]{:S(2)}) collective-permute-start(bf16[512,1024]{1,0:T(8,128)(2,1)} %collective-permute-done.4), channel_id=1, source_target_pairs={{0,8},{8,0},{16,24},{24,16},{1,9},{9,1},{17,25},{25,17},{2,10},{10... | collective-permute-start | bytes 3145736 | tf_op jit(solution)/shard_map/ppermute | solution.py:39
  90.7 33.7 %copy-start.4 = (bf16[8,48,2048]{2,1,0:T(8,128)(2,1)}, bf16[8,48,2048]{2,1,0:T(8,128)(2,1)S(1)}, u32[]{:S(2)}) copy-start(bf16[8,48,2048]{2,1,0:T(8,128)(2,1)S(1)} %get-tuple-element.43) | copy-start | bytes 4718596
  98.5 14.4 %collective-permute-start.6 = (bf16[1024,512]{1,0:T(8,128)(2,1)}, bf16[1024,512]{1,0:T(8,128)(2,1)S(1)}, u32[]{:S(2)}, u32[]{:S(2)}) collective-permute-start(bf16[1024,512]{1,0:T(8,128)(2,1)} %bitcast.11), channel_id=1, source_target_pairs={{0,8},{8,0},{16,24},{24,16},{1,9},{9,1},{17,25},{25,17},{2,10},{10... | collective-permute-start | bytes 3145736 | tf_op jit(solution)/shard_map/ppermute | solution.py:39
  98.6 13.7 %collective-permute-start.8 = (bf16[1024,512]{1,0:T(8,128)(2,1)}, bf16[1024,512]{1,0:T(8,128)(2,1)S(1)}, u32[]{:S(2)}, u32[]{:S(2)}) collective-permute-start(bf16[1024,512]{1,0:T(8,128)(2,1)} %collective-permute-done.7), channel_id=1, source_target_pairs={{0,8},{8,0},{16,24},{24,16},{1,9},{9,1},{17,25},{25,17},{2,10},{10... | collective-permute-start | bytes 3145736 | tf_op jit(solution)/shard_map/ppermute | solution.py:39
  104.6 3.9 %copy-start.13 = (f32[384,1024]{1,0:T(8,128)}, f32[384,1024]{1,0:T(8,128)S(1)}, u32[]{:S(2)}) copy-start(f32[384,1024]{1,0:T(8,128)S(1)} %add_add_fusion.2) | copy-start | bytes 4718596
  108.5 4.5 %copy-start.26 = (bf16[384,1024]{1,0:T(8,128)(2,1)}, bf16[384,1024]{1,0:T(8,128)(2,1)S(1)}, u32[]{:S(2)}) copy-start(bf16[384,1024]{1,0:T(8,128)(2,1)S(1)} %get-tuple-element.28) | copy-start | bytes 2359300
  117.9 41.8 %all-to-all-start.1 = ((bf16[8,48,2048]{2,1,0:T(8,128)(2,1)}), bf16[8,48,2048]{2,1,0:T(8,128)(2,1)}, u32[]{:S(2)}, u32[]{:S(2)}) async-start(bf16[8,48,2048]{2,1,0:T(8,128)(2,1)} %bitcast.13), calls=%async_computation.1 | async-start | bytes 3145728 | tf_op jit(solution)/shard_map/all_to_all | solution.py:174
  122.4 4.0 %copy-start.14 = (f32[384,1024]{1,0:T(8,128)S(1)}, f32[384,1024]{1,0:T(8,128)}, u32[]{:S(2)}) copy-start(f32[384,1024]{1,0:T(8,128)} %copy-done.13) | copy-start | bytes 4718596
  122.4 4.0 %copy-start.25 = (f32[384,1024]{1,0:T(8,128)S(1)}, f32[384,1024]{1,0:T(8,128)}, u32[]{:S(2)}) copy-start(f32[384,1024]{1,0:T(8,128)} %get-tuple-element.74) | copy-start | bytes 4718596
  126.5 4.1 %copy-start.27 = (bf16[384,1024]{1,0:T(8,128)(2,1)S(1)}, bf16[384,1024]{1,0:T(8,128)(2,1)}, u32[]{:S(2)}) copy-start(bf16[384,1024]{1,0:T(8,128)(2,1)} %copy-done.26) | copy-start | bytes 2359300
  130.4 57.2 %collective-permute-start.13 = (bf16[512,1024]{1,0:T(8,128)(2,1)}, bf16[512,1024]{1,0:T(8,128)(2,1)}, u32[]{:S(2)}, u32[]{:S(2)}) collective-permute-start(bf16[512,1024]{1,0:T(8,128)(2,1)} %convolution_convert_fusion.7), channel_id=1, source_target_pairs={{0,8},{8,0},{16,24},{24,16},{1,9},{9,1},{17,25},{25,17},{2,10},{10... | collective-permute-start | bytes 3145736 | tf_op jit(solution)/shard_map/ppermute | solution.py:39
  131.3 10.6 %collective-permute-start.11 = (bf16[1024,512]{1,0:T(8,128)(2,1)S(1)}, bf16[1024,512]{1,0:T(8,128)(2,1)S(1)}, u32[]{:S(2)}, u32[]{:S(2)}) collective-permute-start(bf16[1024,512]{1,0:T(8,128)(2,1)S(1)} %convolution_convert_fusion.9), channel_id=1, source_target_pairs={{0,8},{8,0},{16,24},{24,16},{1,9},{9,1},{17,25},{25,17},{2,10},{10... | collective-permute-start | bytes 3145736 | tf_op jit(solution)/shard_map/ppermute | solution.py:39
  133.5 45.0 %collective-permute-start.9 = (bf16[512,1024]{1,0:T(8,128)(2,1)}, bf16[512,1024]{1,0:T(8,128)(2,1)}, u32[]{:S(2)}, u32[]{:S(2)}) collective-permute-start(bf16[512,1024]{1,0:T(8,128)(2,1)} %convolution_convert_fusion.11), channel_id=1, source_target_pairs={{0,8},{8,0},{16,24},{24,16},{1,9},{9,1},{17,25},{25,17},{2,10},{10... | collective-permute-start | bytes 3145736 | tf_op jit(solution)/shard_map/ppermute | solution.py:39
  135.3 75.7 %collective-permute-start.17 = (bf16[1024,512]{1,0:T(8,128)(2,1)}, bf16[1024,512]{1,0:T(8,128)(2,1)}, u32[]{:S(2)}, u32[]{:S(2)}) collective-permute-start(bf16[1024,512]{1,0:T(8,128)(2,1)} %convolution_convert_fusion.1), channel_id=1, source_target_pairs={{0,8},{8,0},{16,24},{24,16},{1,9},{9,1},{17,25},{25,17},{2,10},{10... | collective-permute-start | bytes 3145736 | tf_op jit(solution)/shard_map/ppermute | solution.py:39
  143.7 27.2 %collective-permute-start.12 = (bf16[1024,512]{1,0:T(8,128)(2,1)}, bf16[1024,512]{1,0:T(8,128)(2,1)}, u32[]{:S(2)}, u32[]{:S(2)}) collective-permute-start(bf16[1024,512]{1,0:T(8,128)(2,1)} %add_convert_fusion.4), channel_id=1, source_target_pairs={{0,16},{8,24},{16,0},{24,8},{1,17},{9,25},{17,1},{25,9},{2,18},{10... | collective-permute-start | bytes 3145736 | tf_op jit(solution)/shard_map/ppermute | solution.py:44
  172.2 55.2 %all-to-all-start.2 = ((bf16[8,48,2048]{2,1,0:T(8,128)(2,1)}), bf16[8,48,2048]{2,1,0:T(8,128)(2,1)}, u32[]{:S(2)}, u32[]{:S(2)}) async-start(bf16[8,48,2048]{2,1,0:T(8,128)(2,1)} %bitcast.118), calls=%async_computation.2 | async-start | bytes 3145728 | tf_op jit(solution)/shard_map/all_to_all | solution.py:174
  180.4 26.2 %collective-permute-start.10 = (bf16[512,1024]{1,0:T(8,128)(2,1)S(1)}, bf16[512,1024]{1,0:T(8,128)(2,1)S(1)}, u32[]{:S(2)}, u32[]{:S(2)}) collective-permute-start(bf16[512,1024]{1,0:T(8,128)(2,1)S(1)} %add_convert_fusion.5), channel_id=1, source_target_pairs={{0,16},{8,24},{16,0},{24,8},{1,17},{9,25},{17,1},{25,9},{2,18},{10... | collective-permute-start | bytes 3145736 | tf_op jit(solution)/shard_map/ppermute | solution.py:44
  187.1 71.6 %collective-permute-start.16 = (bf16[512,1024]{1,0:T(8,128)(2,1)}, bf16[512,1024]{1,0:T(8,128)(2,1)}, u32[]{:S(2)}, u32[]{:S(2)}) collective-permute-start(bf16[512,1024]{1,0:T(8,128)(2,1)} %convolution_convert_fusion.3), channel_id=1, source_target_pairs={{0,8},{8,0},{16,24},{24,16},{1,9},{9,1},{17,25},{25,17},{2,10},{10... | collective-permute-start | bytes 3145736 | tf_op jit(solution)/shard_map/ppermute | solution.py:39
  187.1 46.7 %collective-permute-start.15 = (bf16[512,1024]{1,0:T(8,128)(2,1)}, bf16[512,1024]{1,0:T(8,128)(2,1)}, u32[]{:S(2)}, u32[]{:S(2)}) collective-permute-start(bf16[512,1024]{1,0:T(8,128)(2,1)} %convolution_convert_fusion.5), channel_id=1, source_target_pairs={{0,8},{8,0},{16,24},{24,16},{1,9},{9,1},{17,25},{25,17},{2,10},{10... | collective-permute-start | bytes 3145736 | tf_op jit(solution)/shard_map/ppermute | solution.py:39
  189.6 37.8 %collective-permute-start.14 = (bf16[512,1024]{1,0:T(8,128)(2,1)S(1)}, bf16[512,1024]{1,0:T(8,128)(2,1)}, u32[]{:S(2)}, u32[]{:S(2)}) collective-permute-start(bf16[512,1024]{1,0:T(8,128)(2,1)S(1)} %add_convert_fusion.3), channel_id=1, source_target_pairs={{0,16},{8,24},{16,0},{24,8},{1,17},{9,25},{17,1},{25,9},{2,18},{10... | collective-permute-start | bytes 3145736 | tf_op jit(solution)/shard_map/ppermute | solution.py:44
  206.6 2.4 copy-start.17
  230.9 3.0 %copy-start.19 = (bf16[512,1024]{1,0:T(8,128)(2,1)S(1)}, bf16[512,1024]{1,0:T(8,128)(2,1)}, u32[]{:S(2)}) copy-start(bf16[512,1024]{1,0:T(8,128)(2,1)} %convolution_convert_fusion.6) | copy-start | bytes 3145732
  256.1 2.6 %copy-start.16 = (bf16[512,1024]{1,0:T(8,128)(2,1)S(1)}, bf16[512,1024]{1,0:T(8,128)(2,1)}, u32[]{:S(2)}) copy-start(bf16[512,1024]{1,0:T(8,128)(2,1)} %convolution_convert_fusion.4) | copy-start | bytes 3145732
  (17 other events, 28.5 us)
